TPU v7x, 128 devices: a whole 4x4x4 slice. The times are simulated.
128 devices in a mesh: band: 8 (over y, core), wave: 8 (over z, x_lo), lev: 2 (over x_hi).
Axes of the slice: x: 4 (x_hi: 2, x_lo: 2; x = x_hi * 2 + x_lo), y: 4, z: 4, core: 2. Of those that a mesh axis runs over, the one named last changes fastest.
Arguments:
- fourier: float32 [2560, 96, 2, 4, 128], P('band', 'wave', None, None, 'lev'), may hold values from -6 to 6
- legendre: float32 [96, 1280, 2, 648], P('wave', 'band'), may hold values from -0.25 to 0.25
- pair_m: int32 [96], P('wave'), may hold values from 0 to 639, as said below
- mirror: int32 [2560], replicated, may hold values from 0 to 2559, as said below
Outputs:
- coefficients: float32 [96, 2, 4, 128, 648], P('wave', None, None, 'lev', 'band')
- energy: float32 [1279], replicated
Inputs may be any that keep to these rules, and one draw needn't show every extreme that they name: `pair_m`: values are distinct and both 0 and 639 appear. mirror is an involution; every row of band block b < 8/2 (blocks of 320 rows) is paired with a row of block b + 4.
All inputs are finite; a program needn't handle non-finite values.
Results may differ from a plain program's by a relative error of at most 0.0003.
Values sent between devices are 32-bit elements; how exact they have to be, the bound alone decides.
No kernel may reach another device: no remote copies, remote signals or barrier semaphores. Data moves between devices by JAX's collectives and lax.ppermute only.
A program may use at most 192 MiB of HBM per device.

v0:
```python
import jax
import jax.numpy as jnp
from jax import lax
from jax.sharding import PartitionSpec as P

NDEG = 1280


def passed_along(x, axis, by):
    peers = lax.axis_size(axis)
    return lax.ppermute(x, axis, [(i, (i + by) % peers) for i in range(peers)])


def slot_layout(wavenum, slots):
    first_m = wavenum[:, None, None]
    parity = jnp.arange(2, dtype=jnp.int32)[None, :, None]
    column = jnp.arange(slots, dtype=jnp.int32)[None, None, :]
    count_first = (NDEG - first_m - parity + 1) // 2
    leading = column < count_first
    second_m = NDEG - 1 - first_m
    degree = jnp.where(
        leading, first_m + parity + 2 * column, second_m + parity + 2 * (column - count_first)
    )
    owner_m = jnp.where(leading, first_m, second_m)
    return (leading, degree, owner_m)


def degree_energy(squares, degree, owner_m):
    usable = (degree >= 1) & (degree <= NDEG - 1)
    safe = jnp.maximum(degree, 1).astype(jnp.float32)
    factor = jnp.where(owner_m == 0, 1.0, 2.0).astype(jnp.float32)
    term = jnp.where(usable, factor * squares / (4.0 * safe * (safe + 1.0)), 0.0)
    bins = jnp.where(usable, degree - 1, NDEG - 1)
    summed = jax.ops.segment_sum(term.reshape(-1), bins.reshape(-1), num_segments=NDEG)
    return summed[: NDEG - 1]


def project(folded, legendre, leading, degree, parity):
    count = folded.shape[0]
    pairs = folded.shape[1]
    flat = folded.reshape(count, pairs, -1)
    result = jnp.einsum(
        "qpk,pqc->pkc",
        flat,
        legendre[:, :, parity, :],
        precision=lax.Precision.HIGHEST,
        preferred_element_type=jnp.float32,
    )
    result = result.reshape(pairs, 2, folded.shape[3], folded.shape[4], legendre.shape[3])
    pick = leading[:, parity][:, None, None, :]
    valid = (degree[:, parity] <= NDEG - 1)[:, None, None, :]
    return jnp.where(valid, jnp.where(pick, result[:, 0], result[:, 1]), 0.0)


def shards(fourier, legendre, pair_m, mirror):
    bands = lax.axis_size("band")
    half_bands = bands // 2
    rows = fourier.shape[0]
    half_rows = rows // 2
    position = lax.axis_index("band")
    north_side = position < half_bands
    north_base = position % half_bands * rows
    south_base = north_base + half_bands * rows
    offsets = jnp.arange(half_rows, dtype=jnp.int32)
    first_partner = jnp.take(mirror, north_base + offsets) - south_base
    second_partner = jnp.take(mirror, north_base + half_rows + offsets) - south_base
    outgoing = jnp.where(north_side, fourier[half_rows:], fourier[first_partner])
    incoming = passed_along(outgoing, "band", half_bands)
    north_part = jnp.where(north_side, fourier[:half_rows], incoming)
    south_part = jnp.where(north_side, incoming, fourier[second_partner])
    symmetric = north_part + south_part
    antisym = north_part - south_part
    slots = legendre.shape[3]
    leading, degree, owner_m = slot_layout(pair_m, slots)
    terms = jnp.stack(
        [
            project(symmetric, legendre, leading, degree, 0),
            project(antisym, legendre, leading, degree, 1),
        ],
        1,
    )
    coefficients = lax.psum_scatter(terms, "band", scatter_dimension=4, tiled=True)
    share = slots // bands
    start = position * share
    local_degree = lax.dynamic_slice_in_dim(degree, start, share, 2)
    local_owner = lax.dynamic_slice_in_dim(owner_m, start, share, 2)
    squares = jnp.sum(coefficients * coefficients, axis=(2, 3))
    partial_energy = degree_energy(squares, local_degree, local_owner)
    total = lax.psum(partial_energy, ("band", "wave", "lev"))
    return (coefficients, jnp.log(total))


def solution(mesh):
    return jax.shard_map(
        shards,
        mesh=mesh,
        in_specs=(
            P("band", "wave", None, None, "lev"),
            P("wave", "band", None, None),
            P("wave"),
            P(),
        ),
        out_specs=(P("wave", None, None, "lev", "band"), P()),
        check_vma=False,
    )
```

profile of v0, /device:TPU:0, one launch (start us, length us, event | category | flops | bytes accessed | tf_op | source)
XLA Modules:
  0.0 633.0 jit_solution(1662252053535409024)
XLA Ops:
  7.2 0.0 copy-start
  7.2 0.0 all-reduce.3.cloned.1.call-start
  7.3 0.6 copy-done
  7.9 1.4 gather_fusion.3
  9.3 1.4 gather_fusion.2
  10.8 17.5 %copy.38 = f32[320,12,2,4,64]{4,3,2,1,0:T(4,128)} copy(f32[320,12,2,4,64]{0,4,3,2,1:T(8,128)} %param.6) | data formatting | bytes 15728640 | tf_op args[0]
  28.3 19.8 %gather_fusion = f32[160,12,2,4,64]{4,3,2,1,0:T(4,128)} fusion(f32[320,12,2,4,64]{4,3,2,1,0:T(4,128)} %copy.38, s32[1024]{0:T(1024)S(1)} %pad_clamp_fusion.2), kind=kCustom, calls=%fused_computation.2 | custom fusion | bytes 7864960 | tf_op jit(solution)/shard_map/gather | solution.py:67
  48.1 9.9 %slice_select_fusion.2 = f32[160,12,2,4,64]{4,3,2,1,0:T(4,128)} fusion(f32[160,12,2,4,64]{4,3,2,1,0:T(4,128)} %gather_fusion, f32[320,12,2,4,64]{4,3,2,1,0:T(4,128)} %copy.38, pred[]{:T(512)S(6)} %lt.44), kind=kLoop, calls=%fused_computation.10 | loop fusion | flops 983040 | bytes 11796481 | tf_op jit(solution)/shard_map/jit(_where)/select_n | solution.py:67
  58.0 9.8 %copy.41 = f32[160,12,2,4,64]{0,4,3,2,1:T(8,128)} copy(f32[160,12,2,4,64]{4,3,2,1,0:T(4,128)} %slice_select_fusion.2) | data formatting | bytes 7864320 | tf_op jit(solution)/shard_map/jit(_where)/select_n | solution.py:67
  67.8 6.0 collective-permute-start
  73.8 0.0 copy-start.3
  73.8 19.8 %gather_fusion.1 = f32[160,12,2,4,64]{4,3,2,1,0:T(4,128)} fusion(f32[320,12,2,4,64]{4,3,2,1,0:T(4,128)} %copy.38, s32[1024]{0:T(1024)S(1)} %pad_clamp_fusion), kind=kCustom, calls=%fused_computation.3 | custom fusion | bytes 7864960 | tf_op jit(solution)/shard_map/gather | solution.py:70
  93.6 0.0 copy-done.3
  93.7 0.1 iota_add_fusion.1
  93.7 0.1 add_select_fusion.2
  93.8 0.1 add_select_fusion
  94.0 0.1 slice_compare_fusion.1
  94.1 0.1 iota_compare_fusion
  94.2 0.1 fusion.17
  94.3 15.2 %fusion.16 = (f32[12,160,1,648]{3,2,1,0:T(1,128)}, f32[12,160,1,648]{3,2,1,0:T(1,128)}) fusion(f32[12,160,2,648]{3,2,1,0:T(2,128)} %param.7), kind=kLoop, calls=%fused_computation.64 | loop fusion | bytes 19906560 | tf_op jit(solution)/shard_map/slice | solution.py:45
  109.5 100.1 %collective-permute-done = f32[160,12,2,4,64]{0,4,3,2,1:T(8,128)} collective-permute-done((f32[160,12,2,4,64]{0,4,3,2,1:T(8,128)}, f32[160,12,2,4,64]{0,4,3,2,1:T(8,128)}, u32[]{:S(2)}, u32[]{:S(2)}) %collective-permute-start) | collective-permute-done | bytes 3932192 | tf_op jit(solution)/shard_map/ppermute | solution.py:11
  209.7 9.4 %copy.42 = f32[160,12,2,4,64]{4,3,2,1,0:T(4,128)} copy(f32[160,12,2,4,64]{0,4,3,2,1:T(8,128)} %collective-permute-done) | data formatting | bytes 7864320 | tf_op jit(solution)/shard_map/ppermute | solution.py:11
  219.0 13.0 %fusion.5 = (f32[160,12,2,4,64]{4,3,2,1,0:T(4,128)}, f32[160,12,2,4,64]{4,3,2,1,0:T(4,128)}) fusion(f32[160,12,2,4,64]{4,3,2,1,0:T(4,128)} %copy.42, f32[160,12,2,4,64]{4,3,2,1,0:T(4,128)} %gather_fusion.1, pred[]{:T(512)S(6)} %lt.44, f32[320,12,2,4,64]{4,3,2,1,0:T(4,128)} %copy.38), kind=kLoop, calls=%fused_computation.19 | loop fusion | flops 3932160 | bytes 19660800 | tf_op jit(solution)/shard_map/add | solution.py:71
  232.0 9.8 %copy.45 = f32[160,12,2,4,64]{0,4,3,2,1:T(8,128)} copy(f32[160,12,2,4,64]{4,3,2,1,0:T(4,128)} %get-tuple-element.5) | data formatting | bytes 7864320 | tf_op jit(solution)/shard_map/add | solution.py:71
  241.9 0.0 slice-start
  241.9 10.0 %copy.49 = f32[160,12,2,4,64]{0,4,3,2,1:T(8,128)} copy(f32[160,12,2,4,64]{4,3,2,1,0:T(4,128)} %get-tuple-element.6) | data formatting | bytes 7864320 | tf_op jit(solution)/shard_map/sub | solution.py:72
  251.8 22.8 %fusion.3 = f32[12,512,648]{2,1,0:T(8,128)} fusion(f32[160,12,512]{0,2,1:T(8,128)} %bitcast.31, f32[12,160,1,648]{3,2,1,0:T(1,128)} %get-tuple-element.7), kind=kOutput, calls=%fused_computation.15 | convolution fusion | flops 7644119040 | bytes 24834048 | tf_op jit(solution)/shard_map/qpk,pqc->pkc/dot_general | solution.py:42
  274.7 0.0 slice-done
  274.7 0.0 copy-done.2
  274.7 0.0 slice-done.1
  274.7 19.0 %fusion.2 = f32[12,512,648]{2,1,0:T(8,128)} fusion(f32[160,12,512]{0,2,1:T(8,128)S(1)} %bitcast.30, f32[12,160,1,648]{3,2,1,0:T(1,128)S(1)} %bitcast.33), kind=kOutput, calls=%fused_computation.13 | convolution fusion | flops 7644119040 | bytes 24834048 | tf_op jit(solution)/shard_map/qpk,pqc->pkc/dot_general | solution.py:42
  293.7 12.9 %fusion.1 = f32[12,1,4,64,648]{4,3,2,1,0:T(8,128)} fusion(f32[12,2,4,64,648]{4,3,2,1,0:T(8,128)} %bitcast.28, pred[12,648]{1,0:T(8,128)(4,1)S(1)} %bitcast.35, pred[12,648]{1,0:T(8,128)(4,1)S(1)} %bitcast.34), kind=kLoop, calls=%fused_computation.9 | loop fusion | flops 3981312 | bytes 23903424 | tf_op jit(solution)/shard_map/jit(_where)/select_n | solution.py:52
  306.5 12.8 %fusion = f32[12,1,4,64,648]{4,3,2,1,0:T(8,128)} fusion(f32[12,2,4,64,648]{4,3,2,1,0:T(8,128)} %bitcast.29, pred[12,648]{1,0:T(8,128)(4,1)S(1)} %bitcast.37, pred[12,648]{1,0:T(8,128)(4,1)S(1)} %bitcast.36), kind=kLoop, calls=%fused_computation.7 | loop fusion | flops 3981312 | bytes 23903424 | tf_op jit(solution)/shard_map/jit(_where)/select_n | solution.py:52
  319.3 12.8 %pad_maximum_fusion = f32[12,2,4,64,648]{4,3,2,1,0:T(8,128)} fusion(f32[12,1,4,64,648]{4,3,2,1,0:T(8,128)} %fusion, f32[12,1,4,64,648]{4,3,2,1,0:T(8,128)} %fusion.1), kind=kLoop, calls=%fused_computation.5 | loop fusion | flops 3981312 | bytes 31850496 | tf_op jit(solution)/shard_map/stack | solution.py:75
  332.1 0.0 all-reduce.3.cloned.1.call-update
  332.1 0.0 copy-start.1
  332.1 0.1 add_select_fusion.1
  332.2 0.1 reshape.197
  332.3 0.4 copy-done.4
  332.7 0.6 dynamic-slice
  334.0 204.8 %all-reduce.3.cloned.1.call-done = f32[12,2,4,64,648]{4,3,2,1,0:T(8,128)} async-done(((f32[12,2,4,64,648]{4,3,2,1,0:T(8,128)}), f32[12,2,4,64,648]{4,3,2,1,0:T(8,128)}) %all-reduce.3.cloned.1.call-update) | async-done | bytes 15925264
  538.7 5.3 multiply_reduce_fusion
  544.1 0.1 fusion.8
  544.2 0.1 reshape.199
  544.3 14.8 %scatter_custom_fusion = f32[1280]{0:T(1024)S(1)} fusion(s32[1944]{0:T(1024)S(1)} %reshape.197, f32[1944]{0:T(1024)S(1)} %reshape.199, f32[]{:T(128)} %constant.24.clone.1), kind=kCustom, calls=%fused_computation.50 | custom fusion | flops 1944 | bytes 5124 | tf_op jit(solution)/shard_map/scatter-add | solution.py:34
  559.1 66.1 %psum.7 = f32[1279]{0:T(1024)S(1)} all-reduce(f32[1279]{0:T(1024)S(1)} %bitcast.38), channel_id=1, replica_groups=mesh['band'=8,'wave'=8,'lev'=2] {'band','wave','lev'}, use_global_device_ids=true, to_apply=%region_3.5 | all-reduce | flops 1279 | bytes 10232 | tf_op jit(solution)/shard_map/psum | solution.py:89
  625.2 0.6 log.3
  625.8 0.0 copy-done.1
  (17 shorter events, 0.1 us)
Async XLA Ops:
  7.2 0.7 copy-start
  7.2 531.6 %all-reduce.3.cloned.1.call-start = ((), (), s32[]{:S(2)}) async-start(), calls=%async_computation | async-start | bytes 37748736
  67.8 141.8 %collective-permute-start = (f32[160,12,2,4,64]{0,4,3,2,1:T(8,128)}, f32[160,12,2,4,64]{0,4,3,2,1:T(8,128)}, u32[]{:S(2)}, u32[]{:S(2)}) collective-permute-start(f32[160,12,2,4,64]{0,4,3,2,1:T(8,128)} %copy.41), channel_id=1, source_target_pairs={{0,64},{16,80},{32,96},{48,112},{64,0},{80,16},{96,32},{112,48},{1... | collective-permute-start | bytes 11796488 | tf_op jit(solution)/shard_map/ppermute | solution.py:11
  73.8 19.8 %copy-start.3 = (s32[12]{0:T(128)S(1)}, s32[12]{0:T(128)}, u32[]{:S(2)}) copy-start(s32[12]{0:T(128)} %param.8) | copy-start | bytes 148
  241.9 32.8 %slice-start = ((s8[5898240]{0:T(1024)(128)(4,1)}), s8[1703936]{0:T(1024)(128)(4,1)S(1)}, s32[]{:S(2)}) async-start(s8[5898240]{0:T(1024)(128)(4,1)} %bitcast.32), calls=%async_computation.1 | async-start | bytes 3407872
  251.8 22.8 %copy-start.2 = (f32[160,12,2,4,64]{0,4,3,2,1:T(8,128)S(1)}, f32[160,12,2,4,64]{0,4,3,2,1:T(8,128)}, u32[]{:S(2)}) copy-start(f32[160,12,2,4,64]{0,4,3,2,1:T(8,128)} %copy.49) | copy-start | bytes 11796484
  251.8 22.8 %slice-start.1 = ((s8[5898240]{0:T(1024)(128)(4,1)}), s8[4194304]{0:T(1024)(128)(4,1)S(1)}, s32[]{:S(2)}) async-start(s8[5898240]{0:T(1024)(128)(4,1)} %bitcast.32), calls=%async_computation.2 | async-start | bytes 8388608
  332.1 0.7 copy-start.4
  332.1 293.7 %copy-start.1 = (s32[2560]{0:T(1024)S(1)}, s32[2560]{0:T(1024)}, u32[]{:S(2)}) copy-start(s32[2560]{0:T(1024)} %param.9) | copy-start | bytes 30724
Sparse Core Ops, SparseCore 0:
  332.2 206.4 all-reduce.2
where the time goes:
time: 643 us; the launch traced here: 633 us
  waiting for transfers between devices  305 us (47%)
  local copies, waits for them, and re-layouts  117 us (18%)
  other arithmetic  82.2 us (13%)
  blocking collectives  66.1 us (10%)
  matrix products  41.8 us (7%)
  between operations  15.2 us (2%)
    unnamed x2, waiting for transfers between devices  205 us
    ppermute x1, waiting for transfers between devices, passed_along(): return lax.ppermute(x, axis, [(i, (i + by) % peers) for i in range(peers)])  100 us
    psum x1, blocking collectives, shards(): total = lax.psum(partial_energy, ('band', 'wave', 'lev'))  66.1 us
    dot_general x2, matrix products, project(): jnp.einsum('qpk,pqc->pkc', flat, legendre[:, :, parity, :], precision=lax...  41.8 us
    select_n x2, other arithmetic, project(): return jnp.where(valid, jnp.where(pick, result[:, 0], result[:, 1]), 0.0)  25.6 us
    gather x1, local copies, waits for them, and re-layouts, shards(): south_part = jnp.where(north_side, incoming, fourier[second_partner])  19.8 us
    gather x1, local copies, waits for them, and re-layouts, shards(): fourier[first_partner]  19.8 us
    unnamed x20, local copies, waits for them, and re-layouts  19.1 us
  transfers between devices with their start and end apart: 2, of which 2 were waited for; matrix products, arithmetic and copies ran while one was open for 6% of the time, Pallas kernels for 0%

commit v1 on v0

v1 whole, which is shorter than its diff:
```python
import functools

import jax
import jax.numpy as jnp
from jax import lax
from jax.experimental import pallas as pl
from jax.experimental.pallas import tpu as pltpu
from jax.sharding import PartitionSpec as P

NDEG = 1280
CHUNKS = 3
F32 = jnp.float32
BF16 = jnp.bfloat16
VMEM_LIMIT = 48 * 1024 * 1024


def split_two(x):
    high = x.astype(BF16)
    low = (x - high.astype(F32)).astype(BF16)
    return high, low


def dot_nt(a, b):
    return lax.dot_general(a, b, (((1,), (1,)), ((), ())), preferred_element_type=F32)


def dot_nn(a, b):
    return jnp.dot(a, b, preferred_element_type=F32)


def send_along(x, up, cross):
    size = lax.axis_size("band")
    chips = size // 2
    pairs = [(i, ((i // 2 + up) % chips) * 2 + ((i % 2) ^ cross)) for i in range(size)]
    return lax.ppermute(x, "band", pairs)


def pick_kernel(place_ref, index_ref, field_ref, own_ref, cross_ref, *, own_steps):
    step = pl.program_id(0)
    count = index_ref.shape[0]
    rows = field_ref.shape[2]
    lanes = lax.broadcasted_iota(jnp.int32, (count, rows), 1)
    chosen = jnp.where(index_ref[...] == lanes, 1.0, 0.0).astype(BF16)
    high, low = split_two(field_ref[0])
    picked = dot_nt(chosen, high) + dot_nt(chosen, low)

    @pl.when(step < own_steps)
    def _():
        own_ref[0] = picked

    @pl.when(step >= own_steps)
    def _():
        cross_ref[0] = picked


def pick_rows(place, index, field, chunk, chunks):
    pairs, width, rows = field.shape
    group = pairs // 2
    each = group // chunks
    count = index.shape[0]

    def field_map(step, place_ref):
        mine = step < each
        core = jnp.where(mine, place_ref[0], 1 - place_ref[0])
        return (core * group + chunk * each + jnp.where(mine, step, step - each), 0, 0)

    shape = jax.ShapeDtypeStruct((each, count, width), F32)
    return pl.pallas_call(
        functools.partial(pick_kernel, own_steps=each),
        grid_spec=pltpu.PrefetchScalarGridSpec(
            num_scalar_prefetch=1,
            grid=(2 * each,),
            in_specs=[
                pl.BlockSpec((count, 1), lambda step, place_ref: (0, 0)),
                pl.BlockSpec((1, width, rows), field_map),
            ],
            out_specs=[
                pl.BlockSpec((1, count, width), lambda step, place_ref: (jnp.minimum(step, each - 1), 0, 0)),
                pl.BlockSpec((1, count, width), lambda step, place_ref: (jnp.maximum(step - each, 0), 0, 0)),
            ],
        ),
        out_shape=[shape, shape],
        compiler_params=pltpu.CompilerParams(vmem_limit_bytes=VMEM_LIMIT),
        cost_estimate=pl.CostEstimate(
            flops=8 * each * count * width * rows,
            bytes_accessed=2 * each * width * (rows + count) * 4,
            transcendentals=0,
        ),
        name="pick_rows",
    )(place, index, field)


def layout_kernel(*refs, share):
    out_ref = refs[-1]
    tiles = (len(refs) - 1) // 2
    half = refs[0].shape[1] // 2
    main = lanes = 128
    rest = 2 * main - 6 * (half - main)
    for parity in range(2):
        for tile in range(tiles):
            own_high, own_low = split_two(refs[tile][0, pl.ds(parity, half, stride=2), :])
            cross_high, cross_low = split_two(refs[tiles + tile][0, pl.ds(parity, half, stride=2), :])
            tail_high = [own_high[main:], cross_high[main:]]
            tail_low = [own_low[main:], cross_low[main:]]
            blocks = (
                [own_high[:main], cross_high[:main]],
                [own_low[:main], cross_low[:main]],
                tail_high + tail_high + tail_low + [jnp.zeros((rest, lanes), BF16)],
            )
            for i, block in enumerate(blocks):
                turned = jnp.concatenate(block, 0).T
                for s in range(out_ref.shape[2]):
                    first = max(s * share, tile * lanes)
                    last = min((s + 1) * share, (tile + 1) * lanes)
                    if first < last:
                        out_ref[0, parity, s, first - s * share : last - s * share, 2 * main * i : 2 * main * (i + 1)] = (
                            turned[first - tile * lanes : last - tile * lanes]
                        )


def lay_out(own, cross, share, padded):
    pairs, rows, slots = own.shape
    shares = slots // share
    tiles = (slots + 127) // 128

    def block(tile):
        return pl.BlockSpec((1, rows, 128), lambda step: (step, 0, tile))

    return pl.pallas_call(
        functools.partial(layout_kernel, share=share),
        grid=(pairs,),
        in_specs=[block(tile) for tile in range(tiles)] * 2,
        out_specs=pl.BlockSpec((1, 2, shares, padded, 768), lambda step: (step, 0, 0, 0, 0)),
        out_shape=jax.ShapeDtypeStruct((pairs, 2, shares, padded, 768), BF16),
        compiler_params=pltpu.CompilerParams(vmem_limit_bytes=VMEM_LIMIT),
        cost_estimate=pl.CostEstimate(
            flops=0, bytes_accessed=pairs * (2 * rows * slots * 4 + 2 * shares * padded * 768 * 2), transcendentals=0
        ),
        name="lay_out",
    )(*[own] * tiles, *[cross] * tiles)


def project_kernel(
    place_ref, wave_ref, keep_ref, recv_ref, keep_x_ref, recv_x_ref, table_ref, *refs, share, chunk, chunks
):
    outs, (high_ref, low_ref, tail_ref) = refs[:8], refs[8:]
    step = pl.program_id(0)
    each = pl.num_programs(0)
    group = each * chunks
    core = place_ref[0]
    chip = place_ref[1]
    chips = place_ref[2]
    first_m = wave_ref[core * group + chunk * each + step]
    half = keep_ref.shape[1]
    width = keep_ref.shape[2] // 2
    main = 128
    tail = half - main
    padded = table_ref.shape[3]
    side = jnp.where(chip < chips // 2, 1.0, -1.0)
    for parity in range(2):
        for j, (keep, recv) in enumerate(((keep_ref, recv_ref), (keep_x_ref, recv_x_ref))):
            if parity == 0:
                folded = keep[0] + recv[0]
            else:
                folded = side * (keep[0] - recv[0])
            high, low = split_two(folded)
            for member in range(2):
                part = slice(member * width, (member + 1) * width)
                high_ref[member, j * main : (j + 1) * main] = high[:main, part]
                low_ref[member, j * main : (j + 1) * main] = low[:main, part]
                for k, value in enumerate((high, low, high)):
                    at = (2 * k + j) * tail
                    tail_ref[member, at : at + tail] = value[main:, part]
        used = 6 * tail
        for member in range(2):
            tail_ref[member, used:] = jnp.zeros((2 * main - used, width), BF16)
        count = (NDEG - first_m - parity + 1) // 2
        for position in range(8):
            ahead, other = position // 2, position % 2
            owner = lax.rem(chip + ahead, chips)
            which = 2 * owner + jnp.where(other == 1, 1 - core, core)
            start = which * share
            out_ref = outs[position]

            def product(member):
                table = table_ref[0, parity, which]
                high_part = table[:, : 2 * main]
                return (
                    dot_nn(high_part, high_ref[member])
                    + dot_nn(high_part, low_ref[member])
                    + dot_nn(table[:, 2 * main : 4 * main], high_ref[member])
                    + dot_nn(table[:, 4 * main :], tail_ref[member])
                )

            slot = start + lax.broadcasted_iota(jnp.int32, (padded, width), 0)
            leading = slot < count
            valid = leading | (parity + 2 * (slot - count) <= first_m)
            main_member = jnp.where(start >= count, 1, 0)
            value = jnp.where(valid, product(main_member), 0.0)
            mixed = (start < count) & (start + share > count)
            for unit in range(each_static(refs, share)):
                if unit % 2 != parity:
                    continue
                rows = slice(unit * share, (unit + 1) * share)

                @pl.when(step == unit // 2)
                def _():
                    out_ref[rows, :] = value[:share]

                    @pl.when(mixed)
                    def _():
                        other_value = jnp.where(valid, product(1), 0.0)
                        out_ref[rows, :] = jnp.where(leading, value, other_value)[:share]


def each_static(refs, share):
    return refs[0].shape[0] // share


def project(place, wave, keep, recv, keep_x, recv_x, table, share, chunk, chunks):
    each, half, width = keep.shape
    rows = 2 * each * share
    rows = (rows + 7) // 8 * 8
    padded, depth = table.shape[3:]
    field = pl.BlockSpec((1, half, width), lambda step, *_: (step, 0, 0))
    table_spec = pl.BlockSpec((1,) + table.shape[1:], lambda step, *_: (chunk * each + step, 0, 0, 0, 0))
    out = pl.BlockSpec((rows, width // 2), lambda step, *_: (0, 0))
    scratch = pltpu.VMEM((2, 256, width // 2), BF16)
    return pl.pallas_call(
        functools.partial(project_kernel, share=share, chunk=chunk, chunks=chunks),
        grid_spec=pltpu.PrefetchScalarGridSpec(
            num_scalar_prefetch=2,
            grid=(each,),
            in_specs=[field, field, field, field, table_spec],
            out_specs=[out] * 8,
            scratch_shapes=[scratch, scratch, scratch],
        ),
        out_shape=[jax.ShapeDtypeStruct((rows, width // 2), F32)] * 8,
        compiler_params=pltpu.CompilerParams(vmem_limit_bytes=VMEM_LIMIT),
        cost_estimate=pl.CostEstimate(
            flops=2 * each * 2 * 9 * padded * 1024 * width // 2,
            bytes_accessed=each * (4 * half * width * 4 + 16 * padded * depth * 2 + 16 * share * width * 2),
            transcendentals=0,
        ),
        name="project",
    )(place, wave, keep, recv, keep_x, recv_x, table)


def finish_kernel(place_ref, wave_ref, *refs, share, chunk, chunks):
    parts, (out_ref, energy_ref) = refs[:6], refs[-2:]
    step = pl.program_id(0)
    each = out_ref.shape[0]
    group = each * chunks
    core = place_ref[0]
    which = 2 * place_ref[1] + core
    start = which * share
    lanes = 128
    for side in range(2):

        @pl.when(step == side)
        def _():
            terms = []
            spots = []
            for pair in range(each):
                first_m = wave_ref[(core if side == 0 else 1 - core) * group + chunk * each + pair]
                for parity in range(2):
                    unit = 2 * pair + parity
                    rows = slice(unit * share, (unit + 1) * share)
                    a, b, c = (part[rows, :] for part in parts[3 * side : 3 * side + 3])
                    value = (a + b + c).T
                    out_ref[pair, parity] = value.reshape(out_ref.shape[2:])
                    squares = jnp.sum(value * value, axis=0, keepdims=True)
                    squares = jnp.concatenate([squares, jnp.zeros((1, lanes - share), F32)], 1)
                    column = lax.broadcasted_iota(jnp.int32, (1, lanes), 1)
                    slot = start + column
                    count = (NDEG - first_m - parity + 1) // 2
                    leading = slot < count
                    second_m = NDEG - 1 - first_m
                    degree = jnp.where(leading, first_m + parity + 2 * slot, second_m + parity + 2 * (slot - count))
                    owner_m = jnp.where(leading, first_m, second_m)
                    usable = (column < share) & (degree >= 1) & (degree <= NDEG - 1)
                    safe = jnp.maximum(degree, 1).astype(F32)
                    factor = jnp.where(owner_m == 0, 1.0, 2.0)
                    terms.append(jnp.where(usable, factor * squares / (4.0 * safe * (safe + 1.0)), 0.0))
                    spots.append(jnp.where(usable, degree - 1, 0))
            term = jnp.concatenate(terms, 1)
            spot = jnp.concatenate(spots, 1)
            size = term.shape[1]
            band = lax.broadcasted_iota(jnp.int32, (16, size), 0)
            left = jnp.where(spot // lanes == band, term, 0.0)
            line = lax.broadcasted_iota(jnp.int32, (lanes, size), 0)
            right = jnp.where(spot % lanes == line, 1.0, 0.0).astype(BF16)
            first = left.astype(BF16)
            rest = left - first.astype(F32)
            second = rest.astype(BF16)
            third = (rest - second.astype(F32)).astype(BF16)
            total = dot_nt(first, right) + dot_nt(second, right) + dot_nt(third, right)
            if side == 0:
                energy_ref[...] = total
            else:
                energy_ref[...] += total


def finish(place, wave, parts, held, shape, share, chunk, chunks):
    pairs = shape[0]
    group = pairs // 2
    each = group // chunks
    rows, width = parts[0].shape

    def out_map(step, place_ref, wave_ref):
        core = jnp.where(step == 0, place_ref[0], 1 - place_ref[0])
        return (core * chunks + chunk, 0, 0, 0, 0)

    full = pl.BlockSpec((rows, width), lambda step, *_: (0, 0))
    operands = list(parts)
    in_specs = [full] * 6
    aliases = {}
    if held is not None:
        operands.append(held)
        in_specs.append(pl.BlockSpec(memory_space=pl.ANY))
        aliases = {8: 0}
    return pl.pallas_call(
        functools.partial(finish_kernel, share=share, chunk=chunk, chunks=chunks),
        grid_spec=pltpu.PrefetchScalarGridSpec(
            num_scalar_prefetch=2,
            grid=(2,),
            in_specs=in_specs,
            out_specs=[
                pl.BlockSpec((each,) + shape[1:], out_map),
                pl.BlockSpec((16, 128), lambda step, *_: (0, 0)),
            ],
        ),
        out_shape=[jax.ShapeDtypeStruct(shape, F32), jax.ShapeDtypeStruct((16, 128), F32)],
        input_output_aliases=aliases,
        compiler_params=pltpu.CompilerParams(vmem_limit_bytes=VMEM_LIMIT),
        cost_estimate=pl.CostEstimate(
            flops=10 * 6 * rows * width, bytes_accessed=10 * rows * width * 4, transcendentals=0
        ),
        name="finish",
    )(place, wave, *operands)


def all_sum(x):
    for axis, bit in (("band", 1), ("lev", 1), ("wave", 1), ("wave", 2), ("band", 2), ("wave", 4), ("band", 4)):
        size = lax.axis_size(axis)
        x = x + lax.ppermute(x, axis, [(i, i ^ bit) for i in range(size)])
    return x


def shards(fourier, legendre, pair_m, mirror):
    bands = lax.axis_size("band")
    chips = bands // 2
    rows, pairs, members, comps, levs = fourier.shape
    half_rows = rows // 2
    slots = legendre.shape[3]
    share = slots // bands
    padded = (share + 15) // 16 * 16
    position = lax.axis_index("band")
    chip, core = position // 2, position % 2
    place = jnp.stack([core, chip, jnp.int32(chips)]).astype(jnp.int32)

    north_base = position % chips * rows
    south_base = north_base + chips * rows
    partner = lax.dynamic_slice(mirror, (north_base,), (rows,)) - south_base
    plain = (jnp.arange(rows, dtype=jnp.int32) + half_rows) % rows
    index = jnp.where(position < chips, plain, partner).reshape(rows, 1)
    send_index, keep_index = index[:half_rows], index[half_rows:]
    field = jnp.transpose(fourier, (1, 2, 3, 4, 0)).reshape(pairs, members * comps * levs, rows)

    received = []
    for chunk in range(CHUNKS):
        own, cross = pick_rows(place, send_index, field, chunk, CHUNKS)
        received.append((send_along(own, chips // 2, 0), send_along(cross, chips // 2, 1)))

    group = pairs // 2
    table = legendre.reshape(pairs, rows, slots)
    own_table = lax.dynamic_slice_in_dim(table, core * group, group, 0)
    cross_table = send_along(lax.dynamic_slice_in_dim(table, (1 - core) * group, group, 0), 0, 1)
    kept, kept_cross = pick_rows(place, keep_index, field, 0, 1)
    kept_cross = send_along(kept_cross, 0, 1)
    table = lay_out(own_table, cross_table, share, padded)

    each = group // CHUNKS
    done = []
    for chunk in range(CHUNKS):
        here = slice(chunk * each, (chunk + 1) * each)
        mine, mine_x, up, up_x, far, far_x, down, down_x = project(
            place, pair_m, kept[here], received[chunk][0], kept_cross[here], received[chunk][1],
            table, share, chunk, CHUNKS,
        )
        far = send_along(far, 1, 0)
        far_x = send_along(far_x, -1, 0)
        up_x = send_along(up_x, 1, 1)
        down = send_along(down, -1, 0)
        mine_x = send_along(mine_x, 0, 1)
        up = send_along(up + far, 1, 0)
        down_x = send_along(down_x + far_x, -1, 1)
        done.append((mine, up, down, mine_x, up_x, down_x))

    shape = (pairs, 2, comps, levs, share)
    held = None
    energies = []
    for chunk in range(CHUNKS):
        held, energy = finish(place, pair_m, done[chunk], held, shape, share, chunk, CHUNKS)
        energies.append(energy)
    total = all_sum(functools.reduce(jnp.add, energies))
    return (held, jnp.log(total.reshape(-1)[: NDEG - 1]))


def solution(mesh):
    return jax.shard_map(
        shards,
        mesh=mesh,
        in_specs=(
            P("band", "wave", None, None, "lev"),
            P("wave", "band", None, None),
            P("wave"),
            P(),
        ),
        out_specs=(P("wave", None, None, "lev", "band"), P()),
        check_vma=False,
    )
```

time: 643 us -> 236 us (0.37); the launches traced: 633 us -> 235 us
  waiting for transfers between devices: 305 us -> 85.3 us
  local copies, waits for them, and re-layouts: 117 us -> 27.3 us
  other arithmetic: 82.2 us -> 1.15 us
  Pallas kernels: 0 us -> 77.3 us
  blocking collectives: 66.1 us -> 0 us
  matrix products: 41.8 us -> 0 us
  starting transfers between devices: 6.05 us -> 43.4 us
  between operations: 15.2 us -> 0.88 us
    unnamed x2 -> x0, waiting for transfers between devices: 205 us -> none
    pallas_call x0 -> x11, Pallas kernels: none -> 77.3 us  [the longest x3 33.6 us: project(): pl.pallas_call(functools.partial(project_kernel, share=share, chunk=chunk...]
    psum x1 -> x0, blocking collectives: 66.1 us -> none  [shards(): total = lax.psum(partial_energy, ('band', 'wave', 'lev'))]
    gather x4 -> x0, local copies, waits for them, and re-layouts: 42.4 us -> none  [the longest x1 19.8 us: shards(): south_part = jnp.where(north_side, incoming, fourier[second_partner])]
    dot_general x2 -> x0, matrix products: 41.8 us -> none  [project(): jnp.einsum('qpk,pqc->pkc', flat, legendre[:, :, parity, :], precision=lax...]
    ppermute x1 -> x36, starting transfers between devices: 6.02 us -> 43.4 us  [the longest x29 31.6 us: send_along(): return lax.ppermute(x, 'band', pairs)]
    select_n x10 -> x1, other arithmetic: 36 us -> 0.77 us  [shards(): index = jnp.where(position < chips, plain, partner).reshape(rows, 1)]
    unnamed x20 -> x6, local copies, waits for them, and re-layouts: 19.1 us -> 0.01 us
  transfers between devices with their start and end apart: 2 -> 36, of which waited for: 2 -> 22; matrix products, arithmetic and copies ran while one was open for 6% -> 1% of each run, Pallas kernels for 0% -> 32%
where the time goes in v1:
time: 236 us; the launch traced here: 235 us
  waiting for transfers between devices  85.3 us (36%)
  Pallas kernels  77.3 us (33%)
  starting transfers between devices  43.4 us (18%)
  local copies, waits for them, and re-layouts  27.3 us (12%)
    ppermute x29, waiting for transfers between devices, send_along(): return lax.ppermute(x, 'band', pairs)  69 us
    pallas_call x3, Pallas kernels, project(): pl.pallas_call(functools.partial(project_kernel, share=share, chunk=chunk...  33.6 us
    ppermute x29, starting transfers between devices, send_along(): return lax.ppermute(x, 'band', pairs)  31.6 us
    pallas_call x4, Pallas kernels, pick_rows(): pl.pallas_call(functools.partial(pick_kernel, own_steps=each), grid_spec=...  26.3 us
    ppermute x7, waiting for transfers between devices, all_sum(): x = x + lax.ppermute(x, axis, [(i, i ^ bit) for i in range(size)])  16.2 us
    reshape x1, local copies, waits for them, and re-layouts, shards(): table = legendre.reshape(pairs, rows, slots)  15 us
    ppermute x7, starting transfers between devices, all_sum(): x = x + lax.ppermute(x, axis, [(i, i ^ bit) for i in range(size)])  11.7 us
    pallas_call x1, Pallas kernels, lay_out(): pl.pallas_call(functools.partial(layout_kernel, share=share), grid=(pairs...  10.7 us
  transfers between devices with their start and end apart: 36, of which 22 were waited for; matrix products, arithmetic and copies ran while one was open for 1% of the time, Pallas kernels for 32%

profile of v1, /device:TPU:0, one launch (start us, length us, event | category | flops | bytes accessed | tf_op | source)
XLA Modules:
  0.0 235.4 jit_solution(10940777594658400054)
XLA Ops:
  0.7 15.0 %reshape.17 = f32[12,320,648]{2,1,0:T(8,128)} reshape(f32[12,160,2,648]{3,2,1,0:T(2,128)} %param.5) | data formatting | bytes 19906560 | tf_op jit(solution)/shard_map/reshape | solution.py:376
  15.6 9.6 %constant_dynamic-slice_fusion = (f32[6,320,648]{2,1,0:T(8,128)}, f32[6,320,648]{2,1,0:T(8,128)}) fusion(f32[12,320,648]{2,1,0:T(8,128)} %reshape.17, s32[]{:T(128)S(6)} %select_n.46, s32[]{:T(128)S(6)} %select_n.45), kind=kLoop, calls=%fused_computation.10 | loop fusion | bytes 19906568 | tf_op jit(solution)/shard_map/dynamic_slice | solution.py:378
  26.3 11.8 %pick_rows.4 = (f32[6,160,512]{2,1,0:T(8,128)S(1)}, f32[6,160,512]{2,1,0:T(8,128)}) custom-call(s32[3]{0:T(128)S(1)} %pad_add_fusion.place_ref, s32[160,1]{1,0:T(8,128)S(1)} %copy.8.index_ref, f32[12,512,320]{2,1,0:T(8,128)} %bitcast.11), custom_call_target="tpu_custom_call" | custom-call | flops 1258291200 | bytes 11796480 | tf_op jit(solution)/shard_map/pick_rows/pallas_call | solution.py:68
  38.7 5.0 %pick_rows.7 = (f32[2,160,512]{2,1,0:T(8,128)S(1)}, f32[2,160,512]{2,1,0:T(8,128)}) custom-call(s32[3]{0:T(128)S(1)} %pad_add_fusion.place_ref, s32[160,1]{1,0:T(8,128)S(1)} %copy.9.index_ref, f32[12,512,320]{2,1,0:T(8,128)} %bitcast.12), custom_call_target="tpu_custom_call" | custom-call | flops 419430400 | bytes 3932160 | tf_op jit(solution)/shard_map/pick_rows/pallas_call | solution.py:68
  43.7 3.3 %collective-permute-start.20 = (f32[2,160,512]{2,1,0:T(8,128)S(1)}, f32[2,160,512]{2,1,0:T(8,128)S(1)}, u32[]{:S(2)}, u32[]{:S(2)}) collective-permute-start(f32[2,160,512]{2,1,0:T(8,128)S(1)} %get-tuple-element.62), channel_id=1, source_target_pairs={{0,64},{16,80},{32,96},{48,112},{64,0},{80,16},{96,32},{112,48},{1... | collective-permute-start | bytes 1966088 | tf_op jit(solution)/shard_map/ppermute | solution.py:35
  46.9 5.2 %pick_rows.6 = (f32[2,160,512]{2,1,0:T(8,128)}, f32[2,160,512]{2,1,0:T(8,128)S(1)}) custom-call(s32[3]{0:T(128)S(1)} %pad_add_fusion.place_ref, s32[160,1]{1,0:T(8,128)S(1)} %copy.9.index_ref, f32[12,512,320]{2,1,0:T(8,128)} %bitcast.13), custom_call_target="tpu_custom_call" | custom-call | flops 419430400 | bytes 3932160 | tf_op jit(solution)/shard_map/pick_rows/pallas_call | solution.py:68
  52.2 2.9 %collective-permute-start.11 = (f32[2,160,512]{2,1,0:T(8,128)}, f32[2,160,512]{2,1,0:T(8,128)S(1)}, u32[]{:S(2)}, u32[]{:S(2)}) collective-permute-start(f32[2,160,512]{2,1,0:T(8,128)} %get-tuple-element.52), channel_id=1, source_target_pairs={{0,64},{16,80},{32,96},{48,112},{64,0},{80,16},{96,32},{112,48},{1... | collective-permute-start | bytes 1966088 | tf_op jit(solution)/shard_map/ppermute | solution.py:35
  55.2 7.5 %collective-permute-done.20.recv_ref = f32[2,160,512]{2,1,0:T(8,128)S(1)} collective-permute-done((f32[2,160,512]{2,1,0:T(8,128)S(1)}, f32[2,160,512]{2,1,0:T(8,128)S(1)}, u32[]{:S(2)}, u32[]{:S(2)}) %collective-permute-start.20) | collective-permute-done | bytes 655392 | tf_op jit(solution)/shard_map/ppermute | solution.py:35
  63.9 4.3 %pick_rows.5 = (f32[2,160,512]{2,1,0:T(8,128)S(1)}, f32[2,160,512]{2,1,0:T(8,128)S(1)}) custom-call(s32[3]{0:T(128)S(1)} %pad_add_fusion.place_ref, s32[160,1]{1,0:T(8,128)S(1)} %copy.9.index_ref, f32[12,512,320]{2,1,0:T(8,128)} %bitcast.14), custom_call_target="tpu_custom_call" | custom-call | flops 419430400 | bytes 3932160 | tf_op jit(solution)/shard_map/pick_rows/pallas_call | solution.py:68
  68.2 2.4 %collective-permute-start = (f32[2,160,512]{2,1,0:T(8,128)S(1)}, f32[2,160,512]{2,1,0:T(8,128)S(1)}, u32[]{:S(2)}, u32[]{:S(2)}) collective-permute-start(f32[2,160,512]{2,1,0:T(8,128)S(1)} %get-tuple-element.41), channel_id=1, source_target_pairs={{0,64},{16,80},{32,96},{48,112},{64,0},{80,16},{96,32},{112,48},{1... | collective-permute-start | bytes 1966088 | tf_op jit(solution)/shard_map/ppermute | solution.py:35
  70.6 2.7 %collective-permute-start.2 = (f32[2,160,512]{2,1,0:T(8,128)S(1)}, f32[2,160,512]{2,1,0:T(8,128)S(1)}, u32[]{:S(2)}, u32[]{:S(2)}) collective-permute-start(f32[2,160,512]{2,1,0:T(8,128)S(1)} %get-tuple-element.43), channel_id=1, source_target_pairs={{0,80},{16,64},{32,112},{48,96},{64,16},{80,0},{96,48},{112,32},{1... | collective-permute-start | bytes 1966088 | tf_op jit(solution)/shard_map/ppermute | solution.py:35
  73.3 1.7 fusion.4
  75.0 10.7 %lay_out.1.table_ref = bf16[6,2,8,96,768]{4,3,2,1,0:T(8,128)(2,1)} custom-call(f32[6,320,648]{2,1,0:T(8,128)S(1)} %bitcast.10, f32[6,320,648]{2,1,0:T(8,128)S(1)} %bitcast.10, f32[6,320,648]{2,1,0:T(8,128)S(1)} %bitcast.10, f32[6,320,648]{2,1,0:T(8,128)S(1)} %bitcast.10, f32[6,320,648]{2,1,0:T(8,128)S(1)} %bitcast.10, f32[6,320,648]{2,1,0:T(8,128)S(1)} %bitcast.10, ...), custom_call_target="tpu_custom_call" | custom-call | bytes 24109056 | tf_op jit(solution)/shard_map/lay_out/pallas_call | solution.py:129
  85.8 11.2 %project.5 = (f32[328,256]{1,0:T(8,128)S(1)}, f32[328,256]{1,0:T(8,128)S(1)}, f32[328,256]{1,0:T(8,128)S(1)}, f32[328,256]{1,0:T(8,128)S(1)}, f32[328,256]{1,0:T...) custom-call(s32[3]{0:T(128)S(1)} %pad_add_fusion.place_ref, s32[12]{0:T(128)S(1)} %copy-done, ...), custom_call_target="tpu_custom_call" | custom-call | flops 1811939328 | bytes 9994240 | tf_op jit(solution)/shard_map/project/pallas_call | solution.py:229
  97.0 1.3 collective-permute-start.27
  99.3 4.9 %collective-permute-done.12.recv_x_ref = f32[2,160,512]{2,1,0:T(8,128)S(1)} collective-permute-done((f32[2,160,512]{2,1,0:T(8,128)S(1)}, f32[2,160,512]{2,1,0:T(8,128)S(1)}, u32[]{:S(2)}, u32[]{:S(2)}) %collective-permute-start.12) | collective-permute-done | bytes 655392 | tf_op jit(solution)/shard_map/ppermute | solution.py:35
  104.2 2.0 collective-permute-start.24
  106.2 11.2 %project.4 = (f32[328,256]{1,0:T(8,128)S(1)}, f32[328,256]{1,0:T(8,128)S(1)}, f32[328,256]{1,0:T(8,128)S(1)}, f32[328,256]{1,0:T(8,128)S(1)}, f32[328,256]{1,0:T...) custom-call(s32[3]{0:T(128)S(1)} %pad_add_fusion.place_ref, s32[12]{0:T(128)S(1)} %copy-done, ...), custom_call_target="tpu_custom_call" | custom-call | flops 1811939328 | bytes 9994240 | tf_op jit(solution)/shard_map/project/pallas_call | solution.py:229
  117.4 1.6 collective-permute-done.recv_ref
  119.0 13.3 %collective-permute-done.2.recv_x_ref = f32[2,160,512]{2,1,0:T(8,128)S(1)} collective-permute-done((f32[2,160,512]{2,1,0:T(8,128)S(1)}, f32[2,160,512]{2,1,0:T(8,128)S(1)}, u32[]{:S(2)}, u32[]{:S(2)}) %collective-permute-start.2) | collective-permute-done | bytes 655392 | tf_op jit(solution)/shard_map/ppermute | solution.py:35
  132.3 1.8 collective-permute-start.26
  134.1 6.5 %collective-permute-done.27 = f32[328,256]{1,0:T(8,128)S(1)} collective-permute-done((f32[328,256]{1,0:T(8,128)S(1)}, f32[328,256]{1,0:T(8,128)S(1)}, u32[]{:S(2)}, u32[]{:S(2)}) %collective-permute-start.27) | collective-permute-done | bytes 335904 | tf_op jit(solution)/shard_map/ppermute | solution.py:35
  140.6 1.8 collective-permute-start.18
  142.7 11.2 %project.3 = (f32[328,256]{1,0:T(8,128)S(1)}, f32[328,256]{1,0:T(8,128)S(1)}, f32[328,256]{1,0:T(8,128)S(1)}, f32[328,256]{1,0:T(8,128)S(1)}, f32[328,256]{1,0:T...) custom-call(s32[3]{0:T(128)S(1)} %pad_add_fusion.place_ref, s32[12]{0:T(128)S(1)} %copy-done, ...), custom_call_target="tpu_custom_call" | custom-call | flops 1811939328 | bytes 9994240 | tf_op jit(solution)/shard_map/project/pallas_call | solution.py:229
  153.9 3.1 %collective-permute-start.15 = (f32[328,256]{1,0:T(8,128)S(1)}, f32[328,256]{1,0:T(8,128)S(1)}, u32[]{:S(2)}, u32[]{:S(2)}) collective-permute-start(f32[328,256]{1,0:T(8,128)S(1)} %get-tuple-element.57), channel_id=1, source_target_pairs={{0,96},{16,112},{32,0},{48,16},{64,32},{80,48},{96,64},{112,80},{1... | collective-permute-start | bytes 1007624 | tf_op jit(solution)/shard_map/ppermute | solution.py:35
  157.1 1.9 collective-permute-start.4
  159.3 6.0 %collective-permute-done.15.refs_2_ = f32[328,256]{1,0:T(8,128)S(1)} collective-permute-done((f32[328,256]{1,0:T(8,128)S(1)}, f32[328,256]{1,0:T(8,128)S(1)}, u32[]{:S(2)}, u32[]{:S(2)}) %collective-permute-start.15) | collective-permute-done | bytes 335904 | tf_op jit(solution)/shard_map/ppermute | solution.py:35
  165.5 6.7 %collective-permute-done.9 = f32[328,256]{1,0:T(8,128)S(1)} collective-permute-done((f32[328,256]{1,0:T(8,128)S(1)}, f32[328,256]{1,0:T(8,128)S(1)}, u32[]{:S(2)}, u32[]{:S(2)}) %collective-permute-start.9) | collective-permute-done | bytes 335904 | tf_op jit(solution)/shard_map/ppermute | solution.py:35
  172.8 2.4 %collective-permute-done.17.refs_4_ = f32[328,256]{1,0:T(8,128)S(1)} collective-permute-done((f32[328,256]{1,0:T(8,128)S(1)}, f32[328,256]{1,0:T(8,128)S(1)}, u32[]{:S(2)}, u32[]{:S(2)}) %collective-permute-start.17) | collective-permute-done | bytes 335904 | tf_op jit(solution)/shard_map/ppermute | solution.py:35
  176.1 3.3 %collective-permute-done.28.refs_5_ = f32[328,256]{1,0:T(8,128)S(1)} collective-permute-done((f32[328,256]{1,0:T(8,128)S(1)}, f32[328,256]{1,0:T(8,128)S(1)}, u32[]{:S(2)}, u32[]{:S(2)}) %collective-permute-start.28) | collective-permute-done | bytes 335904 | tf_op jit(solution)/shard_map/ppermute | solution.py:35
  179.4 4.1 %collective-permute-done.23.refs_1_ = f32[328,256]{1,0:T(8,128)S(1)} collective-permute-done((f32[328,256]{1,0:T(8,128)S(1)}, f32[328,256]{1,0:T(8,128)S(1)}, u32[]{:S(2)}, u32[]{:S(2)}) %collective-permute-start.23) | collective-permute-done | bytes 335904 | tf_op jit(solution)/shard_map/ppermute | solution.py:35
  183.5 3.1 %collective-permute-done.19.refs_5_ = f32[328,256]{1,0:T(8,128)S(1)} collective-permute-done((f32[328,256]{1,0:T(8,128)S(1)}, f32[328,256]{1,0:T(8,128)S(1)}, u32[]{:S(2)}, u32[]{:S(2)}) %collective-permute-start.19) | collective-permute-done | bytes 335904 | tf_op jit(solution)/shard_map/ppermute | solution.py:35
  186.6 3.1 %collective-permute-start.10 = (f32[328,256]{1,0:T(8,128)S(1)}, f32[328,256]{1,0:T(8,128)S(1)}, u32[]{:S(2)}, u32[]{:S(2)}) collective-permute-start(f32[328,256]{1,0:T(8,128)S(1)} %add.87), channel_id=1, source_target_pairs={{0,112},{16,96},{32,16},{48,0},{64,48},{80,32},{96,80},{112,64},{1... | collective-permute-start | bytes 1007624 | tf_op jit(solution)/shard_map/ppermute | solution.py:35
  191.4 2.2 finish.3
  193.6 2.2 finish.4
  196.8 2.9 %collective-permute-done.10.refs_5_ = f32[328,256]{1,0:T(8,128)S(1)} collective-permute-done((f32[328,256]{1,0:T(8,128)S(1)}, f32[328,256]{1,0:T(8,128)S(1)}, u32[]{:S(2)}, u32[]{:S(2)}) %collective-permute-start.10) | collective-permute-done | bytes 335904 | tf_op jit(solution)/shard_map/ppermute | solution.py:35
  199.7 4.9 %collective-permute-done.5.refs_1_ = f32[328,256]{1,0:T(8,128)S(1)} collective-permute-done((f32[328,256]{1,0:T(8,128)S(1)}, f32[328,256]{1,0:T(8,128)S(1)}, u32[]{:S(2)}, u32[]{:S(2)}) %collective-permute-start.5) | collective-permute-done | bytes 335904 | tf_op jit(solution)/shard_map/ppermute | solution.py:35
  204.5 2.2 finish.5
  207.9 3.0 %collective-permute-start.30 = (f32[16,128]{1,0:T(8,128)S(1)}, f32[16,128]{1,0:T(8,128)S(1)}, u32[]{:S(2)}, u32[]{:S(2)}) collective-permute-start(f32[16,128]{1,0:T(8,128)S(1)} %add.94), channel_id=1, source_target_pairs={{0,1},{1,0},{2,3},{3,2},{4,5},{5,4},{6,7},{7,6},{8,9},{9,8},{10,11... | collective-permute-start | bytes 24584 | tf_op jit(solution)/shard_map/ppermute | solution.py:346
  210.9 2.1 collective-permute-done.30
  213.1 1.5 collective-permute-start.31
  214.6 2.1 collective-permute-done.31
  216.7 2.0 collective-permute-start.32
  218.8 1.6 collective-permute-done.32
  220.9 3.2 %collective-permute-done.33 = f32[16,128]{1,0:T(8,128)S(1)} collective-permute-done((f32[16,128]{1,0:T(8,128)S(1)}, f32[16,128]{1,0:T(8,128)S(1)}, u32[]{:S(2)}, u32[]{:S(2)}) %collective-permute-start.33) | collective-permute-done | bytes 8224 | tf_op jit(solution)/shard_map/ppermute | solution.py:346
  224.1 3.9 %collective-permute-start.34 = (f32[16,128]{1,0:T(8,128)S(1)}, f32[16,128]{1,0:T(8,128)S(1)}, u32[]{:S(2)}, u32[]{:S(2)}) collective-permute-start(f32[16,128]{1,0:T(8,128)S(1)} %add.98), channel_id=1, source_target_pairs={{0,8},{2,10},{4,12},{6,14},{8,0},{10,2},{12,4},{14,6},{1,9},{3,11}... | collective-permute-start | bytes 24584 | tf_op jit(solution)/shard_map/ppermute | solution.py:346
  228.0 1.6 collective-permute-done.34
  230.4 4.4 %collective-permute-done.35 = f32[16,128]{1,0:T(8,128)S(1)} collective-permute-done((f32[16,128]{1,0:T(8,128)S(1)}, f32[16,128]{1,0:T(8,128)S(1)}, u32[]{:S(2)}, u32[]{:S(2)}) %collective-permute-start.35) | collective-permute-done | bytes 8224 | tf_op jit(solution)/shard_map/ppermute | solution.py:346
  (66 shorter events, 12.0 us)
Async XLA Ops:
  25.2 45.4 %collective-permute-start.3 = (f32[6,320,648]{2,1,0:T(8,128)}, f32[6,320,648]{2,1,0:T(8,128)}, u32[]{:S(2)}, u32[]{:S(2)}) collective-permute-start(f32[6,320,648]{2,1,0:T(8,128)} %get-tuple-element.78), channel_id=1, source_target_pairs={{0,16},{16,0},{32,48},{48,32},{64,80},{80,64},{96,112},{112,96},{1... | collective-permute-start | bytes 14929928 | tf_op jit(solution)/shard_map/ppermute | solution.py:35
  38.1 30.1 %collective-permute-start.1 = (f32[6,160,512]{2,1,0:T(8,128)}, f32[6,160,512]{2,1,0:T(8,128)}, u32[]{:S(2)}, u32[]{:S(2)}) collective-permute-start(f32[6,160,512]{2,1,0:T(8,128)} %get-tuple-element.42), channel_id=1, source_target_pairs={{0,16},{16,0},{32,48},{48,32},{64,80},{80,64},{96,112},{112,96},{1... | collective-permute-start | bytes 5898248 | tf_op jit(solution)/shard_map/ppermute | solution.py:35
  43.7 19.1 %collective-permute-start.20 = (f32[2,160,512]{2,1,0:T(8,128)S(1)}, f32[2,160,512]{2,1,0:T(8,128)S(1)}, u32[]{:S(2)}, u32[]{:S(2)}) collective-permute-start(f32[2,160,512]{2,1,0:T(8,128)S(1)} %get-tuple-element.62), channel_id=1, source_target_pairs={{0,64},{16,80},{32,96},{48,112},{64,0},{80,16},{96,32},{112,48},{1... | collective-permute-start | bytes 1966088 | tf_op jit(solution)/shard_map/ppermute | solution.py:35
  46.9 38.9 %collective-permute-start.21 = (f32[2,160,512]{2,1,0:T(8,128)}, f32[2,160,512]{2,1,0:T(8,128)S(1)}, u32[]{:S(2)}, u32[]{:S(2)}) collective-permute-start(f32[2,160,512]{2,1,0:T(8,128)} %get-tuple-element.63), channel_id=1, source_target_pairs={{0,80},{16,64},{32,112},{48,96},{64,16},{80,0},{96,48},{112,32},{1... | collective-permute-start | bytes 1966088 | tf_op jit(solution)/shard_map/ppermute | solution.py:35
  52.2 46.2 %collective-permute-start.11 = (f32[2,160,512]{2,1,0:T(8,128)}, f32[2,160,512]{2,1,0:T(8,128)S(1)}, u32[]{:S(2)}, u32[]{:S(2)}) collective-permute-start(f32[2,160,512]{2,1,0:T(8,128)} %get-tuple-element.52), channel_id=1, source_target_pairs={{0,64},{16,80},{32,96},{48,112},{64,0},{80,16},{96,32},{112,48},{1... | collective-permute-start | bytes 1966088 | tf_op jit(solution)/shard_map/ppermute | solution.py:35
  62.8 12.2 %slice-start = ((s8[5898240]{0:T(1024)(128)(4,1)}), s8[4194304]{0:T(1024)(128)(4,1)S(1)}, s32[]{:S(2)}) async-start(s8[5898240]{0:T(1024)(128)(4,1)} %bitcast.9), calls=%async_computation | async-start | bytes 8388608
  62.8 12.3 %slice-start.1 = ((s8[5898240]{0:T(1024)(128)(4,1)}), s8[1703936]{0:T(1024)(128)(4,1)S(1)}, s32[]{:S(2)}) async-start(s8[5898240]{0:T(1024)(128)(4,1)} %bitcast.9), calls=%async_computation.1 | async-start | bytes 3407872
  62.8 41.5 %collective-permute-start.12 = (f32[2,160,512]{2,1,0:T(8,128)S(1)}, f32[2,160,512]{2,1,0:T(8,128)S(1)}, u32[]{:S(2)}, u32[]{:S(2)}) collective-permute-start(f32[2,160,512]{2,1,0:T(8,128)S(1)} %get-tuple-element.53), channel_id=1, source_target_pairs={{0,80},{16,64},{32,112},{48,96},{64,16},{80,0},{96,48},{112,32},{1... | collective-permute-start | bytes 1966088 | tf_op jit(solution)/shard_map/ppermute | solution.py:35
  68.2 50.8 %collective-permute-start = (f32[2,160,512]{2,1,0:T(8,128)S(1)}, f32[2,160,512]{2,1,0:T(8,128)S(1)}, u32[]{:S(2)}, u32[]{:S(2)}) collective-permute-start(f32[2,160,512]{2,1,0:T(8,128)S(1)} %get-tuple-element.41), channel_id=1, source_target_pairs={{0,64},{16,80},{32,96},{48,112},{64,0},{80,16},{96,32},{112,48},{1... | collective-permute-start | bytes 1966088 | tf_op jit(solution)/shard_map/ppermute | solution.py:35
  70.6 61.7 %collective-permute-start.2 = (f32[2,160,512]{2,1,0:T(8,128)S(1)}, f32[2,160,512]{2,1,0:T(8,128)S(1)}, u32[]{:S(2)}, u32[]{:S(2)}) collective-permute-start(f32[2,160,512]{2,1,0:T(8,128)S(1)} %get-tuple-element.43), channel_id=1, source_target_pairs={{0,80},{16,64},{32,112},{48,96},{64,16},{80,0},{96,48},{112,32},{1... | collective-permute-start | bytes 1966088 | tf_op jit(solution)/shard_map/ppermute | solution.py:35
  75.0 10.8 %copy-start = (s32[12]{0:T(128)S(1)}, s32[12]{0:T(128)}, u32[]{:S(2)}) copy-start(s32[12]{0:T(128)} %wave_ref.11) | copy-start | bytes 148
  97.0 43.6 %collective-permute-start.27 = (f32[328,256]{1,0:T(8,128)S(1)}, f32[328,256]{1,0:T(8,128)S(1)}, u32[]{:S(2)}, u32[]{:S(2)}) collective-permute-start(f32[328,256]{1,0:T(8,128)S(1)} %get-tuple-element.71), channel_id=1, source_target_pairs={{0,96},{16,112},{32,0},{48,16},{64,32},{80,48},{96,64},{112,80},{1... | collective-permute-start | bytes 1007624 | tf_op jit(solution)/shard_map/ppermute | solution.py:35
  98.3 44.1 %collective-permute-start.22 = (f32[328,256]{1,0:T(8,128)S(1)}, f32[328,256]{1,0:T(8,128)S(1)}, u32[]{:S(2)}, u32[]{:S(2)}) collective-permute-start(f32[328,256]{1,0:T(8,128)S(1)} %get-tuple-element.66), channel_id=1, source_target_pairs={{0,32},{16,48},{32,64},{48,80},{64,96},{80,112},{96,0},{112,16},{1... | collective-permute-start | bytes 1007624 | tf_op jit(solution)/shard_map/ppermute | solution.py:35
  104.2 49.6 %collective-permute-start.24 = (f32[328,256]{1,0:T(8,128)S(1)}, f32[328,256]{1,0:T(8,128)S(1)}, u32[]{:S(2)}, u32[]{:S(2)}) collective-permute-start(f32[328,256]{1,0:T(8,128)S(1)} %get-tuple-element.67), channel_id=1, source_target_pairs={{0,96},{16,112},{32,0},{48,16},{64,32},{80,48},{96,64},{112,80},{1... | collective-permute-start | bytes 1007624 | tf_op jit(solution)/shard_map/ppermute | solution.py:35
  119.0 37.9 %collective-permute-start.25 = (f32[328,256]{1,0:T(8,128)S(1)}, f32[328,256]{1,0:T(8,128)S(1)}, u32[]{:S(2)}, u32[]{:S(2)}) collective-permute-start(f32[328,256]{1,0:T(8,128)S(1)} %get-tuple-element.68), channel_id=1, source_target_pairs={{0,16},{16,0},{32,48},{48,32},{64,80},{80,64},{96,112},{112,96},{1... | collective-permute-start | bytes 1007624 | tf_op jit(solution)/shard_map/ppermute | solution.py:35
  132.3 24.6 %collective-permute-start.26 = (f32[328,256]{1,0:T(8,128)S(1)}, f32[328,256]{1,0:T(8,128)S(1)}, u32[]{:S(2)}, u32[]{:S(2)}) collective-permute-start(f32[328,256]{1,0:T(8,128)S(1)} %get-tuple-element.69), channel_id=1, source_target_pairs={{0,48},{16,32},{32,80},{48,64},{64,112},{80,96},{96,16},{112,0},{1... | collective-permute-start | bytes 1007624 | tf_op jit(solution)/shard_map/ppermute | solution.py:35
  140.6 16.5 %collective-permute-start.18 = (f32[328,256]{1,0:T(8,128)S(1)}, f32[328,256]{1,0:T(8,128)S(1)}, u32[]{:S(2)}, u32[]{:S(2)}) collective-permute-start(f32[328,256]{1,0:T(8,128)S(1)} %get-tuple-element.61), channel_id=1, source_target_pairs={{0,96},{16,112},{32,0},{48,16},{64,32},{80,48},{96,64},{112,80},{1... | collective-permute-start | bytes 1007624 | tf_op jit(solution)/shard_map/ppermute | solution.py:35
  142.4 16.7 %collective-permute-start.13 = (f32[328,256]{1,0:T(8,128)S(1)}, f32[328,256]{1,0:T(8,128)S(1)}, u32[]{:S(2)}, u32[]{:S(2)}) collective-permute-start(f32[328,256]{1,0:T(8,128)S(1)} %get-tuple-element.56), channel_id=1, source_target_pairs={{0,32},{16,48},{32,64},{48,80},{64,96},{80,112},{96,0},{112,16},{1... | collective-permute-start | bytes 1007624 | tf_op jit(solution)/shard_map/ppermute | solution.py:35
  153.9 11.4 %collective-permute-start.15 = (f32[328,256]{1,0:T(8,128)S(1)}, f32[328,256]{1,0:T(8,128)S(1)}, u32[]{:S(2)}, u32[]{:S(2)}) collective-permute-start(f32[328,256]{1,0:T(8,128)S(1)} %get-tuple-element.57), channel_id=1, source_target_pairs={{0,96},{16,112},{32,0},{48,16},{64,32},{80,48},{96,64},{112,80},{1... | collective-permute-start | bytes 1007624 | tf_op jit(solution)/shard_map/ppermute | solution.py:35
  156.9 8.5 %collective-permute-start.16 = (f32[328,256]{1,0:T(8,128)S(1)}, f32[328,256]{1,0:T(8,128)S(1)}, u32[]{:S(2)}, u32[]{:S(2)}) collective-permute-start(f32[328,256]{1,0:T(8,128)S(1)} %get-tuple-element.58), channel_id=1, source_target_pairs={{0,16},{16,0},{32,48},{48,32},{64,80},{80,64},{96,112},{112,96},{1... | collective-permute-start | bytes 1007624 | tf_op jit(solution)/shard_map/ppermute | solution.py:35
  156.9 15.3 %collective-permute-start.9 = (f32[328,256]{1,0:T(8,128)S(1)}, f32[328,256]{1,0:T(8,128)S(1)}, u32[]{:S(2)}, u32[]{:S(2)}) collective-permute-start(f32[328,256]{1,0:T(8,128)S(1)} %get-tuple-element.51), channel_id=1, source_target_pairs={{0,96},{16,112},{32,0},{48,16},{64,32},{80,48},{96,64},{112,80},{1... | collective-permute-start | bytes 1007624 | tf_op jit(solution)/shard_map/ppermute | solution.py:35
  157.1 15.5 %collective-permute-start.4 = (f32[328,256]{1,0:T(8,128)S(1)}, f32[328,256]{1,0:T(8,128)S(1)}, u32[]{:S(2)}, u32[]{:S(2)}) collective-permute-start(f32[328,256]{1,0:T(8,128)S(1)} %get-tuple-element.46), channel_id=1, source_target_pairs={{0,32},{16,48},{32,64},{48,80},{64,96},{80,112},{96,0},{112,16},{1... | collective-permute-start | bytes 1007624 | tf_op jit(solution)/shard_map/ppermute | solution.py:35
  159.2 16.0 %collective-permute-start.17 = (f32[328,256]{1,0:T(8,128)S(1)}, f32[328,256]{1,0:T(8,128)S(1)}, u32[]{:S(2)}, u32[]{:S(2)}) collective-permute-start(f32[328,256]{1,0:T(8,128)S(1)} %get-tuple-element.59), channel_id=1, source_target_pairs={{0,48},{16,32},{32,80},{48,64},{64,112},{80,96},{96,16},{112,0},{1... | collective-permute-start | bytes 1007624 | tf_op jit(solution)/shard_map/ppermute | solution.py:35
  165.3 14.1 %collective-permute-start.28 = (f32[328,256]{1,0:T(8,128)S(1)}, f32[328,256]{1,0:T(8,128)S(1)}, u32[]{:S(2)}, u32[]{:S(2)}) collective-permute-start(f32[328,256]{1,0:T(8,128)S(1)} %add.91), channel_id=1, source_target_pairs={{0,112},{16,96},{32,16},{48,0},{64,48},{80,32},{96,80},{112,64},{1... | collective-permute-start | bytes 1007624 | tf_op jit(solution)/shard_map/ppermute | solution.py:35
  165.5 18.0 %collective-permute-start.23 = (f32[328,256]{1,0:T(8,128)S(1)}, f32[328,256]{1,0:T(8,128)S(1)}, u32[]{:S(2)}, u32[]{:S(2)}) collective-permute-start(f32[328,256]{1,0:T(8,128)S(1)} %add.90), channel_id=1, source_target_pairs={{0,32},{16,48},{32,64},{48,80},{64,96},{80,112},{96,0},{112,16},{1... | collective-permute-start | bytes 1007624 | tf_op jit(solution)/shard_map/ppermute | solution.py:35
  172.2 14.4 %collective-permute-start.19 = (f32[328,256]{1,0:T(8,128)S(1)}, f32[328,256]{1,0:T(8,128)S(1)}, u32[]{:S(2)}, u32[]{:S(2)}) collective-permute-start(f32[328,256]{1,0:T(8,128)S(1)} %add.89), channel_id=1, source_target_pairs={{0,112},{16,96},{32,16},{48,0},{64,48},{80,32},{96,80},{112,64},{1... | collective-permute-start | bytes 1007624 | tf_op jit(solution)/shard_map/ppermute | solution.py:35
  172.7 18.0 %collective-permute-start.14 = (f32[328,256]{1,0:T(8,128)S(1)}, f32[328,256]{1,0:T(8,128)S(1)}, u32[]{:S(2)}, u32[]{:S(2)}) collective-permute-start(f32[328,256]{1,0:T(8,128)S(1)} %add.88), channel_id=1, source_target_pairs={{0,32},{16,48},{32,64},{48,80},{64,96},{80,112},{96,0},{112,16},{1... | collective-permute-start | bytes 1007624 | tf_op jit(solution)/shard_map/ppermute | solution.py:35
  175.2 20.7 %collective-permute-start.6 = (f32[328,256]{1,0:T(8,128)S(1)}, f32[328,256]{1,0:T(8,128)S(1)}, u32[]{:S(2)}, u32[]{:S(2)}) collective-permute-start(f32[328,256]{1,0:T(8,128)S(1)} %get-tuple-element.47), channel_id=1, source_target_pairs={{0,96},{16,112},{32,0},{48,16},{64,32},{80,48},{96,64},{112,80},{1... | collective-permute-start | bytes 1007624 | tf_op jit(solution)/shard_map/ppermute | solution.py:35
  179.4 16.5 %collective-permute-start.7 = (f32[328,256]{1,0:T(8,128)S(1)}, f32[328,256]{1,0:T(8,128)S(1)}, u32[]{:S(2)}, u32[]{:S(2)}) collective-permute-start(f32[328,256]{1,0:T(8,128)S(1)} %get-tuple-element.48), channel_id=1, source_target_pairs={{0,16},{16,0},{32,48},{48,32},{64,80},{80,64},{96,112},{112,96},{1... | collective-permute-start | bytes 1007624 | tf_op jit(solution)/shard_map/ppermute | solution.py:35
  183.5 13.3 %collective-permute-start.8 = (f32[328,256]{1,0:T(8,128)S(1)}, f32[328,256]{1,0:T(8,128)S(1)}, u32[]{:S(2)}, u32[]{:S(2)}) collective-permute-start(f32[328,256]{1,0:T(8,128)S(1)} %get-tuple-element.49), channel_id=1, source_target_pairs={{0,48},{16,32},{32,80},{48,64},{64,112},{80,96},{96,16},{112,0},{1... | collective-permute-start | bytes 1007624 | tf_op jit(solution)/shard_map/ppermute | solution.py:35
  186.6 13.1 %collective-permute-start.10 = (f32[328,256]{1,0:T(8,128)S(1)}, f32[328,256]{1,0:T(8,128)S(1)}, u32[]{:S(2)}, u32[]{:S(2)}) collective-permute-start(f32[328,256]{1,0:T(8,128)S(1)} %add.87), channel_id=1, source_target_pairs={{0,112},{16,96},{32,16},{48,0},{64,48},{80,32},{96,80},{112,64},{1... | collective-permute-start | bytes 1007624 | tf_op jit(solution)/shard_map/ppermute | solution.py:35
  190.7 13.8 %collective-permute-start.5 = (f32[328,256]{1,0:T(8,128)S(1)}, f32[328,256]{1,0:T(8,128)S(1)}, u32[]{:S(2)}, u32[]{:S(2)}) collective-permute-start(f32[328,256]{1,0:T(8,128)S(1)} %add.86), channel_id=1, source_target_pairs={{0,32},{16,48},{32,64},{48,80},{64,96},{80,112},{96,0},{112,16},{1... | collective-permute-start | bytes 1007624 | tf_op jit(solution)/shard_map/ppermute | solution.py:35
  206.8 1.2 collective-permute-start.29
  207.9 5.2 %collective-permute-start.30 = (f32[16,128]{1,0:T(8,128)S(1)}, f32[16,128]{1,0:T(8,128)S(1)}, u32[]{:S(2)}, u32[]{:S(2)}) collective-permute-start(f32[16,128]{1,0:T(8,128)S(1)} %add.94), channel_id=1, source_target_pairs={{0,1},{1,0},{2,3},{3,2},{4,5},{5,4},{6,7},{7,6},{8,9},{9,8},{10,11... | collective-permute-start | bytes 24584 | tf_op jit(solution)/shard_map/ppermute | solution.py:346
  213.1 3.7 %collective-permute-start.31 = (f32[16,128]{1,0:T(8,128)S(1)}, f32[16,128]{1,0:T(8,128)S(1)}, u32[]{:S(2)}, u32[]{:S(2)}) collective-permute-start(f32[16,128]{1,0:T(8,128)S(1)} %add.95), channel_id=1, source_target_pairs={{0,2},{2,0},{4,6},{6,4},{8,10},{10,8},{12,14},{14,12},{1,3},{3,1},... | collective-permute-start | bytes 24584 | tf_op jit(solution)/shard_map/ppermute | solution.py:346
  216.7 3.7 %collective-permute-start.32 = (f32[16,128]{1,0:T(8,128)S(1)}, f32[16,128]{1,0:T(8,128)S(1)}, u32[]{:S(2)}, u32[]{:S(2)}) collective-permute-start(f32[16,128]{1,0:T(8,128)S(1)} %add.96), channel_id=1, source_target_pairs={{0,4},{2,6},{4,0},{6,2},{8,12},{10,14},{12,8},{14,10},{1,5},{3,7},... | collective-permute-start | bytes 24584 | tf_op jit(solution)/shard_map/ppermute | solution.py:346
  220.4 3.7 %collective-permute-start.33 = (f32[16,128]{1,0:T(8,128)S(1)}, f32[16,128]{1,0:T(8,128)S(1)}, u32[]{:S(2)}, u32[]{:S(2)}) collective-permute-start(f32[16,128]{1,0:T(8,128)S(1)} %add.97), channel_id=1, source_target_pairs={{0,32},{16,48},{32,0},{48,16},{64,96},{80,112},{96,64},{112,80},{1... | collective-permute-start | bytes 24584 | tf_op jit(solution)/shard_map/ppermute | solution.py:346
  224.1 5.5 %collective-permute-start.34 = (f32[16,128]{1,0:T(8,128)S(1)}, f32[16,128]{1,0:T(8,128)S(1)}, u32[]{:S(2)}, u32[]{:S(2)}) collective-permute-start(f32[16,128]{1,0:T(8,128)S(1)} %add.98), channel_id=1, source_target_pairs={{0,8},{2,10},{4,12},{6,14},{8,0},{10,2},{12,4},{14,6},{1,9},{3,11}... | collective-permute-start | bytes 24584 | tf_op jit(solution)/shard_map/ppermute | solution.py:346
  229.6 5.2 %collective-permute-start.35 = (f32[16,128]{1,0:T(8,128)S(1)}, f32[16,128]{1,0:T(8,128)S(1)}, u32[]{:S(2)}, u32[]{:S(2)}) collective-permute-start(f32[16,128]{1,0:T(8,128)S(1)} %add.99), channel_id=1, source_target_pairs={{0,64},{16,80},{32,96},{48,112},{64,0},{80,16},{96,32},{112,48},{1... | collective-permute-start | bytes 24584 | tf_op jit(solution)/shard_map/ppermute | solution.py:346

commit v2 on v1

v2 whole, which is shorter than its diff:
```python
import functools

import jax
import jax.numpy as jnp
from jax import lax
from jax.experimental import pallas as pl
from jax.experimental.pallas import tpu as pltpu
from jax.sharding import PartitionSpec as P

NDEG = 1280
CHUNKS = 3
F32 = jnp.float32
BF16 = jnp.bfloat16
VMEM_LIMIT = 48 * 1024 * 1024


def behind(x, after):
    return lax.optimization_barrier((x, after))[0]


def split_two(x):
    high = x.astype(BF16)
    low = (x - high.astype(F32)).astype(BF16)
    return high, low


def dot_nt(a, b):
    return lax.dot_general(a, b, (((1,), (1,)), ((), ())), preferred_element_type=F32)


def dot_nn(a, b):
    return jnp.dot(a, b, preferred_element_type=F32)


def send_along(x, up, cross):
    size = lax.axis_size("band")
    chips = size // 2
    pairs = [(i, ((i // 2 + up) % chips) * 2 + ((i % 2) ^ cross)) for i in range(size)]
    return lax.ppermute(x, "band", pairs)


def pick_kernel(place_ref, index_ref, field_ref, out_ref):
    count = index_ref.shape[0]
    rows = field_ref.shape[2]
    lanes = lax.broadcasted_iota(jnp.int32, (count, rows), 1)
    chosen = jnp.where(index_ref[...] == lanes, 1.0, 0.0).astype(BF16)
    high, low = split_two(field_ref[0])
    out_ref[0] = dot_nt(chosen, high) + dot_nt(chosen, low)


def pick_rows(place, index, field, chunk, chunks):
    pairs, width, rows = field.shape
    each = pairs // chunks
    count = index.shape[0]

    def field_map(step, place_ref):
        return (chunk * each + step, 0, 0)

    return pl.pallas_call(
        pick_kernel,
        grid_spec=pltpu.PrefetchScalarGridSpec(
            num_scalar_prefetch=1,
            grid=(each,),
            in_specs=[
                pl.BlockSpec((count, 1), lambda step, place_ref: (0, 0)),
                pl.BlockSpec((1, width, rows), field_map),
            ],
            out_specs=pl.BlockSpec((1, count, width), lambda step, place_ref: (step, 0, 0)),
        ),
        out_shape=jax.ShapeDtypeStruct((each, count, width), F32),
        compiler_params=pltpu.CompilerParams(vmem_limit_bytes=VMEM_LIMIT),
        cost_estimate=pl.CostEstimate(
            flops=4 * each * count * width * rows,
            bytes_accessed=each * width * (rows + count) * 4,
            transcendentals=0,
        ),
        name="pick_rows",
    )(place, index, field)


def layout_kernel(*refs, share):
    out_ref = refs[-1]
    lanes = main = 128
    half = refs[0].shape[1]
    rest = main - 3 * (half - main)
    for parity in range(2):
        for tile, ref in enumerate(refs[:-1]):
            high, low = split_two(ref[0, :, parity, :])
            blocks = (
                high[:main],
                low[:main],
                jnp.concatenate([high[main:], high[main:], low[main:], jnp.zeros((rest, lanes), BF16)], 0),
            )
            for i, block in enumerate(blocks):
                turned = block.T
                for s in range(out_ref.shape[2]):
                    first = max(s * share, tile * lanes)
                    last = min((s + 1) * share, (tile + 1) * lanes)
                    if first < last:
                        out_ref[0, parity, s, first - s * share : last - s * share, main * i : main * (i + 1)] = turned[
                            first - tile * lanes : last - tile * lanes
                        ]


def lay_out(table, share, padded):
    pairs, half, _, slots = table.shape
    shares = slots // share
    tiles = (slots + 127) // 128

    def block(tile):
        return pl.BlockSpec((1, half, 2, 128), lambda step: (step, 0, 0, tile))

    return pl.pallas_call(
        functools.partial(layout_kernel, share=share),
        grid=(pairs,),
        in_specs=[block(tile) for tile in range(tiles)],
        out_specs=pl.BlockSpec((1, 2, shares, padded, 384), lambda step: (step, 0, 0, 0, 0)),
        out_shape=jax.ShapeDtypeStruct((pairs, 2, shares, padded, 384), BF16),
        compiler_params=pltpu.CompilerParams(vmem_limit_bytes=VMEM_LIMIT),
        cost_estimate=pl.CostEstimate(
            flops=0, bytes_accessed=pairs * (2 * half * slots * 4 + 2 * shares * padded * 384 * 2), transcendentals=0
        ),
        name="lay_out",
    )(*[table] * tiles)


def project_kernel(
    place_ref, wave_ref, keep_ref, recv_ref, table_ref, mine_ref, far_ref, cross_ref, both_ref, mixed_ref, *, share, chunk
):
    step = pl.program_id(0)
    each = pl.num_programs(0)
    core = place_ref[0]
    chip = place_ref[1]
    chips = place_ref[2]
    first_m = wave_ref[chunk * each + step]
    half = keep_ref.shape[1]
    width = keep_ref.shape[2] // 2
    main = 128
    tail = half - main
    padded = table_ref.shape[3]
    units = mine_ref.shape[0] // (table_ref.shape[2] // 2 * share)
    side = jnp.where(chip < chips // 2, 1.0, -1.0)
    for parity in range(2):
        if parity == 0:
            folded = keep_ref[0] + recv_ref[0]
        else:
            folded = side * (keep_ref[0] - recv_ref[0])
        high, low = split_two(folded)
        for member in range(2):
            part = slice(member * width, (member + 1) * width)
            both_ref[member, :main] = high[:main, part]
            both_ref[member, main:] = low[:main, part]
            mixed_ref[member, :main] = high[:main, part]
            for k, value in enumerate((high, low, high)):
                at = main + k * tail
                mixed_ref[member, at : at + tail] = value[main:, part]
            mixed_ref[member, main + 3 * tail :] = jnp.zeros((main - 3 * tail, width), BF16)
        count = (NDEG - first_m - parity + 1) // 2
        for position in range(table_ref.shape[2]):
            ahead, other = position // 2, position % 2
            owner = lax.rem(chip + ahead, chips)
            which = 2 * owner + jnp.where(other == 1, 1 - core, core)
            start = which * share
            out_ref, place_at = mine_ref, ahead
            if other:
                out_ref, place_at = (far_ref, 0) if ahead == 2 else (cross_ref, min(ahead, 2))

            def product(member):
                table = table_ref[0, parity, which]
                high_part = table[:, :main]
                return dot_nn(jnp.concatenate([high_part, high_part], 1), both_ref[member]) + dot_nn(
                    table[:, main:], mixed_ref[member]
                )

            slot = start + lax.broadcasted_iota(jnp.int32, (padded, width), 0)
            leading = slot < count
            valid = leading | (parity + 2 * (slot - count) <= first_m)
            main_member = jnp.where(start >= count, 1, 0)
            value = jnp.where(valid, product(main_member), 0.0)
            mixed = (start < count) & (start + share > count)
            for unit in range(parity, units, 2):
                rows = slice((place_at * units + unit) * share, (place_at * units + unit + 1) * share)

                @pl.when(step == unit // 2)
                def _():
                    out_ref[rows, :] = value[:share]

                    @pl.when(mixed)
                    def _():
                        second = jnp.where(valid, product(1), 0.0)
                        out_ref[rows, :] = jnp.where(leading, value, second)[:share]


def project(place, wave, keep, recv, table, share, chunk):
    each, half, width = recv.shape
    shares, padded, depth = table.shape[2:]
    rows = 2 * each * share
    sizes = [rows * shares // 2, rows, rows * (shares // 2 - 1)]
    scratch = pltpu.VMEM((2, 256, width // 2), BF16)
    return pl.pallas_call(
        functools.partial(project_kernel, share=share, chunk=chunk),
        grid_spec=pltpu.PrefetchScalarGridSpec(
            num_scalar_prefetch=2,
            grid=(each,),
            in_specs=[
                pl.BlockSpec((1, half, width), lambda step, *_: (chunk * each + step, 0, 0)),
                pl.BlockSpec((1, half, width), lambda step, *_: (step, 0, 0)),
                pl.BlockSpec((1,) + table.shape[1:], lambda step, *_: (chunk * each + step, 0, 0, 0, 0)),
            ],
            out_specs=[pl.BlockSpec((size, width // 2), lambda step, *_: (0, 0)) for size in sizes],
            scratch_shapes=[scratch, scratch],
        ),
        out_shape=[jax.ShapeDtypeStruct((size, width // 2), F32) for size in sizes],
        compiler_params=pltpu.CompilerParams(vmem_limit_bytes=VMEM_LIMIT),
        cost_estimate=pl.CostEstimate(
            flops=2 * each * 2 * 9 * padded * 512 * width // 2,
            bytes_accessed=each * (2 * half * width * 4 + 2 * shares * padded * depth * 2) + 4 * sum(sizes) * width // 2,
            transcendentals=0,
        ),
        name="project",
    )(place, wave, keep, recv, table)


def finish_kernel(place_ref, wave_ref, mine_ref, cross_ref, up_ref, down_ref, *refs, share, chunk):
    out_ref, energy_ref = refs[-2:]
    each = out_ref.shape[0]
    core = place_ref[0]
    start = (2 * place_ref[1] + core) * share
    lanes = 128
    terms = []
    spots = []
    for pair in range(each):
        first_m = wave_ref[chunk * each + pair]
        for parity in range(2):
            unit = 2 * pair + parity
            rows = slice(unit * share, (unit + 1) * share)
            value = ((mine_ref[rows, :] + cross_ref[rows, :]) + (up_ref[rows, :] + down_ref[rows, :])).T
            out_ref[pair, parity] = value.reshape(out_ref.shape[2:])
            squares = jnp.sum(value * value, axis=0, keepdims=True)
            squares = jnp.concatenate([squares, jnp.zeros((1, lanes - share), F32)], 1)
            column = lax.broadcasted_iota(jnp.int32, (1, lanes), 1)
            slot = start + column
            count = (NDEG - first_m - parity + 1) // 2
            leading = slot < count
            second_m = NDEG - 1 - first_m
            degree = jnp.where(leading, first_m + parity + 2 * slot, second_m + parity + 2 * (slot - count))
            owner_m = jnp.where(leading, first_m, second_m)
            usable = (column < share) & (degree >= 1) & (degree <= NDEG - 1)
            safe = jnp.maximum(degree, 1).astype(F32)
            factor = jnp.where(owner_m == 0, 1.0, 2.0)
            terms.append(jnp.where(usable, factor * squares / (4.0 * safe * (safe + 1.0)), 0.0))
            spots.append(jnp.where(usable, degree - 1, 0))
    term = jnp.concatenate(terms, 1)
    spot = jnp.concatenate(spots, 1)
    size = term.shape[1]
    band = lax.broadcasted_iota(jnp.int32, (16, size), 0)
    left = jnp.where(spot // lanes == band, term, 0.0)
    line = lax.broadcasted_iota(jnp.int32, (lanes, size), 0)
    right = jnp.where(spot % lanes == line, 1.0, 0.0).astype(BF16)
    first = left.astype(BF16)
    rest = left - first.astype(F32)
    second = rest.astype(BF16)
    third = (rest - second.astype(F32)).astype(BF16)
    energy_ref[...] = dot_nt(first, right) + dot_nt(second, right) + dot_nt(third, right)


def finish(place, wave, parts, held, shape, share, chunk, chunks):
    each = shape[0] // chunks
    rows, width = parts[2].shape
    full = pl.BlockSpec((rows, width), lambda step, *_: (0, 0))
    operands = list(parts)
    in_specs = [full] * 4
    aliases = {}
    if held is not None:
        operands.append(held)
        in_specs.append(pl.BlockSpec(memory_space=pl.ANY))
        aliases = {6: 0}
    return pl.pallas_call(
        functools.partial(finish_kernel, share=share, chunk=chunk),
        grid_spec=pltpu.PrefetchScalarGridSpec(
            num_scalar_prefetch=2,
            grid=(1,),
            in_specs=in_specs,
            out_specs=[
                pl.BlockSpec((each,) + shape[1:], lambda step, *_: (chunk, 0, 0, 0, 0)),
                pl.BlockSpec((16, 128), lambda step, *_: (0, 0)),
            ],
        ),
        out_shape=[jax.ShapeDtypeStruct(shape, F32), jax.ShapeDtypeStruct((16, 128), F32)],
        input_output_aliases=aliases,
        compiler_params=pltpu.CompilerParams(vmem_limit_bytes=VMEM_LIMIT),
        cost_estimate=pl.CostEstimate(
            flops=10 * 4 * rows * width, bytes_accessed=6 * rows * width * 4, transcendentals=0
        ),
        name="finish",
    )(place, wave, *operands)


def all_sum(x):
    for axis, bit in (("band", 1), ("lev", 1), ("wave", 1), ("wave", 2), ("band", 2), ("wave", 4), ("band", 4)):
        size = lax.axis_size(axis)
        x = x + lax.ppermute(x, axis, [(i, i ^ bit) for i in range(size)])
    return x


def shards(fourier, legendre, pair_m, mirror):
    bands = lax.axis_size("band")
    chips = bands // 2
    rows, pairs, members, comps, levs = fourier.shape
    half_rows = rows // 2
    slots = legendre.shape[3]
    share = slots // bands
    padded = (share + 15) // 16 * 16
    position = lax.axis_index("band")
    chip, core = position // 2, position % 2
    place = jnp.stack([core, chip, jnp.int32(chips)]).astype(jnp.int32)

    north_base = position % chips * rows
    south_base = north_base + chips * rows
    partner = lax.dynamic_slice(mirror, (north_base,), (rows,)) - south_base
    plain = (jnp.arange(rows, dtype=jnp.int32) + half_rows) % rows
    index = jnp.where(position < chips, plain, partner).reshape(rows, 1)
    send_index, keep_index = index[:half_rows], index[half_rows:]
    field = jnp.transpose(fourier, (1, 2, 3, 4, 0)).reshape(pairs, members * comps * levs, rows)

    received = []
    for chunk in range(CHUNKS):
        piece = pick_rows(place, send_index, field, chunk, CHUNKS)
        received.append(send_along(piece, chips // 2, 0))
        place, legendre, piece = lax.optimization_barrier((place, legendre, piece))

    kept = pick_rows(place, keep_index, field, 0, 1)
    table = lay_out(legendre, share, padded)

    shape = (pairs, 2, comps, levs, share)
    length = 2 * pairs // CHUNKS * share
    cut = (length // 2 + 7) // 8 * 8

    mine, cross, far = {}, {}, {}

    def part(chunk, ahead, first=0, last=length):
        at = 0 if ahead == 2 else min(ahead, 2) * length
        other = cross[chunk][0 if ahead == 2 else 1][at + first : at + last]
        return mine[chunk][ahead * length + first : ahead * length + last] + other

    def begin(chunk, after):
        mine[chunk], *others = project(place, pair_m, kept, behind(received[chunk], after), table, share, chunk)
        cross[chunk] = [send_along(other, 0, 1) for other in others]

    def send_far(chunk, after):
        cross[chunk][0] = behind(cross[chunk][0], after)
        up, down = part(chunk, 2, 0, cut), part(chunk, 2, cut, length)
        far[chunk] = (send_along(up, 1, 0), send_along(down, -1, 0))
        return up, down

    def send_near(chunk, after):
        far_up, far_down = behind(far[chunk], after)
        up = part(chunk, 1) + jnp.pad(far_up, ((0, length - cut), (0, 0)))
        down = part(chunk, 3) + jnp.pad(far_down, ((cut, 0), (0, 0)))
        far[chunk] = (send_along(up, 1, 0), send_along(down, -1, 0))
        return up, down

    begin(0, ())
    begin(1, ())
    send_far(0, ())
    begin(2, far[0])
    send_far(1, ())
    send_far(2, ())
    for chunk in range(CHUNKS):
        send_near(chunk, ())
    held = None
    energies = []
    for chunk in range(CHUNKS):
        held, energy = finish(
            place, pair_m, (mine[chunk], cross[chunk][1]) + far[chunk], held, shape, share, chunk, CHUNKS
        )
        energies.append(energy)
    total = all_sum(functools.reduce(jnp.add, energies))
    return (held, jnp.log(total.reshape(-1)[: NDEG - 1]))


def solution(mesh):
    return jax.shard_map(
        shards,
        mesh=mesh,
        in_specs=(
            P("band", "wave", None, None, "lev"),
            P("wave", "band", None, None),
            P("wave"),
            P(),
        ),
        out_specs=(P("wave", None, None, "lev", "band"), P()),
        check_vma=False,
    )
```

time: 236 us -> 249 us (1.055)
  Pallas kernels: 77.3 us -> 128 us
  local copies, waits for them, and re-layouts: 27.3 us -> 2.82 us
  waiting for transfers between devices: 85.3 us -> 71 us
  other arithmetic: 1.15 us -> 7.39 us
  starting transfers between devices: 43.4 us -> 38.5 us
    pallas_call x1, Pallas kernels: 10.7 us -> 38.8 us  [lay_out(): pl.pallas_call(functools.partial(layout_kernel, share=share), grid=(pairs...]
    pallas_call x3, Pallas kernels: 33.6 us -> 56.6 us  [project(): pl.pallas_call(functools.partial(project_kernel, share=share, chunk=chunk...]
    reshape x1 -> x0, local copies, waits for them, and re-layouts: 15 us -> none  [shards(): table = legendre.reshape(pairs, rows, slots)]
    ppermute x29 -> x21, waiting for transfers between devices: 69 us -> 55.8 us  [send_along(): return lax.ppermute(x, 'band', pairs)]
    dynamic_slice x1 -> x0, local copies, waits for them, and re-layouts: 9.6 us -> none  [shards(): lax.dynamic_slice_in_dim(table, (1 - core) * group, group, 0)]
    add x6 -> x9, other arithmetic: 0.28 us -> 6.51 us  [the longest x6 3.42 us: part(): return mine[chunk][ahead * length + first:ahead * length + last] + other]
    ppermute x29 -> x21, starting transfers between devices: 31.6 us -> 25.7 us  [send_along(): return lax.ppermute(x, 'band', pairs)]
  transfers between devices with their start and end apart: 36 -> 28, of which waited for: 22 -> 18; matrix products, arithmetic and copies ran while one was open for 1% -> 3% of each run, Pallas kernels for 32% -> 49%
where the time goes in v2:
time: 249 us; the launch traced here: 248 us
  Pallas kernels  128 us (51%)
  waiting for transfers between devices  71 us (29%)
  starting transfers between devices  38.5 us (15%)
  other arithmetic  7.39 us (3%)
  local copies, waits for them, and re-layouts  2.82 us (1%)
    pallas_call x3, Pallas kernels, project(): pl.pallas_call(functools.partial(project_kernel, share=share, chunk=chunk...  56.6 us
    ppermute x21, waiting for transfers between devices, send_along(): return lax.ppermute(x, 'band', pairs)  55.8 us
    pallas_call x1, Pallas kernels, lay_out(): pl.pallas_call(functools.partial(layout_kernel, share=share), grid=(pairs...  38.8 us
    ppermute x21, starting transfers between devices, send_along(): return lax.ppermute(x, 'band', pairs)  25.7 us
    pallas_call x4, Pallas kernels, pick_rows(): pl.pallas_call(pick_kernel, grid_spec=pltpu.PrefetchScalarGridSpec(num_sc...  25.2 us
    ppermute x7, waiting for transfers between devices, all_sum(): x = x + lax.ppermute(x, axis, [(i, i ^ bit) for i in range(size)])  15.2 us
    ppermute x7, starting transfers between devices, all_sum(): x = x + lax.ppermute(x, axis, [(i, i ^ bit) for i in range(size)])  12.8 us
    pallas_call x3, Pallas kernels, finish(): pl.pallas_call(functools.partial(finish_kernel, share=share, chunk=chunk)...  7.04 us
  transfers between devices with their start and end apart: 28, of which 18 were waited for; matrix products, arithmetic and copies ran while one was open for 3% of the time, Pallas kernels for 49%

profile of v2, /device:TPU:0, one launch (start us, length us, event | category | flops | bytes accessed | tf_op | source)
XLA Modules:
  0.0 248.1 jit_solution(1946309703074404082)
XLA Ops:
  1.7 4.2 %pick_rows.4 = f32[4,160,512]{2,1,0:T(8,128)S(1)} custom-call(s32[3]{0:T(128)S(1)} %pad_add_fusion.place_ref, s32[160,1]{1,0:T(8,128)S(1)} %copy.8.index_ref, f32[12,512,320]{2,1,0:T(8,128)} %bitcast.9), custom_call_target="tpu_custom_call" | custom-call | flops 419430400 | bytes 3932160 | tf_op jit(solution)/shard_map/pick_rows/pallas_call | solution.py:59
  5.9 3.3 %collective-permute-start.1 = (f32[4,160,512]{2,1,0:T(8,128)S(1)}, f32[4,160,512]{2,1,0:T(8,128)S(1)}, u32[]{:S(2)}, u32[]{:S(2)}) collective-permute-start(f32[4,160,512]{2,1,0:T(8,128)S(1)} %pick_rows.4), channel_id=1, source_target_pairs={{0,64},{16,80},{32,96},{48,112},{64,0},{80,16},{96,32},{112,48},{1... | collective-permute-start | bytes 3932168 | tf_op jit(solution)/shard_map/ppermute | solution.py:39
  9.2 5.2 %pick_rows.5 = f32[4,160,512]{2,1,0:T(8,128)} custom-call(s32[3]{0:T(128)S(1)} %pad_add_fusion.place_ref, s32[160,1]{1,0:T(8,128)S(1)} %copy.8.index_ref, f32[12,512,320]{2,1,0:T(8,128)} %bitcast.10), custom_call_target="tpu_custom_call" | custom-call | flops 419430400 | bytes 3932160 | tf_op jit(solution)/shard_map/pick_rows/pallas_call | solution.py:59
  14.7 5.2 %pick_rows.6 = f32[4,160,512]{2,1,0:T(8,128)} custom-call(s32[3]{0:T(128)S(1)} %pad_add_fusion.place_ref, s32[160,1]{1,0:T(8,128)S(1)} %copy.8.index_ref, f32[12,512,320]{2,1,0:T(8,128)} %bitcast.11), custom_call_target="tpu_custom_call" | custom-call | flops 419430400 | bytes 3932160 | tf_op jit(solution)/shard_map/pick_rows/pallas_call | solution.py:59
  19.9 38.8 %lay_out.1.table_ref = bf16[12,2,8,96,384]{4,3,2,1,0:T(8,128)(2,1)} custom-call(f32[12,160,2,648]{3,2,1,0:T(2,128)} %refs_5_, f32[12,160,2,648]{3,2,1,0:T(2,128)} %refs_5_, f32[12,160,2,648]{3,2,1,0:T(2,128)} %refs_5_, f32[12,160,2,648]{3,2,1,0:T(2,128)} %refs_5_, f32[12,160,2,648]{3,2,1,0:T(2,128)} %refs_5_, f32[12,160,2,648]{3,2,1,0:T(2,128)} %refs_5_), custom_call_target="tpu_custom_call" | custom-call | bytes 24109056 | tf_op jit(solution)/shard_map/lay_out/pallas_call | solution.py:113
  58.8 10.6 %pick_rows.7.keep_ref = f32[12,160,512]{2,1,0:T(8,128)S(1)} custom-call(s32[3]{0:T(128)S(1)} %pad_add_fusion.place_ref, s32[160,1]{1,0:T(8,128)S(1)} %copy.11.index_ref, f32[12,512,320]{2,1,0:T(8,128)} %bitcast.12), custom_call_target="tpu_custom_call" | custom-call | flops 1258291200 | bytes 11796480 | tf_op jit(solution)/shard_map/pick_rows/pallas_call | solution.py:59
  69.4 1.9 copy-done
  71.3 18.9 %project.3 = (f32[2592,256]{1,0:T(8,128)}, f32[648,256]{1,0:T(8,128)S(1)}, f32[1944,256]{1,0:T(8,128)}) custom-call(s32[3]{0:T(128)S(1)} %pad_add_fusion.place_ref, s32[12]{0:T(128)S(1)} %copy-done.8, f32[12,160,512]{2,1,0:T(8,128)} %copy-done, f32[4,160,512]{2,1,0:T(8,128)S(1)} %collective-permute-done.1.recv_ref, bf16[12,2,8,96,384]{4,3,2,1,0:T(8,128)(2,1)} %lay_out.1.table_ref), custom_call_target="tpu_custom_call" | custom-call | flops 1811939328 | bytes 12648448 | tf_op jit(solution)/shard_map/project/pallas_call | solution.py:200
  90.2 3.3 %collective-permute-start = (f32[4,160,512]{2,1,0:T(8,128)}, f32[4,160,512]{2,1,0:T(8,128)S(1)}, u32[]{:S(2)}, u32[]{:S(2)}) collective-permute-start(f32[4,160,512]{2,1,0:T(8,128)} %pick_rows.6), channel_id=1, source_target_pairs={{0,64},{16,80},{32,96},{48,112},{64,0},{80,16},{96,32},{112,48},{1... | collective-permute-start | bytes 3932168 | tf_op jit(solution)/shard_map/ppermute | solution.py:39
  96.6 2.6 %collective-permute-start.4 = (f32[320,256]{1,0:T(8,128)S(1)}, f32[320,256]{1,0:T(8,128)S(1)}, u32[]{:S(2)}, u32[]{:S(2)}) collective-permute-start(f32[320,256]{1,0:T(8,128)S(1)} %slice_add_fusion.11), channel_id=1, source_target_pairs={{0,96},{16,112},{32,0},{48,16},{64,32},{80,48},{96,64},{112,80},{1... | collective-permute-start | bytes 983048 | tf_op jit(solution)/shard_map/ppermute | solution.py:39
  99.2 18.7 %project.5 = (f32[2592,256]{1,0:T(8,128)}, f32[648,256]{1,0:T(8,128)S(1)}, f32[1944,256]{1,0:T(8,128)}) custom-call(s32[3]{0:T(128)S(1)} %pad_add_fusion.place_ref, s32[12]{0:T(128)S(1)} %copy-done.8, f32[12,160,512]{2,1,0:T(8,128)} %copy-done, f32[4,160,512]{2,1,0:T(8,128)} %collective-permute-done.11.recv_ref, bf16[12,2,8,96,384]{4,3,2,1,0:T(8,128)(2,1)} %lay_out.1.table_ref), custom_call_target="tpu_custom_call" | custom-call | flops 1811939328 | bytes 12648448 | tf_op jit(solution)/shard_map/project/pallas_call | solution.py:200
  117.9 5.6 %collective-permute-done.recv_ref = f32[4,160,512]{2,1,0:T(8,128)S(1)} collective-permute-done((f32[4,160,512]{2,1,0:T(8,128)}, f32[4,160,512]{2,1,0:T(8,128)S(1)}, u32[]{:S(2)}, u32[]{:S(2)}) %collective-permute-start) | collective-permute-done | bytes 1310752 | tf_op jit(solution)/shard_map/ppermute | solution.py:39
  123.6 7.1 %collective-permute-done.4 = f32[320,256]{1,0:T(8,128)S(1)} collective-permute-done((f32[320,256]{1,0:T(8,128)S(1)}, f32[320,256]{1,0:T(8,128)S(1)}, u32[]{:S(2)}, u32[]{:S(2)}) %collective-permute-start.4) | collective-permute-done | bytes 327712 | tf_op jit(solution)/shard_map/ppermute | solution.py:39
  130.6 19.0 %project.4 = (f32[2592,256]{1,0:T(8,128)}, f32[648,256]{1,0:T(8,128)S(1)}, f32[1944,256]{1,0:T(8,128)}) custom-call(s32[3]{0:T(128)S(1)} %pad_add_fusion.place_ref, s32[12]{0:T(128)S(1)} %copy-done.8, f32[12,160,512]{2,1,0:T(8,128)} %copy-done, f32[4,160,512]{2,1,0:T(8,128)S(1)} %collective-permute-done.recv_ref, bf16[12,2,8,96,384]{4,3,2,1,0:T(8,128)(2,1)} %lay_out.1.table_ref), custom_call_target="tpu_custom_call" | custom-call | flops 1811939328 | bytes 12648448 | tf_op jit(solution)/shard_map/project/pallas_call | solution.py:200
  150.3 2.7 %collective-permute-start.15 = (f32[320,256]{1,0:T(8,128)S(1)}, f32[320,256]{1,0:T(8,128)S(1)}, u32[]{:S(2)}, u32[]{:S(2)}) collective-permute-start(f32[320,256]{1,0:T(8,128)S(1)} %slice_add_fusion.9), channel_id=1, source_target_pairs={{0,96},{16,112},{32,0},{48,16},{64,32},{80,48},{96,64},{112,80},{1... | collective-permute-start | bytes 983048 | tf_op jit(solution)/shard_map/ppermute | solution.py:39
  153.1 1.2 collective-permute-done.6
  154.3 1.6 collective-permute-start.14
  155.9 1.2 slice_add_fusion.7
  157.1 1.5 collective-permute-start.7
  158.8 1.4 collective-permute-done.15
  160.2 1.4 collective-permute-start.19
  161.6 4.6 %collective-permute-done.14 = f32[328,256]{1,0:T(8,128)S(1)} collective-permute-done((f32[328,256]{1,0:T(8,128)S(1)}, f32[328,256]{1,0:T(8,128)S(1)}, u32[]{:S(2)}, u32[]{:S(2)}) %collective-permute-start.14) | collective-permute-done | bytes 335904 | tf_op jit(solution)/shard_map/ppermute | solution.py:39
  166.2 1.5 collective-permute-start.8
  168.6 1.4 fusion.2
  170.0 6.9 %collective-permute-done.8 = f32[320,256]{1,0:T(8,128)S(1)} collective-permute-done((f32[320,256]{1,0:T(8,128)S(1)}, f32[320,256]{1,0:T(8,128)S(1)}, u32[]{:S(2)}, u32[]{:S(2)}) %collective-permute-start.8) | collective-permute-done | bytes 327712 | tf_op jit(solution)/shard_map/ppermute | solution.py:39
  177.2 2.9 %collective-permute-start.17 = (f32[648,256]{1,0:T(8,128)}, f32[648,256]{1,0:T(8,128)}, u32[]{:S(2)}, u32[]{:S(2)}) collective-permute-start(f32[648,256]{1,0:T(8,128)} %get-tuple-element.60), channel_id=1, source_target_pairs={{0,96},{16,112},{32,0},{48,16},{64,32},{80,48},{96,64},{112,80},{1... | collective-permute-start | bytes 1990664 | tf_op jit(solution)/shard_map/ppermute | solution.py:39
  180.1 1.5 fusion.4
  181.6 1.5 collective-permute-start.10
  183.1 4.5 %collective-permute-done.19.up_ref = f32[648,256]{1,0:T(8,128)S(1)} collective-permute-done((f32[648,256]{1,0:T(8,128)S(1)}, f32[648,256]{1,0:T(8,128)S(1)}, u32[]{:S(2)}, u32[]{:S(2)}) %collective-permute-start.19) | collective-permute-done | bytes 663584 | tf_op jit(solution)/shard_map/ppermute | solution.py:39
  188.0 3.1 %collective-permute-done.20.down_ref = f32[648,256]{1,0:T(8,128)S(1)} collective-permute-done((f32[648,256]{1,0:T(8,128)S(1)}, f32[648,256]{1,0:T(8,128)S(1)}, u32[]{:S(2)}, u32[]{:S(2)}) %collective-permute-start.20) | collective-permute-done | bytes 663584 | tf_op jit(solution)/shard_map/ppermute | solution.py:39
  191.1 2.0 finish.3
  193.1 8.8 %collective-permute-done.16.up_ref = f32[648,256]{1,0:T(8,128)S(1)} collective-permute-done((f32[648,256]{1,0:T(8,128)}, f32[648,256]{1,0:T(8,128)S(1)}, u32[]{:S(2)}, u32[]{:S(2)}) %collective-permute-start.16) | collective-permute-done | bytes 663584 | tf_op jit(solution)/shard_map/ppermute | solution.py:39
  201.9 3.6 %collective-permute-done.17.down_ref = f32[648,256]{1,0:T(8,128)} collective-permute-done((f32[648,256]{1,0:T(8,128)}, f32[648,256]{1,0:T(8,128)}, u32[]{:S(2)}, u32[]{:S(2)}) %collective-permute-start.17) | collective-permute-done | bytes 663584 | tf_op jit(solution)/shard_map/ppermute | solution.py:39
  205.4 3.1 %finish.4 = (f32[12,2,4,64,81]{4,3,2,1,0:T(8,128)}, f32[16,128]{1,0:T(8,128)S(1)}) custom-call(s32[3]{0:T(128)S(1)} %pad_add_fusion.place_ref, s32[12]{0:T(128)S(1)} %copy-done.8, f32[2592,256]{1,0:T(8,128)S(1)} %copy-done.2, f32[1944,256]{1,0:T(8,128)S(1)} %copy-done.5, ...), custom_call_target="tpu_custom_call", output_to_operand_aliasing={{0}: (6, {})} | custom-call | flops 6635520 | bytes 3981312 | tf_op jit(solution)/shard_map/finish/pallas_call | solution.py:278
  208.5 9.0 %collective-permute-done.10.down_ref = f32[648,256]{1,0:T(8,128)S(1)} collective-permute-done((f32[648,256]{1,0:T(8,128)}, f32[648,256]{1,0:T(8,128)S(1)}, u32[]{:S(2)}, u32[]{:S(2)}) %collective-permute-start.10) | collective-permute-done | bytes 663584 | tf_op jit(solution)/shard_map/ppermute | solution.py:39
  217.5 2.0 finish.5
  219.5 1.2 collective-permute-done.21
  220.7 3.0 %collective-permute-start.22 = (f32[16,128]{1,0:T(8,128)S(1)}, f32[16,128]{1,0:T(8,128)S(1)}, u32[]{:S(2)}, u32[]{:S(2)}) collective-permute-start(f32[16,128]{1,0:T(8,128)S(1)} %add.146), channel_id=1, source_target_pairs={{0,1},{1,0},{2,3},{3,2},{4,5},{5,4},{6,7},{7,6},{8,9},{9,8},{10,11... | collective-permute-start | bytes 24584 | tf_op jit(solution)/shard_map/ppermute | solution.py:302
  223.7 2.1 collective-permute-done.22
  225.8 1.5 collective-permute-start.23
  227.3 2.1 collective-permute-done.23
  229.5 1.9 collective-permute-start.24
  231.4 1.7 collective-permute-done.24
  233.5 3.3 %collective-permute-done.25 = f32[16,128]{1,0:T(8,128)S(1)} collective-permute-done((f32[16,128]{1,0:T(8,128)S(1)}, f32[16,128]{1,0:T(8,128)S(1)}, u32[]{:S(2)}, u32[]{:S(2)}) %collective-permute-start.25) | collective-permute-done | bytes 8224 | tf_op jit(solution)/shard_map/ppermute | solution.py:302
  236.8 3.9 %collective-permute-start.26 = (f32[16,128]{1,0:T(8,128)S(1)}, f32[16,128]{1,0:T(8,128)S(1)}, u32[]{:S(2)}, u32[]{:S(2)}) collective-permute-start(f32[16,128]{1,0:T(8,128)S(1)} %add.150), channel_id=1, source_target_pairs={{0,8},{2,10},{4,12},{6,14},{8,0},{10,2},{12,4},{14,6},{1,9},{3,11}... | collective-permute-start | bytes 24584 | tf_op jit(solution)/shard_map/ppermute | solution.py:302
  240.7 1.6 collective-permute-done.26
  242.3 2.1 collective-permute-start.27
  244.4 3.1 %collective-permute-done.27 = f32[16,128]{1,0:T(8,128)S(1)} collective-permute-done((f32[16,128]{1,0:T(8,128)S(1)}, f32[16,128]{1,0:T(8,128)S(1)}, u32[]{:S(2)}, u32[]{:S(2)}) %collective-permute-start.27) | collective-permute-done | bytes 8224 | tf_op jit(solution)/shard_map/ppermute | solution.py:302
  (64 shorter events, 8.0 us)
Async XLA Ops:
  5.9 65.4 %collective-permute-start.1 = (f32[4,160,512]{2,1,0:T(8,128)S(1)}, f32[4,160,512]{2,1,0:T(8,128)S(1)}, u32[]{:S(2)}, u32[]{:S(2)}) collective-permute-start(f32[4,160,512]{2,1,0:T(8,128)S(1)} %pick_rows.4), channel_id=1, source_target_pairs={{0,64},{16,80},{32,96},{48,112},{64,0},{80,16},{96,32},{112,48},{1... | collective-permute-start | bytes 3932168 | tf_op jit(solution)/shard_map/ppermute | solution.py:39
  14.5 84.7 %collective-permute-start.11 = (f32[4,160,512]{2,1,0:T(8,128)}, f32[4,160,512]{2,1,0:T(8,128)}, u32[]{:S(2)}, u32[]{:S(2)}) collective-permute-start(f32[4,160,512]{2,1,0:T(8,128)} %pick_rows.5), channel_id=1, source_target_pairs={{0,64},{16,80},{32,96},{48,112},{64,0},{80,16},{96,32},{112,48},{1... | collective-permute-start | bytes 3932168 | tf_op jit(solution)/shard_map/ppermute | solution.py:39
  58.7 12.5 %copy-start.8 = (s32[12]{0:T(128)S(1)}, s32[12]{0:T(128)}, u32[]{:S(2)}) copy-start(s32[12]{0:T(128)} %wave_ref.11) | copy-start | bytes 148
  69.4 1.9 copy-start
  90.2 3.5 %collective-permute-start.2 = (f32[648,256]{1,0:T(8,128)S(1)}, f32[648,256]{1,0:T(8,128)S(1)}, u32[]{:S(2)}, u32[]{:S(2)}) collective-permute-start(f32[648,256]{1,0:T(8,128)S(1)} %get-tuple-element.37), channel_id=1, source_target_pairs={{0,16},{16,0},{32,48},{48,32},{64,80},{80,64},{96,112},{112,96},{1... | collective-permute-start | bytes 1990664 | tf_op jit(solution)/shard_map/ppermute | solution.py:39
  90.2 33.3 %collective-permute-start = (f32[4,160,512]{2,1,0:T(8,128)}, f32[4,160,512]{2,1,0:T(8,128)S(1)}, u32[]{:S(2)}, u32[]{:S(2)}) collective-permute-start(f32[4,160,512]{2,1,0:T(8,128)} %pick_rows.6), channel_id=1, source_target_pairs={{0,64},{16,80},{32,96},{48,112},{64,0},{80,16},{96,32},{112,48},{1... | collective-permute-start | bytes 3932168 | tf_op jit(solution)/shard_map/ppermute | solution.py:39
  93.5 63.5 %collective-permute-start.18 = (f32[1944,256]{1,0:T(8,128)}, f32[1944,256]{1,0:T(8,128)S(1)}, u32[]{:S(2)}, u32[]{:S(2)}) collective-permute-start(f32[1944,256]{1,0:T(8,128)} %get-tuple-element.49), channel_id=1, source_target_pairs={{0,16},{16,0},{32,48},{48,32},{64,80},{80,64},{96,112},{112,96},{1... | collective-permute-start | bytes 5971976 | tf_op jit(solution)/shard_map/ppermute | solution.py:39
  94.8 35.8 %collective-permute-start.3 = (f32[328,256]{1,0:T(8,128)S(1)}, f32[328,256]{1,0:T(8,128)S(1)}, u32[]{:S(2)}, u32[]{:S(2)}) collective-permute-start(f32[328,256]{1,0:T(8,128)S(1)} %slice_add_fusion.8), channel_id=1, source_target_pairs={{0,32},{16,48},{32,64},{48,80},{64,96},{80,112},{96,0},{112,16},{1... | collective-permute-start | bytes 1007624 | tf_op jit(solution)/shard_map/ppermute | solution.py:39
  96.6 34.1 %collective-permute-start.4 = (f32[320,256]{1,0:T(8,128)S(1)}, f32[320,256]{1,0:T(8,128)S(1)}, u32[]{:S(2)}, u32[]{:S(2)}) collective-permute-start(f32[320,256]{1,0:T(8,128)S(1)} %slice_add_fusion.11), channel_id=1, source_target_pairs={{0,96},{16,112},{32,0},{48,16},{64,32},{80,48},{96,64},{112,80},{1... | collective-permute-start | bytes 983048 | tf_op jit(solution)/shard_map/ppermute | solution.py:39
  117.9 49.8 %collective-permute-start.12 = (f32[1944,256]{1,0:T(8,128)}, f32[1944,256]{1,0:T(8,128)S(1)}, u32[]{:S(2)}, u32[]{:S(2)}) collective-permute-start(f32[1944,256]{1,0:T(8,128)} %get-tuple-element.45), channel_id=1, source_target_pairs={{0,16},{16,0},{32,48},{48,32},{64,80},{80,64},{96,112},{112,96},{1... | collective-permute-start | bytes 5971976 | tf_op jit(solution)/shard_map/ppermute | solution.py:39
  123.6 26.7 %copy-start.2 = (f32[2592,256]{1,0:T(8,128)S(1)}, f32[2592,256]{1,0:T(8,128)}, u32[]{:S(2)}) copy-start(f32[2592,256]{1,0:T(8,128)} %get-tuple-element.44.mine_ref) | copy-start | bytes 7962628
  123.6 26.7 %collective-permute-start.13 = (f32[648,256]{1,0:T(8,128)S(1)}, f32[648,256]{1,0:T(8,128)S(1)}, u32[]{:S(2)}, u32[]{:S(2)}) collective-permute-start(f32[648,256]{1,0:T(8,128)S(1)} %get-tuple-element.46), channel_id=1, source_target_pairs={{0,16},{16,0},{32,48},{48,32},{64,80},{80,64},{96,112},{112,96},{1... | collective-permute-start | bytes 1990664 | tf_op jit(solution)/shard_map/ppermute | solution.py:39
  130.6 19.0 %copy-start.9 = (f32[320,256]{1,0:T(8,128)}, f32[320,256]{1,0:T(8,128)S(1)}, u32[]{:S(2)}) copy-start(f32[320,256]{1,0:T(8,128)S(1)} %collective-permute-done.4) | copy-start | bytes 983044
  149.6 9.0 %copy-start.1 = (f32[2592,256]{1,0:T(8,128)S(1)}, f32[2592,256]{1,0:T(8,128)}, u32[]{:S(2)}) copy-start(f32[2592,256]{1,0:T(8,128)} %get-tuple-element.36.mine_ref) | copy-start | bytes 7962628
  149.6 9.0 %copy-start.10 = (f32[320,256]{1,0:T(8,128)S(1)}, f32[320,256]{1,0:T(8,128)}, u32[]{:S(2)}) copy-start(f32[320,256]{1,0:T(8,128)} %copy-done.9) | copy-start | bytes 983044
  149.6 30.5 %collective-permute-start.5 = (f32[1944,256]{1,0:T(8,128)}, f32[1944,256]{1,0:T(8,128)S(1)}, u32[]{:S(2)}, u32[]{:S(2)}) collective-permute-start(f32[1944,256]{1,0:T(8,128)} %get-tuple-element.40), channel_id=1, source_target_pairs={{0,16},{16,0},{32,48},{48,32},{64,80},{80,64},{96,112},{112,96},{1... | collective-permute-start | bytes 5971976 | tf_op jit(solution)/shard_map/ppermute | solution.py:39
  149.7 4.6 %collective-permute-start.6 = (f32[648,256]{1,0:T(8,128)S(1)}, f32[648,256]{1,0:T(8,128)S(1)}, u32[]{:S(2)}, u32[]{:S(2)}) collective-permute-start(f32[648,256]{1,0:T(8,128)S(1)} %get-tuple-element.41), channel_id=1, source_target_pairs={{0,16},{16,0},{32,48},{48,32},{64,80},{80,64},{96,112},{112,96},{1... | collective-permute-start | bytes 1990664 | tf_op jit(solution)/shard_map/ppermute | solution.py:39
  150.3 10.0 %collective-permute-start.15 = (f32[320,256]{1,0:T(8,128)S(1)}, f32[320,256]{1,0:T(8,128)S(1)}, u32[]{:S(2)}, u32[]{:S(2)}) collective-permute-start(f32[320,256]{1,0:T(8,128)S(1)} %slice_add_fusion.9), channel_id=1, source_target_pairs={{0,96},{16,112},{32,0},{48,16},{64,32},{80,48},{96,64},{112,80},{1... | collective-permute-start | bytes 983048 | tf_op jit(solution)/shard_map/ppermute | solution.py:39
  154.3 11.9 %collective-permute-start.14 = (f32[328,256]{1,0:T(8,128)S(1)}, f32[328,256]{1,0:T(8,128)S(1)}, u32[]{:S(2)}, u32[]{:S(2)}) collective-permute-start(f32[328,256]{1,0:T(8,128)S(1)} %slice_add_fusion.6), channel_id=1, source_target_pairs={{0,32},{16,48},{32,64},{48,80},{64,96},{80,112},{96,0},{112,16},{1... | collective-permute-start | bytes 1007624 | tf_op jit(solution)/shard_map/ppermute | solution.py:39
  155.9 5.7 %copy-start.3 = (f32[2592,256]{1,0:T(8,128)S(1)}, f32[2592,256]{1,0:T(8,128)}, u32[]{:S(2)}) copy-start(f32[2592,256]{1,0:T(8,128)} %get-tuple-element.39.mine_ref) | copy-start | bytes 7962628
  157.1 20.2 %collective-permute-start.7 = (f32[328,256]{1,0:T(8,128)S(1)}, f32[328,256]{1,0:T(8,128)S(1)}, u32[]{:S(2)}, u32[]{:S(2)}) collective-permute-start(f32[328,256]{1,0:T(8,128)S(1)} %slice_add_fusion.7), channel_id=1, source_target_pairs={{0,32},{16,48},{32,64},{48,80},{64,96},{80,112},{96,0},{112,16},{1... | collective-permute-start | bytes 1007624 | tf_op jit(solution)/shard_map/ppermute | solution.py:39
  160.2 27.4 %collective-permute-start.19 = (f32[648,256]{1,0:T(8,128)S(1)}, f32[648,256]{1,0:T(8,128)S(1)}, u32[]{:S(2)}, u32[]{:S(2)}) collective-permute-start(f32[648,256]{1,0:T(8,128)S(1)} %get-tuple-element.59), channel_id=1, source_target_pairs={{0,32},{16,48},{32,64},{48,80},{64,96},{80,112},{96,0},{112,16},{1... | collective-permute-start | bytes 1990664 | tf_op jit(solution)/shard_map/ppermute | solution.py:39
  166.2 10.6 %collective-permute-start.8 = (f32[320,256]{1,0:T(8,128)S(1)}, f32[320,256]{1,0:T(8,128)S(1)}, u32[]{:S(2)}, u32[]{:S(2)}) collective-permute-start(f32[320,256]{1,0:T(8,128)S(1)} %slice_add_fusion.10), channel_id=1, source_target_pairs={{0,96},{16,112},{32,0},{48,16},{64,32},{80,48},{96,64},{112,80},{1... | collective-permute-start | bytes 983048 | tf_op jit(solution)/shard_map/ppermute | solution.py:39
  167.7 13.9 %copy-start.4 = (f32[1944,256]{1,0:T(8,128)}, f32[1944,256]{1,0:T(8,128)S(1)}, u32[]{:S(2)}) copy-start(f32[1944,256]{1,0:T(8,128)S(1)} %collective-permute-done.12.cross_ref) | copy-start | bytes 5971972
  167.7 23.4 %collective-permute-start.20 = (f32[648,256]{1,0:T(8,128)S(1)}, f32[648,256]{1,0:T(8,128)S(1)}, u32[]{:S(2)}, u32[]{:S(2)}) collective-permute-start(f32[648,256]{1,0:T(8,128)S(1)} %get-tuple-element.58), channel_id=1, source_target_pairs={{0,96},{16,112},{32,0},{48,16},{64,32},{80,48},{96,64},{112,80},{1... | collective-permute-start | bytes 1990664 | tf_op jit(solution)/shard_map/ppermute | solution.py:39
  176.9 25.0 %collective-permute-start.16 = (f32[648,256]{1,0:T(8,128)}, f32[648,256]{1,0:T(8,128)S(1)}, u32[]{:S(2)}, u32[]{:S(2)}) collective-permute-start(f32[648,256]{1,0:T(8,128)} %get-tuple-element.61), channel_id=1, source_target_pairs={{0,32},{16,48},{32,64},{48,80},{64,96},{80,112},{96,0},{112,16},{1... | collective-permute-start | bytes 1990664 | tf_op jit(solution)/shard_map/ppermute | solution.py:39
  177.2 28.2 %collective-permute-start.17 = (f32[648,256]{1,0:T(8,128)}, f32[648,256]{1,0:T(8,128)}, u32[]{:S(2)}, u32[]{:S(2)}) collective-permute-start(f32[648,256]{1,0:T(8,128)} %get-tuple-element.60), channel_id=1, source_target_pairs={{0,96},{16,112},{32,0},{48,16},{64,32},{80,48},{96,64},{112,80},{1... | collective-permute-start | bytes 1990664 | tf_op jit(solution)/shard_map/ppermute | solution.py:39
  180.1 7.5 %copy-start.6 = (f32[1944,256]{1,0:T(8,128)}, f32[1944,256]{1,0:T(8,128)S(1)}, u32[]{:S(2)}) copy-start(f32[1944,256]{1,0:T(8,128)S(1)} %collective-permute-done.5.cross_ref) | copy-start | bytes 5971972
  181.6 35.9 %collective-permute-start.10 = (f32[648,256]{1,0:T(8,128)}, f32[648,256]{1,0:T(8,128)S(1)}, u32[]{:S(2)}, u32[]{:S(2)}) collective-permute-start(f32[648,256]{1,0:T(8,128)} %get-tuple-element.62), channel_id=1, source_target_pairs={{0,96},{16,112},{32,0},{48,16},{64,32},{80,48},{96,64},{112,80},{1... | collective-permute-start | bytes 1990664 | tf_op jit(solution)/shard_map/ppermute | solution.py:39
  187.6 17.8 %copy-start.5 = (f32[1944,256]{1,0:T(8,128)S(1)}, f32[1944,256]{1,0:T(8,128)}, u32[]{:S(2)}) copy-start(f32[1944,256]{1,0:T(8,128)} %copy-done.4) | copy-start | bytes 5971972
  187.6 29.9 %collective-permute-start.9 = (f32[648,256]{1,0:T(8,128)}, f32[648,256]{1,0:T(8,128)S(1)}, u32[]{:S(2)}, u32[]{:S(2)}) collective-permute-start(f32[648,256]{1,0:T(8,128)} %get-tuple-element.63), channel_id=1, source_target_pairs={{0,32},{16,48},{32,64},{48,80},{64,96},{80,112},{96,0},{112,16},{1... | collective-permute-start | bytes 1990664 | tf_op jit(solution)/shard_map/ppermute | solution.py:39
  205.4 12.1 %copy-start.7 = (f32[1944,256]{1,0:T(8,128)S(1)}, f32[1944,256]{1,0:T(8,128)}, u32[]{:S(2)}) copy-start(f32[1944,256]{1,0:T(8,128)} %copy-done.6) | copy-start | bytes 5971972
  219.5 1.2 collective-permute-start.21
  220.7 5.2 %collective-permute-start.22 = (f32[16,128]{1,0:T(8,128)S(1)}, f32[16,128]{1,0:T(8,128)S(1)}, u32[]{:S(2)}, u32[]{:S(2)}) collective-permute-start(f32[16,128]{1,0:T(8,128)S(1)} %add.146), channel_id=1, source_target_pairs={{0,1},{1,0},{2,3},{3,2},{4,5},{5,4},{6,7},{7,6},{8,9},{9,8},{10,11... | collective-permute-start | bytes 24584 | tf_op jit(solution)/shard_map/ppermute | solution.py:302
  225.8 3.7 %collective-permute-start.23 = (f32[16,128]{1,0:T(8,128)S(1)}, f32[16,128]{1,0:T(8,128)S(1)}, u32[]{:S(2)}, u32[]{:S(2)}) collective-permute-start(f32[16,128]{1,0:T(8,128)S(1)} %add.147), channel_id=1, source_target_pairs={{0,2},{2,0},{4,6},{6,4},{8,10},{10,8},{12,14},{14,12},{1,3},{3,1},... | collective-permute-start | bytes 24584 | tf_op jit(solution)/shard_map/ppermute | solution.py:302
  229.5 3.7 %collective-permute-start.24 = (f32[16,128]{1,0:T(8,128)S(1)}, f32[16,128]{1,0:T(8,128)S(1)}, u32[]{:S(2)}, u32[]{:S(2)}) collective-permute-start(f32[16,128]{1,0:T(8,128)S(1)} %add.148), channel_id=1, source_target_pairs={{0,4},{2,6},{4,0},{6,2},{8,12},{10,14},{12,8},{14,10},{1,5},{3,7},... | collective-permute-start | bytes 24584 | tf_op jit(solution)/shard_map/ppermute | solution.py:302
  233.1 3.7 %collective-permute-start.25 = (f32[16,128]{1,0:T(8,128)S(1)}, f32[16,128]{1,0:T(8,128)S(1)}, u32[]{:S(2)}, u32[]{:S(2)}) collective-permute-start(f32[16,128]{1,0:T(8,128)S(1)} %add.149), channel_id=1, source_target_pairs={{0,32},{16,48},{32,0},{48,16},{64,96},{80,112},{96,64},{112,80},{1... | collective-permute-start | bytes 24584 | tf_op jit(solution)/shard_map/ppermute | solution.py:302
  236.8 5.5 %collective-permute-start.26 = (f32[16,128]{1,0:T(8,128)S(1)}, f32[16,128]{1,0:T(8,128)S(1)}, u32[]{:S(2)}, u32[]{:S(2)}) collective-permute-start(f32[16,128]{1,0:T(8,128)S(1)} %add.150), channel_id=1, source_target_pairs={{0,8},{2,10},{4,12},{6,14},{8,0},{10,2},{12,4},{14,6},{1,9},{3,11}... | collective-permute-start | bytes 24584 | tf_op jit(solution)/shard_map/ppermute | solution.py:302
  242.3 5.2 %collective-permute-start.27 = (f32[16,128]{1,0:T(8,128)S(1)}, f32[16,128]{1,0:T(8,128)S(1)}, u32[]{:S(2)}, u32[]{:S(2)}) collective-permute-start(f32[16,128]{1,0:T(8,128)S(1)} %add.151), channel_id=1, source_target_pairs={{0,64},{16,80},{32,96},{48,112},{64,0},{80,16},{96,32},{112,48},{1... | collective-permute-start | bytes 24584 | tf_op jit(solution)/shard_map/ppermute | solution.py:302

commit v3 on v2

v3 whole, which is shorter than its diff:
```python
import functools

import jax
import jax.numpy as jnp
from jax import lax
from jax.experimental import pallas as pl
from jax.experimental.pallas import tpu as pltpu
from jax.sharding import PartitionSpec as P

NDEG = 1280
MESSAGES = (2, 4, 6)
RUNS = ((0, 1), (2,))
F32 = jnp.float32
BF16 = jnp.bfloat16
VMEM_LIMIT = 48 * 1024 * 1024


def behind(x, after):
    return lax.optimization_barrier((x, after))[0]


def split_two(x):
    high = x.astype(BF16)
    low = (x - high.astype(F32)).astype(BF16)
    return high, low


def dot_nt(a, b):
    return lax.dot_general(a, b, (((1,), (1,)), ((), ())), preferred_element_type=F32)


def dot_nn(a, b):
    return jnp.dot(a, b, preferred_element_type=F32)


def send_along(x, up, cross):
    size = lax.axis_size("band")
    chips = size // 2
    pairs = [(i, ((i // 2 + up) % chips) * 2 + ((i % 2) ^ cross)) for i in range(size)]
    return lax.ppermute(x, "band", pairs)


def pick_kernel(index_ref, field_ref, send_ref, keep_ref, main_ref, tail_ref):
    count, main = main_ref.shape
    half = count // 2
    rows = field_ref.shape[2]

    @pl.when(pl.program_id(0) == 0)
    def _():
        lanes = lax.broadcasted_iota(jnp.int32, (count, rows), 1)
        chosen = jnp.where(index_ref[...] == lanes, 1.0, 0.0)
        main_ref[...] = chosen[:, :main].astype(BF16)
        tail_ref[...] = jnp.concatenate([chosen[:, main:], chosen[:, main:]], 1).astype(BF16)

    high, low = split_two(field_ref[0])
    tail = jnp.concatenate([high[:, main:], low[:, main:]], 1)
    picked = dot_nt(main_ref[...], high[:, :main]) + dot_nt(main_ref[...], low[:, :main]) + dot_nt(tail_ref[...], tail)
    send_ref[0] = picked[:half]
    keep_ref[0] = picked[half:]


def pick_rows(index, field, first, each):
    pairs, width, rows = field.shape
    count = index.shape[0]
    half = count // 2
    main = 256
    shape = jax.ShapeDtypeStruct((each, half, width), F32)
    out = pl.BlockSpec((1, half, width), lambda step: (step, 0, 0))
    return pl.pallas_call(
        pick_kernel,
        grid=(each,),
        in_specs=[
            pl.BlockSpec((count, 1), lambda step: (0, 0)),
            pl.BlockSpec((1, width, rows), lambda step: (first + step, 0, 0)),
        ],
        out_specs=[out, out],
        out_shape=[shape, shape],
        scratch_shapes=[pltpu.VMEM((count, main), BF16), pltpu.VMEM((count, 2 * (rows - main)), BF16)],
        compiler_params=pltpu.CompilerParams(vmem_limit_bytes=VMEM_LIMIT),
        cost_estimate=pl.CostEstimate(flops=10**12, bytes_accessed=10**10, transcendentals=0),
        name="pick_rows",
    )(index, field)


def layout_kernel(*refs, share):
    out_ref = refs[-1]
    lanes = main = 128
    half = refs[0].shape[1]
    rest = main - 3 * (half - main)
    for parity in range(2):
        for tile, ref in enumerate(refs[:-1]):
            high, low = split_two(ref.reshape(1, 2 * half, lanes)[0, pl.ds(parity, half, stride=2), :])
            blocks = (
                high[:main],
                low[:main],
                jnp.concatenate([high[main:], high[main:], low[main:], jnp.zeros((rest, lanes), BF16)], 0),
            )
            for i, block in enumerate(blocks):
                turned = block.T
                for s in range(out_ref.shape[2]):
                    first = max(s * share, tile * lanes)
                    last = min((s + 1) * share, (tile + 1) * lanes)
                    if first < last:
                        out_ref[0, parity, s, first - s * share : last - s * share, main * i : main * (i + 1)] = turned[
                            first - tile * lanes : last - tile * lanes
                        ]


def lay_out(table, share, padded):
    pairs, half, _, slots = table.shape
    shares = slots // share
    tiles = (slots + 127) // 128

    def block(tile):
        return pl.BlockSpec((1, half, 2, 128), lambda step: (step, 0, 0, tile))

    return pl.pallas_call(
        functools.partial(layout_kernel, share=share),
        grid=(pairs,),
        in_specs=[block(tile) for tile in range(tiles)],
        out_specs=pl.BlockSpec((1, 2, shares, padded, 384), lambda step: (step, 0, 0, 0, 0)),
        out_shape=jax.ShapeDtypeStruct((pairs, 2, shares, padded, 384), BF16),
        compiler_params=pltpu.CompilerParams(vmem_limit_bytes=VMEM_LIMIT),
        cost_estimate=pl.CostEstimate(flops=10**12, bytes_accessed=10**10, transcendentals=0),
        name="lay_out",
    )(*[table] * tiles)


def project_kernel(
    place_ref, wave_ref, *refs, share, first, ways, starts
):
    count = len(starts)
    keep_refs, recv_refs = refs[:count], refs[count : 2 * count]
    table_ref, mine_ref, *cross_refs, field_ref, result_ref = refs[2 * count :]
    step = pl.program_id(0)
    core = place_ref[0]
    chip = place_ref[1]
    chips = place_ref[2]
    first_m = wave_ref[first + step]
    half = keep_refs[0].shape[1]
    width = keep_refs[0].shape[2] // 2
    main = 128
    tail = half - main
    shares, padded = table_ref.shape[2:4]
    middle = shares // 2
    side = jnp.where(chip < chips // 2, 1.0, -1.0)
    for parity in range(2):
        keep, recv = keep_refs[0][0], recv_refs[0][0]
        for start, keep_ref, recv_ref in zip(starts[1:], keep_refs[1:], recv_refs[1:]):
            keep = jnp.where(step >= start, keep_ref[0], keep)
            recv = jnp.where(step >= start, recv_ref[0], recv)
        folded = side * (keep - recv) if parity else keep + recv
        high, low = split_two(folded)
        for member in range(2):
            part = slice(member * width, (member + 1) * width)
            field_ref[member, :main] = high[:main, part]
            field_ref[member, main : 2 * main] = low[:main, part]
            field_ref[member, 2 * main : 3 * main] = high[:main, part]
            for k, value in enumerate((high, low, high)):
                at = 3 * main + k * tail
                field_ref[member, at : at + tail] = value[main:, part]
            field_ref[member, 3 * main + 3 * tail :] = jnp.zeros((main - 3 * tail, width), BF16)
        count = (NDEG - first_m - parity + 1) // 2

        def product(member, begin, end):
            table = table_ref[0, parity, begin:end].reshape((end - begin) * padded, table_ref.shape[4])
            table = jnp.concatenate([table[:, :main], table], 1)
            result = dot_nn(table, field_ref[member])
            result_ref[member, begin:end] = result.reshape(end - begin, padded, width)

        product(0, 0, middle)
        product(1, middle, shares)
        pl.when(count > middle * share)(lambda: product(0, middle, shares))
        pl.when(count < middle * share)(lambda: product(1, middle - 1, middle))

        def store(which, rows, way):
            value = result_ref[0, which]
            if which >= middle - 1:
                slot = which * share + lax.broadcasted_iota(jnp.int32, (padded, width), 0)
                valid = parity + 2 * (slot - count) <= first_m
                value = jnp.where(slot < count, value, jnp.where(valid, result_ref[1, which], 0.0))
            value = value[:share]
            ahead = lax.rem(which // 2 + chips - chip, chips)
            back = chips // 2 + way
            toward = (1 + way) // 2
            spot = jnp.where(ahead == 0, 3, jnp.where(ahead == chips // 2, toward, jnp.where(ahead == back, 2, 1 - toward)))
            mine = core == which % 2

            @pl.when(mine)
            def _():
                mine_ref[spot, rows, :] = value

            base = 0
            for cross_ref in cross_refs:
                size = cross_ref.shape[0]

                @pl.when(jnp.logical_not(mine) & (spot >= base) & (spot < base + size))
                def _():
                    cross_ref[jnp.clip(spot - base, 0, size - 1), rows, :] = value

                base += size

        for pair, (way, at) in enumerate(ways):

            @pl.when(step == pair)
            def _():
                for which in range(shares):
                    begin = at + parity * share
                    store(which, slice(begin, begin + share), way)


def project(place, wave, keeps, recvs, table, share, first, ways, rows, messages):
    half, width = recvs[0].shape[1:]
    shares, padded, depth = table.shape[2:]
    sizes_in = [recv.shape[0] for recv in recvs]
    starts = [sum(sizes_in[:i]) for i in range(len(recvs))]

    def field(start, size):
        return pl.BlockSpec((1, half, width), lambda step, *_: (jnp.clip(step - start, 0, size - 1), 0, 0))

    fields = [field(start, size) for start, size in zip(starts, sizes_in)]
    sizes = [(count, rows, width // 2) for count in (shares // 2, *messages)]
    return pl.pallas_call(
        functools.partial(project_kernel, share=share, first=first, ways=ways, starts=starts),
        grid_spec=pltpu.PrefetchScalarGridSpec(
            num_scalar_prefetch=2,
            grid=(len(ways),),
            in_specs=[
                *fields,
                *fields,
                pl.BlockSpec((1,) + table.shape[1:], lambda step, *_: (first + step, 0, 0, 0, 0)),
            ],
            out_specs=[pl.BlockSpec(size, lambda step, *_: (0, 0, 0)) for size in sizes],
            scratch_shapes=[
                pltpu.VMEM((2, 512, width // 2), BF16),
                pltpu.VMEM((2, shares, padded, width // 2), F32),
            ],
        ),
        out_shape=[jax.ShapeDtypeStruct(size, F32) for size in sizes],
        compiler_params=pltpu.CompilerParams(vmem_limit_bytes=VMEM_LIMIT),
        cost_estimate=pl.CostEstimate(flops=10**12, bytes_accessed=10**10, transcendentals=0),
        name="project",
    )(place, wave, *keeps, *recvs, table)


def finish_kernel(place_ref, wave_ref, mine_ref, cross_ref, far_up_ref, far_down_ref, near_up_ref, near_down_ref, *refs, share, first, ways
):
    out_ref, energy_ref = refs[-2:]
    low = far_up_ref.shape[0]
    each = out_ref.shape[0]
    core = place_ref[0]
    start = (2 * place_ref[1] + core) * share
    lanes = 128
    terms = []
    spots = []
    for pair in range(each):
        first_m = wave_ref[first + pair]
        for parity in range(2):
            at = ways[pair][1] + parity * share
            rows = slice(at, at + share)
            if at < low:
                arrived = far_up_ref[rows, :] + near_down_ref[rows, :]
            else:
                arrived = far_down_ref[at - low : at - low + share, :] + near_up_ref[rows, :]
            value = ((mine_ref[0, rows, :] + cross_ref[0, rows, :]) + arrived).T
            out_ref[pair, parity] = value.reshape(out_ref.shape[2:])
            squares = jnp.sum(value * value, axis=0, keepdims=True)
            squares = jnp.concatenate([squares, jnp.zeros((1, lanes - share), F32)], 1)
            column = lax.broadcasted_iota(jnp.int32, (1, lanes), 1)
            slot = start + column
            count = (NDEG - first_m - parity + 1) // 2
            leading = slot < count
            second_m = NDEG - 1 - first_m
            degree = jnp.where(leading, first_m + parity + 2 * slot, second_m + parity + 2 * (slot - count))
            owner_m = jnp.where(leading, first_m, second_m)
            usable = (column < share) & (degree >= 1) & (degree <= NDEG - 1)
            safe = jnp.maximum(degree, 1).astype(F32)
            factor = jnp.where(owner_m == 0, 1.0, 2.0)
            terms.append(jnp.where(usable, factor * squares / (4.0 * safe * (safe + 1.0)), 0.0))
            spots.append(jnp.where(usable, degree - 1, 0))
    term = jnp.concatenate(terms, 1)
    spot = jnp.concatenate(spots, 1)
    size = term.shape[1]
    band = lax.broadcasted_iota(jnp.int32, (16, size), 0)
    left = jnp.where(spot // lanes == band, term, 0.0)
    line = lax.broadcasted_iota(jnp.int32, (lanes, size), 0)
    right = jnp.where(spot % lanes == line, 1.0, 0.0).astype(BF16)
    first = left.astype(BF16)
    rest = left - first.astype(F32)
    second = rest.astype(BF16)
    third = (rest - second.astype(F32)).astype(BF16)
    energy_ref[...] = dot_nt(first, right) + dot_nt(second, right) + dot_nt(third, right)


def finish(place, wave, mine, cross, far, near, held, shape, share, first, ways):
    each = len(ways)
    _, rows, width = mine.shape
    messages = far + near
    operands = [mine, cross] + messages
    in_specs = [
        pl.BlockSpec((1, rows, width), lambda step, *_: (3, 0, 0)),
        pl.BlockSpec((1, rows, width), lambda step, *_: (cross.shape[0] - 1, 0, 0)),
    ] + [pl.BlockSpec(message.shape, lambda step, *_: (0, 0)) for message in messages]
    aliases = {}
    if held is not None:
        operands.append(held)
        in_specs.append(pl.BlockSpec(memory_space=pl.ANY))
        aliases = {1 + len(operands): 0}
    return pl.pallas_call(
        functools.partial(finish_kernel, share=share, first=first, ways=ways),
        grid_spec=pltpu.PrefetchScalarGridSpec(
            num_scalar_prefetch=2,
            grid=(1,),
            in_specs=in_specs,
            out_specs=[
                pl.BlockSpec((each,) + shape[1:], lambda step, *_: (first // each, 0, 0, 0, 0)),
                pl.BlockSpec((16, 128), lambda step, *_: (0, 0)),
            ],
        ),
        out_shape=[jax.ShapeDtypeStruct(shape, F32), jax.ShapeDtypeStruct((16, 128), F32)],
        input_output_aliases=aliases,
        compiler_params=pltpu.CompilerParams(vmem_limit_bytes=VMEM_LIMIT),
        cost_estimate=pl.CostEstimate(flops=10**12, bytes_accessed=10**10, transcendentals=0),
        name="finish",
    )(place, wave, *operands)


def all_sum(x):
    for axis, bit in (("band", 1), ("lev", 1), ("wave", 1), ("wave", 2), ("band", 2), ("wave", 4), ("band", 4)):
        size = lax.axis_size(axis)
        x = x + lax.ppermute(x, axis, [(i, i ^ bit) for i in range(size)])
    return x


def shards(fourier, legendre, pair_m, mirror):
    bands = lax.axis_size("band")
    chips = bands // 2
    rows, pairs, members, comps, levs = fourier.shape
    half_rows = rows // 2
    slots = legendre.shape[3]
    share = slots // bands
    padded = (share + 15) // 16 * 16
    position = lax.axis_index("band")
    chip, core = position // 2, position % 2
    place = jnp.stack([core, chip, jnp.int32(chips)]).astype(jnp.int32)

    north_base = position % chips * rows
    south_base = north_base + chips * rows
    partner = lax.dynamic_slice(mirror, (north_base,), (rows,)) - south_base
    plain = (jnp.arange(rows, dtype=jnp.int32) + half_rows) % rows
    index = jnp.where(position < chips, plain, partner).reshape(rows, 1)
    field = jnp.transpose(fourier, (1, 2, 3, 4, 0)).reshape(pairs, members * comps * levs, rows)

    kept, received = [], []
    for i, each in enumerate(MESSAGES):
        message, keep = pick_rows(index, field, sum(MESSAGES[:i]), each)
        kept.append(keep)
        received.append(send_along(message, chips // 2, 0))
        index, legendre, message = lax.optimization_barrier((index, legendre, message))

    table = lay_out(legendre, share, padded)

    ways, lengths, firsts = [], [], []
    for run in RUNS:
        each = sum(MESSAGES[i] for i in run)
        ups = (each + len(ways)) // 2
        low = (2 * ups * share + 7) // 8 * 8
        high = (2 * (each - ups) * share + 7) // 8 * 8
        firsts.append(sum(MESSAGES[: run[0]]))
        ways.append([(-1, 2 * i * share) if i < ups else (1, low + 2 * (i - ups) * share) for i in range(each)])
        lengths.append((low, high))
    mine, cross, far, near = {}, {}, {}, {}

    def begin(run, messages, after):
        mine[run], *others = project(
            place, pair_m, [kept[i] for i in RUNS[run]], behind([received[i] for i in RUNS[run]], after), table, share,
            firsts[run], ways[run], sum(lengths[run]), messages,
        )
        cross[run] = [send_along(other, 0, 1) for other in others]

    def other_core(run, spot):
        for message in cross[run]:
            if spot < message.shape[0]:
                return message[spot]
            spot -= message.shape[0]

    def send_early(run, after):
        totals = [mine[run][spot] + other for spot, other in enumerate(behind([other_core(run, 0), other_core(run, 1)], after))]
        near[run] = [send_along(totals[0], 1, 0), send_along(totals[1], -1, 0)]
        return totals

    def send_late(run):
        low, _ = lengths[run]
        total, other = mine[run][2], other_core(run, 2)
        totals = [
            total[:low] + other[:low] + near[run][0][:low],
            total[low:] + other[low:] + near[run][1][low:],
        ]
        far[run] = [send_along(totals[0], 1, 0), send_along(totals[1], -1, 0)]
        return totals

    begin(0, (1, 1, 1, 1), ())
    begin(1, (1, 1, 2), [send_early(0, ()), cross[0][2:]])
    sent = send_late(0)
    send_early(1, sent)
    send_late(1)
    shape = (pairs, 2, comps, levs, share)
    held = None
    energies = []
    for run in range(len(RUNS)):
        held, energy = finish(
            place, pair_m, mine[run], cross[run][-1], far[run], near[run], held, shape, share, firsts[run], ways[run]
        )
        energies.append(energy)
    total = all_sum(functools.reduce(jnp.add, energies))
    return (held, jnp.log(total.reshape(-1)[: NDEG - 1]))


def solution(mesh):
    return jax.shard_map(
        shards,
        mesh=mesh,
        in_specs=(
            P("band", "wave", None, None, "lev"),
            P("wave", "band", None, None),
            P("wave"),
            P(),
        ),
        out_specs=(P("wave", None, None, "lev", "band"), P()),
        check_vma=False,
    )
```

time: 249 us -> 200 us (0.80)
  Pallas kernels: 128 us -> 72.4 us
  waiting for transfers between devices: 71 us -> 83.3 us
  starting transfers between devices: 38.5 us -> 30.3 us
    pallas_call x10 -> x7, Pallas kernels: 88.9 us -> 55.3 us  [the longest x2 32.9 us: project(): pl.pallas_call(functools.partial(project_kernel, share=share, first=first...]
    pallas_call x1, Pallas kernels: 38.8 us -> 17.1 us  [lay_out(): pl.pallas_call(functools.partial(layout_kernel, share=share), grid=(pairs...]
    ppermute x21 -> x18, waiting for transfers between devices: 55.8 us -> 65.7 us  [send_along(): return lax.ppermute(x, 'band', pairs)]
    ppermute x21 -> x18, starting transfers between devices: 25.7 us -> 19.9 us  [send_along(): return lax.ppermute(x, 'band', pairs)]
    add x9 -> x4, other arithmetic: 6.51 us -> 6.55 us  [the longest x2 3.29 us: send_early(): mine[run][spot] + other]
  transfers between devices with their start and end apart: 28 -> 25, of which waited for: 18 -> 18; matrix products, arithmetic and copies ran while one was open for 3% -> 4% of each run, Pallas kernels for 49% -> 33%
where the time goes in v3:
time: 200 us; the launch traced here: 199 us
  waiting for transfers between devices  83.3 us (42%)
  Pallas kernels  72.4 us (36%)
  starting transfers between devices  30.3 us (15%)
  other arithmetic  7.43 us (4%)
  local copies, waits for them, and re-layouts  5.12 us (3%)
    ppermute x18, waiting for transfers between devices, send_along(): return lax.ppermute(x, 'band', pairs)  65.7 us
    pallas_call x2, Pallas kernels, project(): pl.pallas_call(functools.partial(project_kernel, share=share, first=first...  32.9 us
    ppermute x18, starting transfers between devices, send_along(): return lax.ppermute(x, 'band', pairs)  19.9 us
    ppermute x7, waiting for transfers between devices, all_sum(): x = x + lax.ppermute(x, axis, [(i, i ^ bit) for i in range(size)])  17.6 us
    pallas_call x1, Pallas kernels, lay_out(): pl.pallas_call(functools.partial(layout_kernel, share=share), grid=(pairs...  17.1 us
    pallas_call x3, Pallas kernels, pick_rows(): pl.pallas_call(pick_kernel, grid=(each,), in_specs=[pl.BlockSpec((count,...  14.3 us
    ppermute x7, starting transfers between devices, all_sum(): x = x + lax.ppermute(x, axis, [(i, i ^ bit) for i in range(size)])  10.3 us
    pallas_call x2, Pallas kernels, finish(): pl.pallas_call(functools.partial(finish_kernel, share=share, first=first,...  8.11 us
  transfers between devices with their start and end apart: 25, of which 18 were waited for; matrix products, arithmetic and copies ran while one was open for 4% of the time, Pallas kernels for 33%

profile of v3, /device:TPU:0, one launch (start us, length us, event | category | flops | bytes accessed | tf_op | source)
XLA Modules:
  0.0 199.3 jit_solution(2962798708344378646)
XLA Ops:
  0.7 0.8 fusion.4
  1.6 2.9 %pick_rows.3 = (f32[2,160,512]{2,1,0:T(8,128)}, f32[2,160,512]{2,1,0:T(8,128)S(1)}) custom-call(s32[320,1]{1,0:T(8,128)S(1)} %copy.7.index_ref, f32[12,512,320]{2,1,0:T(8,128)} %bitcast.39), custom_call_target="tpu_custom_call" | custom-call | flops 999999995904 | bytes 10000000000 | tf_op jit(solution)/shard_map/pick_rows/pallas_call | solution.py:69
  4.5 3.3 %collective-permute-start.1 = (f32[2,160,512]{2,1,0:T(8,128)}, f32[2,160,512]{2,1,0:T(8,128)}, u32[]{:S(2)}, u32[]{:S(2)}) collective-permute-start(f32[2,160,512]{2,1,0:T(8,128)} %get-tuple-element.33), channel_id=1, source_target_pairs={{0,64},{16,80},{32,96},{48,112},{64,0},{80,16},{96,32},{112,48},{1... | collective-permute-start | bytes 1966088 | tf_op jit(solution)/shard_map/ppermute | solution.py:40
  7.8 0.8 copy.8.index_ref
  8.6 4.8 %pick_rows.4 = (f32[4,160,512]{2,1,0:T(8,128)}, f32[4,160,512]{2,1,0:T(8,128)S(1)}) custom-call(s32[320,1]{1,0:T(8,128)S(1)} %copy.8.index_ref, f32[12,512,320]{2,1,0:T(8,128)} %bitcast.40), custom_call_target="tpu_custom_call" | custom-call | flops 999999995904 | bytes 10000000000 | tf_op jit(solution)/shard_map/pick_rows/pallas_call | solution.py:69
  13.4 1.1 copy-done.9
  14.9 6.5 %pick_rows.5 = (f32[6,160,512]{2,1,0:T(8,128)}, f32[6,160,512]{2,1,0:T(8,128)S(1)}) custom-call(s32[320,1]{1,0:T(8,128)S(1)} %copy.9.index_ref, f32[12,512,320]{2,1,0:T(8,128)} %bitcast.41), custom_call_target="tpu_custom_call" | custom-call | flops 999999995904 | bytes 10000000000 | tf_op jit(solution)/shard_map/pick_rows/pallas_call | solution.py:69
  21.4 3.3 %collective-permute-start = (f32[6,160,512]{2,1,0:T(8,128)}, f32[6,160,512]{2,1,0:T(8,128)}, u32[]{:S(2)}, u32[]{:S(2)}) collective-permute-start(f32[6,160,512]{2,1,0:T(8,128)} %get-tuple-element.39), channel_id=1, source_target_pairs={{0,64},{16,80},{32,96},{48,112},{64,0},{80,16},{96,32},{112,48},{1... | collective-permute-start | bytes 5898248 | tf_op jit(solution)/shard_map/ppermute | solution.py:40
  24.7 17.1 %lay_out.1.refs_4_.refs_2_ = bf16[12,2,8,96,384]{4,3,2,1,0:T(8,128)(2,1)} custom-call(f32[12,160,2,648]{3,2,1,0:T(2,128)} %refs_5_, f32[12,160,2,648]{3,2,1,0:T(2,128)} %refs_5_, f32[12,160,2,648]{3,2,1,0:T(2,128)} %refs_5_, f32[12,160,2,648]{3,2,1,0:T(2,128)} %refs_5_, f32[12,160,2,648]{3,2,1,0:T(2,128)} %refs_5_, f32[12,160,2,648]{3,2,1,0:T(2,128)} %refs_5_), custom_call_target="tpu_custom_call" | custom-call | flops 999999995904 | bytes 10000000000 | tf_op jit(solution)/shard_map/lay_out/pallas_call | solution.py:117
  41.9 10.2 %collective-permute-done.2.refs_3_ = f32[4,160,512]{2,1,0:T(8,128)} collective-permute-done((f32[4,160,512]{2,1,0:T(8,128)}, f32[4,160,512]{2,1,0:T(8,128)}, u32[]{:S(2)}, u32[]{:S(2)}) %collective-permute-start.2) | collective-permute-done | bytes 1310752 | tf_op jit(solution)/shard_map/ppermute | solution.py:40
  52.1 16.7 %project.2 = (f32[4,976,256]{2,1,0:T(8,128)}, f32[1,976,256]{2,1,0:T(8,128)S(1)}, f32[1,976,256]{2,1,0:T(8,128)S(1)}, f32[1,976,256]{2,1,0:T(8,128)S(1)}, f32[1,976,256]{2,1,0:T(8,128)S(1)}) custom-call(s32[3]{0:T(128)S(1)} %pad_add_fusion.place_ref, s32[12]{0:T(128)S(1)} %copy-done.8, f32[2,160,512]{2,1,0:T(8,128)S(1)} %get-tuple-element.40.refs_0_, ...), custom_call_target="tpu_custom_call" | custom-call | flops 999999995904 | bytes 10000000000 | tf_op jit(solution)/shard_map/project/pallas_call | solution.py:223
  68.7 0.5 collective-permute-start.4
  69.3 0.5 collective-permute-start.6
  69.8 1.6 collective-permute-done.3
  71.3 1.4 collective-permute-done.4
  72.8 3.0 %bitcast_add_fusion.2 = (f32[976,256]{1,0:T(8,128)}, f32[976,256]{1,0:T(8,128)}) fusion(f32[976,256]{1,0:T(8,128)S(1)} %bitcast.38, f32[4,976,256]{2,1,0:T(8,128)} %get-tuple-element.46.mine_ref, f32[976,256]{1,0:T(8,128)S(1)} %bitcast.37), kind=kLoop, calls=%fused_computation.2 | loop fusion | flops 499712 | bytes 5996544 | tf_op jit(solution)/shard_map/add | solution.py:388
  75.8 3.1 %collective-permute-start.11 = (f32[976,256]{1,0:T(8,128)}, f32[976,256]{1,0:T(8,128)}, u32[]{:S(2)}, u32[]{:S(2)}) collective-permute-start(f32[976,256]{1,0:T(8,128)} %get-tuple-element.70), channel_id=1, source_target_pairs={{0,96},{16,112},{32,0},{48,16},{64,32},{80,48},{96,64},{112,80},{1... | collective-permute-start | bytes 2998280 | tf_op jit(solution)/shard_map/ppermute | solution.py:40
  78.9 15.3 %collective-permute-done.refs_1_ = f32[6,160,512]{2,1,0:T(8,128)} collective-permute-done((f32[6,160,512]{2,1,0:T(8,128)}, f32[6,160,512]{2,1,0:T(8,128)}, u32[]{:S(2)}, u32[]{:S(2)}) %collective-permute-start) | collective-permute-done | bytes 1966112 | tf_op jit(solution)/shard_map/ppermute | solution.py:40
  94.3 1.0 copy-done.6
  95.2 16.2 %project.3 = (f32[4,976,256]{2,1,0:T(8,128)}, f32[1,976,256]{2,1,0:T(8,128)S(1)}, f32[1,976,256]{2,1,0:T(8,128)S(1)}, f32[2,976,256]{2,1,0:T(8,128)}) custom-call(s32[3]{0:T(128)S(1)} %pad_add_fusion.place_ref, s32[12]{0:T(128)S(1)} %copy-done.8, f32[6,160,512]{2,1,0:T(8,128)S(1)} %get-tuple-element.38.refs_0_, f32[6,160,512]{2,1,0:T(8,128)} %collective-permute-done.refs_1_, ...), custom_call_target="tpu_custom_call" | custom-call | flops 999999995904 | bytes 10000000000 | tf_op jit(solution)/shard_map/project/pallas_call | solution.py:223
  111.5 0.5 collective-permute-start.9
  112.1 2.8 %collective-permute-done.11.near_down_ref = f32[976,256]{1,0:T(8,128)} collective-permute-done((f32[976,256]{1,0:T(8,128)}, f32[976,256]{1,0:T(8,128)}, u32[]{:S(2)}, u32[]{:S(2)}) %collective-permute-start.11) | collective-permute-done | bytes 999456 | tf_op jit(solution)/shard_map/ppermute | solution.py:40
  114.9 2.0 slice_add_fusion.3
  117.2 3.2 %collective-permute-start.14 = (f32[976,256]{1,0:T(8,128)S(1)}, f32[976,256]{1,0:T(8,128)S(1)}, u32[]{:S(2)}, u32[]{:S(2)}) collective-permute-start(f32[976,256]{1,0:T(8,128)S(1)} %get-tuple-element.68), channel_id=1, source_target_pairs={{0,96},{16,112},{32,0},{48,16},{64,32},{80,48},{96,64},{112,80},{1... | collective-permute-start | bytes 2998280 | tf_op jit(solution)/shard_map/ppermute | solution.py:40
  120.4 3.2 %collective-permute-start.17 = (f32[488,256]{1,0:T(8,128)S(1)}, f32[488,256]{1,0:T(8,128)S(1)}, u32[]{:S(2)}, u32[]{:S(2)}) collective-permute-start(f32[488,256]{1,0:T(8,128)S(1)} %get-tuple-element.66), channel_id=1, source_target_pairs={{0,96},{16,112},{32,0},{48,16},{64,32},{80,48},{96,64},{112,80},{1... | collective-permute-start | bytes 1499144 | tf_op jit(solution)/shard_map/ppermute | solution.py:40
  123.6 19.2 %collective-permute-done.14.near_down_ref = f32[976,256]{1,0:T(8,128)S(1)} collective-permute-done((f32[976,256]{1,0:T(8,128)S(1)}, f32[976,256]{1,0:T(8,128)S(1)}, u32[]{:S(2)}, u32[]{:S(2)}) %collective-permute-start.14) | collective-permute-done | bytes 999456 | tf_op jit(solution)/shard_map/ppermute | solution.py:40
  142.9 3.7 %collective-permute-done.12.near_up_ref = f32[976,256]{1,0:T(8,128)S(1)} collective-permute-done((f32[976,256]{1,0:T(8,128)S(1)}, f32[976,256]{1,0:T(8,128)S(1)}, u32[]{:S(2)}, u32[]{:S(2)}) %collective-permute-start.12) | collective-permute-done | bytes 999456 | tf_op jit(solution)/shard_map/ppermute | solution.py:40
  146.6 1.3 slice_add_fusion
  147.9 1.3 copy-done
  149.2 2.0 collective-permute-start.13
  151.2 2.3 %collective-permute-done.17.far_down_ref = f32[488,256]{1,0:T(8,128)S(1)} collective-permute-done((f32[488,256]{1,0:T(8,128)S(1)}, f32[488,256]{1,0:T(8,128)S(1)}, u32[]{:S(2)}, u32[]{:S(2)}) %collective-permute-start.17) | collective-permute-done | bytes 499744 | tf_op jit(solution)/shard_map/ppermute | solution.py:40
  153.6 3.7 %collective-permute-done.16.far_up_ref = f32[488,256]{1,0:T(8,128)S(1)} collective-permute-done((f32[488,256]{1,0:T(8,128)S(1)}, f32[488,256]{1,0:T(8,128)S(1)}, u32[]{:S(2)}, u32[]{:S(2)}) %collective-permute-start.16) | collective-permute-done | bytes 499744 | tf_op jit(solution)/shard_map/ppermute | solution.py:40
  157.3 4.4 %finish.2 = (f32[12,2,4,64,81]{4,3,2,1,0:T(8,128)}, f32[16,128]{1,0:T(8,128)S(1)}) custom-call(s32[3]{0:T(128)S(1)} %pad_add_fusion.place_ref, s32[12]{0:T(128)S(1)} %copy-done.8, f32[4,976,256]{2,1,0:T(8,128)} %get-tuple-element.46.mine_ref, f32[1,976,256]{2,1,0:T(8,128)S(1)} %copy-done.7, f32[488,256]{1,0:T(8,128)S(1)} %collective-permute-done.16.far_up_ref, ...), custom_call_target="tpu_custom_call" | custom-call | flops 999999995904 | bytes 10000000000 | tf_op jit(solution)/shard_map/finish/pallas_call | solution.py:309
  161.7 1.9 collective-permute-done.15.far_down_ref
  163.6 3.4 %collective-permute-done.13.far_up_ref = f32[488,256]{1,0:T(8,128)} collective-permute-done((f32[488,256]{1,0:T(8,128)}, f32[488,256]{1,0:T(8,128)}, u32[]{:S(2)}, u32[]{:S(2)}) %collective-permute-start.13) | collective-permute-done | bytes 499744 | tf_op jit(solution)/shard_map/ppermute | solution.py:40
  167.0 3.8 %finish.3 = (f32[12,2,4,64,81]{4,3,2,1,0:T(8,128)}, f32[16,128]{1,0:T(8,128)S(1)}) custom-call(s32[3]{0:T(128)S(1)} %pad_add_fusion.place_ref, s32[12]{0:T(128)S(1)} %copy-done.8, f32[4,976,256]{2,1,0:T(8,128)} %get-tuple-element.54.mine_ref, f32[2,976,256]{2,1,0:T(8,128)S(1)} %copy-done.1, ...), custom_call_target="tpu_custom_call", output_to_operand_aliasing={{0}: (8, {})} | custom-call | flops 999999995904 | bytes 10000000000 | tf_op jit(solution)/shard_map/finish/pallas_call | solution.py:309
  170.8 1.2 collective-permute-done.18
  171.9 3.0 %collective-permute-start.19 = (f32[16,128]{1,0:T(8,128)S(1)}, f32[16,128]{1,0:T(8,128)S(1)}, u32[]{:S(2)}, u32[]{:S(2)}) collective-permute-start(f32[16,128]{1,0:T(8,128)S(1)} %add.122), channel_id=1, source_target_pairs={{0,1},{1,0},{2,3},{3,2},{4,5},{5,4},{6,7},{7,6},{8,9},{9,8},{10,11... | collective-permute-start | bytes 24584 | tf_op jit(solution)/shard_map/ppermute | solution.py:331
  175.0 2.1 %collective-permute-done.19 = f32[16,128]{1,0:T(8,128)S(1)} collective-permute-done((f32[16,128]{1,0:T(8,128)S(1)}, f32[16,128]{1,0:T(8,128)S(1)}, u32[]{:S(2)}, u32[]{:S(2)}) %collective-permute-start.19) | collective-permute-done | bytes 8224 | tf_op jit(solution)/shard_map/ppermute | solution.py:331
  177.1 1.5 collective-permute-start.20
  178.6 2.2 %collective-permute-done.20 = f32[16,128]{1,0:T(8,128)S(1)} collective-permute-done((f32[16,128]{1,0:T(8,128)S(1)}, f32[16,128]{1,0:T(8,128)S(1)}, u32[]{:S(2)}, u32[]{:S(2)}) %collective-permute-start.20) | collective-permute-done | bytes 8224 | tf_op jit(solution)/shard_map/ppermute | solution.py:331
  180.7 1.9 collective-permute-start.21
  182.7 1.7 collective-permute-done.21
  184.4 3.6 %collective-permute-done.22 = f32[16,128]{1,0:T(8,128)S(1)} collective-permute-done((f32[16,128]{1,0:T(8,128)S(1)}, f32[16,128]{1,0:T(8,128)S(1)}, u32[]{:S(2)}, u32[]{:S(2)}) %collective-permute-start.22) | collective-permute-done | bytes 8224 | tf_op jit(solution)/shard_map/ppermute | solution.py:331
  188.1 3.9 %collective-permute-start.23 = (f32[16,128]{1,0:T(8,128)S(1)}, f32[16,128]{1,0:T(8,128)S(1)}, u32[]{:S(2)}, u32[]{:S(2)}) collective-permute-start(f32[16,128]{1,0:T(8,128)S(1)} %add.126), channel_id=1, source_target_pairs={{0,8},{2,10},{4,12},{6,14},{8,0},{10,2},{12,4},{14,6},{1,9},{3,11}... | collective-permute-start | bytes 24584 | tf_op jit(solution)/shard_map/ppermute | solution.py:331
  191.9 1.6 collective-permute-done.23
  193.6 5.2 %collective-permute-done.24 = f32[16,128]{1,0:T(8,128)S(1)} collective-permute-done((f32[16,128]{1,0:T(8,128)S(1)}, f32[16,128]{1,0:T(8,128)S(1)}, u32[]{:S(2)}, u32[]{:S(2)}) %collective-permute-start.24) | collective-permute-done | bytes 8224 | tf_op jit(solution)/shard_map/ppermute | solution.py:331
  198.7 0.6 slice_log_fusion
  (57 shorter events, 1.1 us)
Async XLA Ops:
  1.4 3.1 %copy-start.12 = (s32[320,1]{0,1:T(1,128)}, s32[320,1]{0,1:T(1,128)S(1)}, u32[]{:S(2)}) copy-start(s32[320,1]{0,1:T(1,128)S(1)} %reshape.25) | copy-start | bytes 3844
  4.5 37.3 %collective-permute-start.1 = (f32[2,160,512]{2,1,0:T(8,128)}, f32[2,160,512]{2,1,0:T(8,128)}, u32[]{:S(2)}, u32[]{:S(2)}) collective-permute-start(f32[2,160,512]{2,1,0:T(8,128)} %get-tuple-element.33), channel_id=1, source_target_pairs={{0,64},{16,80},{32,96},{48,112},{64,0},{80,16},{96,32},{112,48},{1... | collective-permute-start | bytes 1966088 | tf_op jit(solution)/shard_map/ppermute | solution.py:40
  8.6 6.1 %copy-start.13 = (s32[320,1]{0,1:T(1,128)S(1)}, s32[320,1]{0,1:T(1,128)}, u32[]{:S(2)}) copy-start(s32[320,1]{0,1:T(1,128)} %copy-done.12) | copy-start | bytes 3844
  13.4 1.1 copy-start.9
  14.5 37.6 %collective-permute-start.2 = (f32[4,160,512]{2,1,0:T(8,128)}, f32[4,160,512]{2,1,0:T(8,128)}, u32[]{:S(2)}, u32[]{:S(2)}) collective-permute-start(f32[4,160,512]{2,1,0:T(8,128)} %get-tuple-element.36), channel_id=1, source_target_pairs={{0,64},{16,80},{32,96},{48,112},{64,0},{80,16},{96,32},{112,48},{1... | collective-permute-start | bytes 3932168 | tf_op jit(solution)/shard_map/ppermute | solution.py:40
  21.4 72.8 %collective-permute-start = (f32[6,160,512]{2,1,0:T(8,128)}, f32[6,160,512]{2,1,0:T(8,128)}, u32[]{:S(2)}, u32[]{:S(2)}) collective-permute-start(f32[6,160,512]{2,1,0:T(8,128)} %get-tuple-element.39), channel_id=1, source_target_pairs={{0,64},{16,80},{32,96},{48,112},{64,0},{80,16},{96,32},{112,48},{1... | collective-permute-start | bytes 5898248 | tf_op jit(solution)/shard_map/ppermute | solution.py:40
  24.7 27.3 %copy-start.8 = (s32[12]{0:T(128)S(1)}, s32[12]{0:T(128)}, u32[]{:S(2)}) copy-start(s32[12]{0:T(128)} %wave_ref.7) | copy-start | bytes 148
  68.7 2.6 %collective-permute-start.3 = (f32[1,976,256]{2,1,0:T(8,128)S(1)}, f32[1,976,256]{2,1,0:T(8,128)S(1)}, u32[]{:S(2)}, u32[]{:S(2)}) collective-permute-start(f32[1,976,256]{2,1,0:T(8,128)S(1)} %get-tuple-element.47), channel_id=1, source_target_pairs={{0,16},{16,0},{32,48},{48,32},{64,80},{80,64},{96,112},{112,96},{1... | collective-permute-start | bytes 2998280 | tf_op jit(solution)/shard_map/ppermute | solution.py:40
  68.7 4.0 %collective-permute-start.4 = (f32[1,976,256]{2,1,0:T(8,128)S(1)}, f32[1,976,256]{2,1,0:T(8,128)S(1)}, u32[]{:S(2)}, u32[]{:S(2)}) collective-permute-start(f32[1,976,256]{2,1,0:T(8,128)S(1)} %get-tuple-element.48), channel_id=1, source_target_pairs={{0,16},{16,0},{32,48},{48,32},{64,80},{80,64},{96,112},{112,96},{1... | collective-permute-start | bytes 2998280 | tf_op jit(solution)/shard_map/ppermute | solution.py:40
  69.2 25.0 %collective-permute-start.5 = (f32[1,976,256]{2,1,0:T(8,128)S(1)}, f32[1,976,256]{2,1,0:T(8,128)S(1)}, u32[]{:S(2)}, u32[]{:S(2)}) collective-permute-start(f32[1,976,256]{2,1,0:T(8,128)S(1)} %get-tuple-element.51), channel_id=1, source_target_pairs={{0,16},{16,0},{32,48},{48,32},{64,80},{80,64},{96,112},{112,96},{1... | collective-permute-start | bytes 2998280 | tf_op jit(solution)/shard_map/ppermute | solution.py:40
  69.3 25.0 %collective-permute-start.6 = (f32[1,976,256]{2,1,0:T(8,128)S(1)}, f32[1,976,256]{2,1,0:T(8,128)S(1)}, u32[]{:S(2)}, u32[]{:S(2)}) collective-permute-start(f32[1,976,256]{2,1,0:T(8,128)S(1)} %get-tuple-element.52), channel_id=1, source_target_pairs={{0,16},{16,0},{32,48},{48,32},{64,80},{80,64},{96,112},{112,96},{1... | collective-permute-start | bytes 2998280 | tf_op jit(solution)/shard_map/ppermute | solution.py:40
  75.8 39.1 %collective-permute-start.11 = (f32[976,256]{1,0:T(8,128)}, f32[976,256]{1,0:T(8,128)}, u32[]{:S(2)}, u32[]{:S(2)}) collective-permute-start(f32[976,256]{1,0:T(8,128)} %get-tuple-element.70), channel_id=1, source_target_pairs={{0,96},{16,112},{32,0},{48,16},{64,32},{80,48},{96,64},{112,80},{1... | collective-permute-start | bytes 2998280 | tf_op jit(solution)/shard_map/ppermute | solution.py:40
  78.9 36.0 %collective-permute-start.10 = (f32[976,256]{1,0:T(8,128)}, f32[976,256]{1,0:T(8,128)}, u32[]{:S(2)}, u32[]{:S(2)}) collective-permute-start(f32[976,256]{1,0:T(8,128)} %get-tuple-element.71), channel_id=1, source_target_pairs={{0,32},{16,48},{32,64},{48,80},{64,96},{80,112},{96,0},{112,16},{1... | collective-permute-start | bytes 2998280 | tf_op jit(solution)/shard_map/ppermute | solution.py:40
  94.2 17.3 %copy-start.11 = (f32[1,976,256]{2,1,0:T(8,128)}, f32[1,976,256]{2,1,0:T(8,128)S(1)}, u32[]{:S(2)}) copy-start(f32[1,976,256]{2,1,0:T(8,128)S(1)} %collective-permute-done.5) | copy-start | bytes 2998276
  94.2 1.0 copy-start.6
  111.5 5.5 %copy-start.10 = (f32[4,976,256]{2,1,0:T(8,128)S(1)}, f32[4,976,256]{2,1,0:T(8,128)}, u32[]{:S(2)}) copy-start(f32[4,976,256]{2,1,0:T(8,128)} %get-tuple-element.54.mine_ref) | copy-start | bytes 11993092
  111.5 5.4 %collective-permute-start.8 = (f32[1,976,256]{2,1,0:T(8,128)S(1)}, f32[1,976,256]{2,1,0:T(8,128)S(1)}, u32[]{:S(2)}, u32[]{:S(2)}) collective-permute-start(f32[1,976,256]{2,1,0:T(8,128)S(1)} %get-tuple-element.56), channel_id=1, source_target_pairs={{0,16},{16,0},{32,48},{48,32},{64,80},{80,64},{96,112},{112,96},{1... | collective-permute-start | bytes 2998280 | tf_op jit(solution)/shard_map/ppermute | solution.py:40
  111.5 5.4 %collective-permute-start.9 = (f32[1,976,256]{2,1,0:T(8,128)S(1)}, f32[1,976,256]{2,1,0:T(8,128)S(1)}, u32[]{:S(2)}, u32[]{:S(2)}) collective-permute-start(f32[1,976,256]{2,1,0:T(8,128)S(1)} %get-tuple-element.57), channel_id=1, source_target_pairs={{0,16},{16,0},{32,48},{48,32},{64,80},{80,64},{96,112},{112,96},{1... | collective-permute-start | bytes 2998280 | tf_op jit(solution)/shard_map/ppermute | solution.py:40
  112.0 34.6 %collective-permute-start.7 = (f32[2,976,256]{2,1,0:T(8,128)}, f32[2,976,256]{2,1,0:T(8,128)S(1)}, u32[]{:S(2)}, u32[]{:S(2)}) collective-permute-start(f32[2,976,256]{2,1,0:T(8,128)} %get-tuple-element.55), channel_id=1, source_target_pairs={{0,16},{16,0},{32,48},{48,32},{64,80},{80,64},{96,112},{112,96},{1... | collective-permute-start | bytes 5996552 | tf_op jit(solution)/shard_map/ppermute | solution.py:40
  117.2 40.1 %copy-start.7 = (f32[1,976,256]{2,1,0:T(8,128)S(1)}, f32[1,976,256]{2,1,0:T(8,128)}, u32[]{:S(2)}) copy-start(f32[1,976,256]{2,1,0:T(8,128)} %copy-done.6) | copy-start | bytes 2998276
  117.2 25.6 %collective-permute-start.14 = (f32[976,256]{1,0:T(8,128)S(1)}, f32[976,256]{1,0:T(8,128)S(1)}, u32[]{:S(2)}, u32[]{:S(2)}) collective-permute-start(f32[976,256]{1,0:T(8,128)S(1)} %get-tuple-element.68), channel_id=1, source_target_pairs={{0,96},{16,112},{32,0},{48,16},{64,32},{80,48},{96,64},{112,80},{1... | collective-permute-start | bytes 2998280 | tf_op jit(solution)/shard_map/ppermute | solution.py:40
  120.4 26.2 %collective-permute-start.12 = (f32[976,256]{1,0:T(8,128)S(1)}, f32[976,256]{1,0:T(8,128)S(1)}, u32[]{:S(2)}, u32[]{:S(2)}) collective-permute-start(f32[976,256]{1,0:T(8,128)S(1)} %get-tuple-element.69), channel_id=1, source_target_pairs={{0,32},{16,48},{32,64},{48,80},{64,96},{80,112},{96,0},{112,16},{1... | collective-permute-start | bytes 2998280 | tf_op jit(solution)/shard_map/ppermute | solution.py:40
  120.4 33.2 %collective-permute-start.17 = (f32[488,256]{1,0:T(8,128)S(1)}, f32[488,256]{1,0:T(8,128)S(1)}, u32[]{:S(2)}, u32[]{:S(2)}) collective-permute-start(f32[488,256]{1,0:T(8,128)S(1)} %get-tuple-element.66), channel_id=1, source_target_pairs={{0,96},{16,112},{32,0},{48,16},{64,32},{80,48},{96,64},{112,80},{1... | collective-permute-start | bytes 1499144 | tf_op jit(solution)/shard_map/ppermute | solution.py:40
  123.6 33.7 %collective-permute-start.16 = (f32[488,256]{1,0:T(8,128)S(1)}, f32[488,256]{1,0:T(8,128)S(1)}, u32[]{:S(2)}, u32[]{:S(2)}) collective-permute-start(f32[488,256]{1,0:T(8,128)S(1)} %get-tuple-element.67), channel_id=1, source_target_pairs={{0,32},{16,48},{32,64},{48,80},{64,96},{80,112},{96,0},{112,16},{1... | collective-permute-start | bytes 1499144 | tf_op jit(solution)/shard_map/ppermute | solution.py:40
  142.8 10.7 %copy-start.2 = (f32[976,256]{1,0:T(8,128)}, f32[976,256]{1,0:T(8,128)S(1)}, u32[]{:S(2)}) copy-start(f32[976,256]{1,0:T(8,128)S(1)} %collective-permute-done.14.near_down_ref) | copy-start | bytes 2998276
  146.6 7.0 %copy-start.4 = (f32[976,256]{1,0:T(8,128)}, f32[976,256]{1,0:T(8,128)S(1)}, u32[]{:S(2)}) copy-start(f32[976,256]{1,0:T(8,128)S(1)} %collective-permute-done.12.near_up_ref) | copy-start | bytes 2998276
  147.9 1.3 copy-start
  149.2 14.4 %collective-permute-start.15 = (f32[488,256]{1,0:T(8,128)}, f32[488,256]{1,0:T(8,128)}, u32[]{:S(2)}, u32[]{:S(2)}) collective-permute-start(f32[488,256]{1,0:T(8,128)} %get-tuple-element.64), channel_id=1, source_target_pairs={{0,96},{16,112},{32,0},{48,16},{64,32},{80,48},{96,64},{112,80},{1... | collective-permute-start | bytes 1499144 | tf_op jit(solution)/shard_map/ppermute | solution.py:40
  149.2 17.7 %collective-permute-start.13 = (f32[488,256]{1,0:T(8,128)}, f32[488,256]{1,0:T(8,128)}, u32[]{:S(2)}, u32[]{:S(2)}) collective-permute-start(f32[488,256]{1,0:T(8,128)} %get-tuple-element.65), channel_id=1, source_target_pairs={{0,32},{16,48},{32,64},{48,80},{64,96},{80,112},{96,0},{112,16},{1... | collective-permute-start | bytes 1499144 | tf_op jit(solution)/shard_map/ppermute | solution.py:40
  157.3 9.7 %copy-start.1 = (f32[2,976,256]{2,1,0:T(8,128)S(1)}, f32[2,976,256]{2,1,0:T(8,128)}, u32[]{:S(2)}) copy-start(f32[2,976,256]{2,1,0:T(8,128)} %copy-done) | copy-start | bytes 5996548
  157.3 9.7 %copy-start.3 = (f32[976,256]{1,0:T(8,128)S(1)}, f32[976,256]{1,0:T(8,128)}, u32[]{:S(2)}) copy-start(f32[976,256]{1,0:T(8,128)} %copy-done.2) | copy-start | bytes 2998276
  157.3 9.7 %copy-start.5 = (f32[976,256]{1,0:T(8,128)S(1)}, f32[976,256]{1,0:T(8,128)}, u32[]{:S(2)}) copy-start(f32[976,256]{1,0:T(8,128)} %copy-done.4) | copy-start | bytes 2998276
  170.8 1.2 collective-permute-start.18
  171.9 5.2 %collective-permute-start.19 = (f32[16,128]{1,0:T(8,128)S(1)}, f32[16,128]{1,0:T(8,128)S(1)}, u32[]{:S(2)}, u32[]{:S(2)}) collective-permute-start(f32[16,128]{1,0:T(8,128)S(1)} %add.122), channel_id=1, source_target_pairs={{0,1},{1,0},{2,3},{3,2},{4,5},{5,4},{6,7},{7,6},{8,9},{9,8},{10,11... | collective-permute-start | bytes 24584 | tf_op jit(solution)/shard_map/ppermute | solution.py:331
  177.1 3.7 %collective-permute-start.20 = (f32[16,128]{1,0:T(8,128)S(1)}, f32[16,128]{1,0:T(8,128)S(1)}, u32[]{:S(2)}, u32[]{:S(2)}) collective-permute-start(f32[16,128]{1,0:T(8,128)S(1)} %add.123), channel_id=1, source_target_pairs={{0,2},{2,0},{4,6},{6,4},{8,10},{10,8},{12,14},{14,12},{1,3},{3,1},... | collective-permute-start | bytes 24584 | tf_op jit(solution)/shard_map/ppermute | solution.py:331
  180.7 3.7 %collective-permute-start.21 = (f32[16,128]{1,0:T(8,128)S(1)}, f32[16,128]{1,0:T(8,128)S(1)}, u32[]{:S(2)}, u32[]{:S(2)}) collective-permute-start(f32[16,128]{1,0:T(8,128)S(1)} %add.124), channel_id=1, source_target_pairs={{0,4},{2,6},{4,0},{6,2},{8,12},{10,14},{12,8},{14,10},{1,5},{3,7},... | collective-permute-start | bytes 24584 | tf_op jit(solution)/shard_map/ppermute | solution.py:331
  184.4 3.7 %collective-permute-start.22 = (f32[16,128]{1,0:T(8,128)S(1)}, f32[16,128]{1,0:T(8,128)S(1)}, u32[]{:S(2)}, u32[]{:S(2)}) collective-permute-start(f32[16,128]{1,0:T(8,128)S(1)} %add.125), channel_id=1, source_target_pairs={{0,32},{16,48},{32,0},{48,16},{64,96},{80,112},{96,64},{112,80},{1... | collective-permute-start | bytes 24584 | tf_op jit(solution)/shard_map/ppermute | solution.py:331
  188.1 5.5 %collective-permute-start.23 = (f32[16,128]{1,0:T(8,128)S(1)}, f32[16,128]{1,0:T(8,128)S(1)}, u32[]{:S(2)}, u32[]{:S(2)}) collective-permute-start(f32[16,128]{1,0:T(8,128)S(1)} %add.126), channel_id=1, source_target_pairs={{0,8},{2,10},{4,12},{6,14},{8,0},{10,2},{12,4},{14,6},{1,9},{3,11}... | collective-permute-start | bytes 24584 | tf_op jit(solution)/shard_map/ppermute | solution.py:331
  193.6 5.2 %collective-permute-start.24 = (f32[16,128]{1,0:T(8,128)S(1)}, f32[16,128]{1,0:T(8,128)S(1)}, u32[]{:S(2)}, u32[]{:S(2)}) collective-permute-start(f32[16,128]{1,0:T(8,128)S(1)} %add.127), channel_id=1, source_target_pairs={{0,64},{16,80},{32,96},{48,112},{64,0},{80,16},{96,32},{112,48},{1... | collective-permute-start | bytes 24584 | tf_op jit(solution)/shard_map/ppermute | solution.py:331

commit v4 on v3

v4 whole, which is shorter than its diff:
```python
import functools

import jax
import jax.numpy as jnp
from jax import lax
from jax.experimental import pallas as pl
from jax.experimental.pallas import tpu as pltpu
from jax.sharding import PartitionSpec as P

NDEG = 1280
MESSAGES = (2, 4, 6)
RUNS = ((0, 1), (2,))
F32 = jnp.float32
BF16 = jnp.bfloat16
VMEM_LIMIT = 48 * 1024 * 1024
VMEM_SMALL = 16 * 1024 * 1024


def behind(x, after):
    return lax.optimization_barrier((x, after))[0]


def split_two(x):
    high = x.astype(BF16)
    low = (x - high.astype(F32)).astype(BF16)
    return high, low


def split_three(x):
    high = x.astype(BF16)
    rest = x - high.astype(F32)
    middle = rest.astype(BF16)
    return high, middle, (rest - middle.astype(F32)).astype(BF16)


def dot_nt(a, b):
    return lax.dot_general(a, b, (((1,), (1,)), ((), ())), preferred_element_type=F32)


def dot_nn(a, b):
    return jnp.dot(a, b, preferred_element_type=F32)


def send_along(x, up, cross):
    size = lax.axis_size("band")
    chips = size // 2
    pairs = [(i, ((i // 2 + up) % chips) * 2 + ((i % 2) ^ cross)) for i in range(size)]
    return lax.ppermute(x, "band", pairs)


def pick_kernel(index_ref, field_ref, send_ref, keep_ref, main_ref, tail_ref):
    count, main = main_ref.shape
    half = count // 2
    rows = field_ref.shape[2]

    @pl.when(pl.program_id(0) == 0)
    def _():
        lanes = lax.broadcasted_iota(jnp.int32, (count, rows), 1)
        chosen = jnp.where(index_ref[...] == lanes, 1.0, 0.0)
        main_ref[...] = chosen[:, :main].astype(BF16)
        tail_ref[...] = jnp.concatenate([chosen[:, main:], chosen[:, main:]], 1).astype(BF16)

    high, low = split_two(field_ref[0])
    tail = jnp.concatenate([high[:, main:], low[:, main:]], 1)
    picked = dot_nt(main_ref[...], high[:, :main]) + dot_nt(main_ref[...], low[:, :main]) + dot_nt(tail_ref[...], tail)
    send_ref[0] = picked[:half]
    keep_ref[0] = picked[half:]


def pick_rows(index, field, first, each):
    pairs, width, rows = field.shape
    count = index.shape[0]
    half = count // 2
    main = 256
    shape = jax.ShapeDtypeStruct((each, half, width), F32)
    out = pl.BlockSpec((1, half, width), lambda step: (step, 0, 0))
    return pl.pallas_call(
        pick_kernel,
        grid=(each,),
        in_specs=[
            pl.BlockSpec((count, 1), lambda step: (0, 0)),
            pl.BlockSpec((1, width, rows), lambda step: (first + step, 0, 0)),
        ],
        out_specs=[out, out],
        out_shape=[shape, shape],
        scratch_shapes=[pltpu.VMEM((count, main), BF16), pltpu.VMEM((count, 2 * (rows - main)), BF16)],
        compiler_params=pltpu.CompilerParams(vmem_limit_bytes=VMEM_LIMIT),
        cost_estimate=pl.CostEstimate(flops=10**12, bytes_accessed=10**10, transcendentals=0),
        name="pick_rows",
    )(index, field)


def layout_kernel(*refs, share):
    out_ref = refs[-1]
    lanes = main = 128
    half = refs[0].shape[1]
    rest = main - 3 * (half - main)
    for parity in range(2):
        for tile, ref in enumerate(refs[:-1]):
            high, low = split_two(ref.reshape(1, 2 * half, lanes)[0, pl.ds(parity, half, stride=2), :])
            blocks = (
                high[:main],
                low[:main],
                jnp.concatenate([high[main:], high[main:], low[main:], jnp.zeros((rest, lanes), BF16)], 0),
            )
            for i, block in enumerate(blocks):
                turned = block.T
                for s in range(out_ref.shape[2]):
                    first = max(s * share, tile * lanes)
                    last = min((s + 1) * share, (tile + 1) * lanes)
                    if first < last:
                        out_ref[0, parity, s, first - s * share : last - s * share, main * i : main * (i + 1)] = turned[
                            first - tile * lanes : last - tile * lanes
                        ]


def lay_out(table, share, padded):
    pairs, half, _, slots = table.shape
    shares = slots // share
    tiles = (slots + 127) // 128

    def block(tile):
        return pl.BlockSpec((1, half, 2, 128), lambda step: (step, 0, 0, tile))

    return pl.pallas_call(
        functools.partial(layout_kernel, share=share),
        grid=(pairs,),
        in_specs=[block(tile) for tile in range(tiles)],
        out_specs=pl.BlockSpec((1, 2, shares, padded, 384), lambda step: (step, 0, 0, 0, 0)),
        out_shape=jax.ShapeDtypeStruct((pairs, 2, shares, padded, 384), BF16),
        compiler_params=pltpu.CompilerParams(vmem_limit_bytes=VMEM_LIMIT),
        cost_estimate=pl.CostEstimate(flops=10**12, bytes_accessed=10**10, transcendentals=0),
        name="lay_out",
    )(*[table] * tiles)


def owner_of(place, step, ups, chip, chips):
    up = jnp.where(step < ups, 1, 0)
    ahead = (1 + up, 2 + up, jnp.where(step < ups, 1, chips - 1), 0)[place]
    return lax.rem(chip + ahead, chips)


def project_kernel(place_ref, wave_ref, *refs, share, first, starts, ups):
    count = len(starts)
    keep_refs, recv_refs = refs[:count], refs[count : 2 * count]
    table_ref, mine_ref, *cross_refs, field_ref, result_ref = refs[2 * count :]
    step = pl.program_id(0)
    core = place_ref[0]
    chip = place_ref[1]
    chips = place_ref[2]
    first_m = wave_ref[first + step]
    half = keep_refs[0].shape[1]
    width = keep_refs[0].shape[2] // 2
    main = 128
    tail = half - main
    shares, padded = table_ref.shape[2:4]
    middle = shares // 2
    side = jnp.where(chip < chips // 2, 1.0, -1.0)
    for parity in range(2):
        keep, recv = keep_refs[0][0], recv_refs[0][0]
        for start, keep_ref, recv_ref in zip(starts[1:], keep_refs[1:], recv_refs[1:]):
            keep = jnp.where(step >= start, keep_ref[0], keep)
            recv = jnp.where(step >= start, recv_ref[0], recv)
        folded = side * (keep - recv) if parity else keep + recv
        high, low = split_two(folded)
        for member in range(2):
            part = slice(member * width, (member + 1) * width)
            field_ref[member, :main] = high[:main, part]
            field_ref[member, main : 2 * main] = low[:main, part]
            field_ref[member, 2 * main : 3 * main] = high[:main, part]
            for k, value in enumerate((high, low, high)):
                at = 3 * main + k * tail
                field_ref[member, at : at + tail] = value[main:, part]
            field_ref[member, 3 * main + 3 * tail :] = jnp.zeros((main - 3 * tail, width), BF16)
        count = lax.shift_right_logical(NDEG - first_m - parity + 1, 1)

        def product(member, begin, end):
            table = table_ref[0, parity, begin:end].reshape((end - begin) * padded, table_ref.shape[4])
            table = jnp.concatenate([table[:, :main], table], 1)
            result_ref[member, begin:end] = dot_nn(table, field_ref[member]).reshape(end - begin, padded, width)

        product(0, 0, middle)
        product(1, middle, shares)
        pl.when(count > middle * share)(lambda: product(0, middle, shares))
        pl.when(count < middle * share)(lambda: product(1, middle - 1, middle))

        for local in range(ups):

            @pl.when(lax.rem(step, ups) == local)
            def _():
                begin = (2 * local + parity) * share
                rows = slice(begin, begin + share)
                outs = [mine_ref.at[spot] for spot in range(4)] + [ref.at[i] for ref in cross_refs for i in range(ref.shape[0])]
                for i, out_ref in enumerate(outs):
                    which = 2 * owner_of(i % 4, step, ups, chip, chips) + (core if i < 4 else 1 - core)
                    slot = which * share + lax.broadcasted_iota(jnp.int32, (padded, width), 0)
                    valid = parity + 2 * (slot - count) <= first_m
                    value = jnp.where(slot < count, result_ref[0, which], jnp.where(valid, result_ref[1, which], 0.0))
                    out_ref[rows, :] = value[:share]


def project(place, wave, keeps, recvs, table, share, first, messages):
    half, width = recvs[0].shape[1:]
    shares, padded, depth = table.shape[2:]
    sizes = [recv.shape[0] for recv in recvs]
    starts = [sum(sizes[:i]) for i in range(len(recvs))]
    ups = sum(sizes) // 2
    rows = run_rows(ups, share)

    def field(start, size):
        return pl.BlockSpec((1, half, width), lambda step, *_: (jnp.clip(step - start, 0, size - 1), 0, 0))

    fields = [field(start, size) for start, size in zip(starts, sizes)]
    counts = (shares // 2, *messages)
    return pl.pallas_call(
        functools.partial(project_kernel, share=share, first=first, starts=starts, ups=ups),
        grid_spec=pltpu.PrefetchScalarGridSpec(
            num_scalar_prefetch=2,
            grid=(2 * ups,),
            in_specs=[
                *fields,
                *fields,
                pl.BlockSpec((1,) + table.shape[1:], lambda step, *_: (first + step, 0, 0, 0, 0)),
            ],
            out_specs=[pl.BlockSpec((count, rows, width // 2), lambda step, *_: (0, step // ups, 0)) for count in counts],
            scratch_shapes=[
                pltpu.VMEM((2, 512, width // 2), BF16),
                pltpu.VMEM((2, shares, padded, width // 2), F32),
            ],
        ),
        out_shape=[jax.ShapeDtypeStruct((count, 2 * rows, width // 2), F32) for count in counts],
        compiler_params=pltpu.CompilerParams(vmem_limit_bytes=VMEM_LIMIT),
        cost_estimate=pl.CostEstimate(flops=10**12, bytes_accessed=10**10, transcendentals=0),
        name="project",
    )(place, wave, *keeps, *recvs, table)


def run_rows(ups, share):
    return (2 * ups * share + 7) // 8 * 8


def energy_kernel(
    place_ref, wave_ref, mine_ref, cross_ref, far_up_ref, far_down_ref, near_up_ref, near_down_ref, so_far_ref, out_ref,
    *, share, first, ways,
):
    low = far_up_ref.shape[0]
    lanes = out_ref.shape[1]
    halves = []
    for rows, far_ref, near_ref in (
        (slice(None, low), far_up_ref, near_down_ref),
        (slice(low, None), far_down_ref, near_up_ref),
    ):
        value = (mine_ref[0, rows, :] + cross_ref[0, rows, :]) + (far_ref[...] + near_ref[rows, :])
        squares = value * value
        halves.append(squares[:, :lanes] + squares[:, lanes:])
    squares = jnp.concatenate(halves, 0)
    ones = jnp.ones((8, lanes), BF16)
    squares = sum(dot_nt(ones, piece) for piece in split_three(squares))[:1]

    size = squares.shape[1]
    column = lax.broadcasted_iota(jnp.int32, (1, size), 1)
    start = (2 * place_ref[1] + place_ref[0]) * share
    first_m = jnp.zeros((1, size), jnp.int32)
    parity = jnp.zeros((1, size), jnp.int32)
    slot = jnp.full((1, size), -1, jnp.int32)
    for pair, at in enumerate(ways):
        for s in range(2):
            begin = at + s * share
            inside = (column >= begin) & (column < begin + share)
            first_m = jnp.where(inside, wave_ref[first + pair], first_m)
            parity = jnp.where(inside, s, parity)
            slot = jnp.where(inside, column - begin + start, slot)
    count = lax.shift_right_logical(NDEG - first_m - parity + 1, 1)
    leading = slot < count
    second_m = NDEG - 1 - first_m
    degree = jnp.where(leading, first_m + parity + 2 * slot, second_m + parity + 2 * (slot - count))
    owner_m = jnp.where(leading, first_m, second_m)
    usable = (slot >= 0) & (degree >= 1) & (degree <= NDEG - 1)
    safe = jnp.maximum(degree, 1).astype(F32)
    factor = jnp.where(owner_m == 0, 1.0, 2.0)
    term = jnp.where(usable, factor * squares / (4.0 * safe * (safe + 1.0)), 0.0)
    spot = jnp.where(usable, degree - 1, 0)
    band = lax.broadcasted_iota(jnp.int32, (out_ref.shape[0], size), 0)
    left = jnp.where(lax.shift_right_logical(spot, 7) == band, term, 0.0)
    line = lax.broadcasted_iota(jnp.int32, (lanes, size), 0)
    right = jnp.where((spot & (lanes - 1)) == line, 1.0, 0.0).astype(BF16)
    out_ref[...] = so_far_ref[...] + sum(dot_nt(piece, right) for piece in split_three(left))


def run_energy(place, wave, parts, so_far, share, first, ways):
    _, rows, width = parts[0].shape
    return pl.pallas_call(
        functools.partial(energy_kernel, share=share, first=first, ways=ways),
        grid_spec=pltpu.PrefetchScalarGridSpec(
            num_scalar_prefetch=2,
            grid=(1,),
            in_specs=own_parts(parts) + [pl.BlockSpec(so_far.shape, lambda step, *_: (0, 0))],
            out_specs=pl.BlockSpec(so_far.shape, lambda step, *_: (0, 0)),
        ),
        out_shape=jax.ShapeDtypeStruct(so_far.shape, F32),
        compiler_params=pltpu.CompilerParams(vmem_limit_bytes=VMEM_SMALL),
        cost_estimate=pl.CostEstimate(flops=10 * rows * width, bytes_accessed=4 * rows * width * 4, transcendentals=0),
        name="run_energy",
    )(place, wave, *parts, so_far)


def own_parts(parts):
    _, rows, width = parts[0].shape
    return [
        pl.BlockSpec((1, rows, width), lambda step, *_: (parts[0].shape[0] - 1, 0, 0)),
        pl.BlockSpec((1, rows, width), lambda step, *_: (parts[1].shape[0] - 1, 0, 0)),
    ] + [pl.BlockSpec(part.shape, lambda step, *_: (0, 0)) for part in parts[2:]]


def place_kernel(mine_ref, cross_ref, far_up_ref, far_down_ref, near_up_ref, near_down_ref, *refs, share, ways):
    out_ref = refs[-1]
    low = far_up_ref.shape[0]
    for pair, at in enumerate(ways):
        for parity in range(2):
            begin = at + parity * share
            rows = slice(begin, begin + share)
            if begin < low:
                arrived = far_up_ref[rows, :] + near_down_ref[rows, :]
            else:
                arrived = far_down_ref[begin - low : begin - low + share, :] + near_up_ref[rows, :]
            value = ((mine_ref[0, rows, :] + cross_ref[0, rows, :]) + arrived).T
            out_ref[pair, parity] = value.reshape(out_ref.shape[2:])


def place_run(parts, held, shape, share, first, ways):
    each = len(ways)
    _, rows, width = parts[0].shape
    return pl.pallas_call(
        functools.partial(place_kernel, share=share, ways=ways),
        grid=(1,),
        in_specs=own_parts(parts) + [pl.BlockSpec(memory_space=pl.ANY)] * len(held),
        out_specs=pl.BlockSpec((each,) + shape[1:], lambda step: (first // each, 0, 0, 0, 0)),
        out_shape=jax.ShapeDtypeStruct(shape, F32),
        input_output_aliases={len(parts): 0} if held else {},
        compiler_params=pltpu.CompilerParams(vmem_limit_bytes=VMEM_SMALL),
        cost_estimate=pl.CostEstimate(flops=4 * rows * width, bytes_accessed=5 * rows * width * 4, transcendentals=0),
        name="place_run",
    )(*parts, *held)


def all_sum(x):
    for axis, bit in (("band", 1), ("band", 2), ("band", 4), ("wave", 1), ("lev", 1), ("wave", 2), ("wave", 4)):
        size = lax.axis_size(axis)
        x = x + lax.ppermute(x, axis, [(i, i ^ bit) for i in range(size)])
    return x


def shards(fourier, legendre, pair_m, mirror):
    bands = lax.axis_size("band")
    chips = bands // 2
    rows, pairs, members, comps, levs = fourier.shape
    half_rows = rows // 2
    slots = legendre.shape[3]
    share = slots // bands
    padded = (share + 15) // 16 * 16
    position = lax.axis_index("band")
    chip, core = position // 2, position % 2
    place = jnp.stack([core, chip, jnp.int32(chips)]).astype(jnp.int32)

    north_base = position % chips * rows
    south_base = north_base + chips * rows
    partner = lax.dynamic_slice(mirror, (north_base,), (rows,)) - south_base
    plain = (jnp.arange(rows, dtype=jnp.int32) + half_rows) % rows
    index = jnp.where(position < chips, plain, partner).reshape(rows, 1)
    field = jnp.transpose(fourier, (1, 2, 3, 4, 0)).reshape(pairs, members * comps * levs, rows)

    kept, received = [], []
    for i, each in enumerate(MESSAGES):
        message, keep = pick_rows(index, field, sum(MESSAGES[:i]), each)
        kept.append(keep)
        received.append(send_along(message, chips // 2, 0))
        index, legendre, message = lax.optimization_barrier((index, legendre, message))

    table = lay_out(legendre, share, padded)

    firsts = [sum(MESSAGES[: run[0]]) for run in RUNS]
    ways = []
    mine, cross, near, far = {}, {}, {}, {}
    for run in RUNS:
        ups = sum(MESSAGES[i] for i in run) // 2
        ways.append([half * run_rows(ups, share) + 2 * i * share for half in range(2) for i in range(ups)])

    def begin(run, messages, after):
        mine[run], *others = project(
            place, pair_m, [kept[i] for i in RUNS[run]], behind([received[i] for i in RUNS[run]], after), table, share,
            firsts[run], messages,
        )
        cross[run] = [send_along(other, 0, 1) for other in others]

    def send_early(run, after):
        totals = [mine[run][spot] + other[0] for spot, other in enumerate(behind(cross[run][:2], after))]
        near[run] = [send_along(totals[0], 1, 0), send_along(totals[1], -1, 0)]
        return totals

    def send_late(run):
        total, other = mine[run][2], cross[run][2][0]
        low = total.shape[0] // 2
        totals = [
            total[:low] + other[:low] + near[run][0][:low],
            total[low:] + other[low:] + near[run][1][low:],
        ]
        far[run] = [send_along(totals[0], 1, 0), send_along(totals[1], -1, 0)]
        return totals

    begin(0, (1, 1, 1, 1), ())
    begin(1, (1, 1, 2), [send_early(0, ()), cross[0][2:]])
    send_early(1, near[0])
    send_late(0)
    send_late(1)
    shape = (pairs, 2, comps, levs, share)
    held = []
    total = jnp.zeros((16, 128), F32)
    for run in range(len(RUNS)):
        parts = [mine[run], cross[run][-1]] + far[run] + near[run]
        total = run_energy(place, pair_m, parts, behind(total, held), share, firsts[run], ways[run])
        held = [place_run(parts, held, shape, share, firsts[run], ways[run])]
    total = all_sum(total)
    return (held[0], jnp.log(total.reshape(-1)[: NDEG - 1]))


def solution(mesh):
    return jax.shard_map(
        shards,
        mesh=mesh,
        in_specs=(
            P("band", "wave", None, None, "lev"),
            P("wave", "band", None, None),
            P("wave"),
            P(),
        ),
        out_specs=(P("wave", None, None, "lev", "band"), P()),
        check_vma=False,
    )
```

time: 200 us -> 198 us (0.990)
  Pallas kernels: 72.4 us -> 69 us
    pallas_call x2, Pallas kernels: 32.9 us -> 28.6 us  [project(): pl.pallas_call(functools.partial(project_kernel, share=share, first=first...]
    ppermute x18, waiting for transfers between devices: 65.7 us -> 69 us  [send_along(): return lax.ppermute(x, 'band', pairs)]
    add x3 -> x2, other arithmetic: 3.29 us -> 4.86 us  [send_early(): mine[run][spot] + other[0]]
    pallas_call x2 -> x4, Pallas kernels: 8.11 us -> 9.07 us  [the longest x2 4.83 us: place_run(): pl.pallas_call(functools.partial(place_kernel, share=share, ways=ways), g...]
where the time goes in v4:
time: 198 us; the launch traced here: 197 us
  waiting for transfers between devices  84.9 us (43%)
  Pallas kernels  69 us (35%)
  starting transfers between devices  30.6 us (15%)
  other arithmetic  7.45 us (4%)
  local copies, waits for them, and re-layouts  3.79 us (2%)
    ppermute x18, waiting for transfers between devices, send_along(): return lax.ppermute(x, 'band', pairs)  69 us
    pallas_call x2, Pallas kernels, project(): pl.pallas_call(functools.partial(project_kernel, share=share, first=first...  28.6 us
    ppermute x18, starting transfers between devices, send_along(): return lax.ppermute(x, 'band', pairs)  20.2 us
    pallas_call x1, Pallas kernels, lay_out(): pl.pallas_call(functools.partial(layout_kernel, share=share), grid=(pairs...  17.1 us
    ppermute x7, waiting for transfers between devices, all_sum(): x = x + lax.ppermute(x, axis, [(i, i ^ bit) for i in range(size)])  16 us
    pallas_call x3, Pallas kernels, pick_rows(): pl.pallas_call(pick_kernel, grid=(each,), in_specs=[pl.BlockSpec((count,...  14.3 us
    ppermute x7, starting transfers between devices, all_sum(): x = x + lax.ppermute(x, axis, [(i, i ^ bit) for i in range(size)])  10.4 us
    add x2, other arithmetic, send_early(): mine[run][spot] + other[0]  4.86 us
  transfers between devices with their start and end apart: 25, of which 18 were waited for; matrix products, arithmetic and copies ran while one was open for 4% of the time, Pallas kernels for 33%

profile of v4, /device:TPU:0, one launch (start us, length us, event | category | flops | bytes accessed | tf_op | source)
XLA Modules:
  0.0 196.6 jit_solution(7204166787531155877)
XLA Ops:
  0.7 0.8 fusion.4
  1.6 2.9 %pick_rows.3 = (f32[2,160,512]{2,1,0:T(8,128)}, f32[2,160,512]{2,1,0:T(8,128)S(1)}) custom-call(s32[320,1]{1,0:T(8,128)S(1)} %copy.7.index_ref, f32[12,512,320]{2,1,0:T(8,128)} %bitcast.31), custom_call_target="tpu_custom_call" | custom-call | flops 999999995904 | bytes 10000000000 | tf_op jit(solution)/shard_map/pick_rows/pallas_call | solution.py:77
  4.5 3.3 %collective-permute-start.1 = (f32[2,160,512]{2,1,0:T(8,128)}, f32[2,160,512]{2,1,0:T(8,128)}, u32[]{:S(2)}, u32[]{:S(2)}) collective-permute-start(f32[2,160,512]{2,1,0:T(8,128)} %get-tuple-element.30), channel_id=1, source_target_pairs={{0,64},{16,80},{32,96},{48,112},{64,0},{80,16},{96,32},{112,48},{1... | collective-permute-start | bytes 1966088 | tf_op jit(solution)/shard_map/ppermute | solution.py:48
  7.8 0.8 copy.8.index_ref
  8.6 4.8 %pick_rows.4 = (f32[4,160,512]{2,1,0:T(8,128)}, f32[4,160,512]{2,1,0:T(8,128)S(1)}) custom-call(s32[320,1]{1,0:T(8,128)S(1)} %copy.8.index_ref, f32[12,512,320]{2,1,0:T(8,128)} %bitcast.32), custom_call_target="tpu_custom_call" | custom-call | flops 999999995904 | bytes 10000000000 | tf_op jit(solution)/shard_map/pick_rows/pallas_call | solution.py:77
  13.5 1.1 copy-done.5
  14.5 0.3 collective-permute-start.2
  14.9 6.5 %pick_rows.5 = (f32[6,160,512]{2,1,0:T(8,128)}, f32[6,160,512]{2,1,0:T(8,128)S(1)}) custom-call(s32[320,1]{1,0:T(8,128)S(1)} %copy.9.index_ref, f32[12,512,320]{2,1,0:T(8,128)} %bitcast.33), custom_call_target="tpu_custom_call" | custom-call | flops 999999995904 | bytes 10000000000 | tf_op jit(solution)/shard_map/pick_rows/pallas_call | solution.py:77
  21.4 3.3 %collective-permute-start = (f32[6,160,512]{2,1,0:T(8,128)}, f32[6,160,512]{2,1,0:T(8,128)}, u32[]{:S(2)}, u32[]{:S(2)}) collective-permute-start(f32[6,160,512]{2,1,0:T(8,128)} %get-tuple-element.36), channel_id=1, source_target_pairs={{0,64},{16,80},{32,96},{48,112},{64,0},{80,16},{96,32},{112,48},{1... | collective-permute-start | bytes 5898248 | tf_op jit(solution)/shard_map/ppermute | solution.py:48
  24.7 17.1 %lay_out.1.refs_4_.refs_2_ = bf16[12,2,8,96,384]{4,3,2,1,0:T(8,128)(2,1)} custom-call(f32[12,160,2,648]{3,2,1,0:T(2,128)} %refs_5_, f32[12,160,2,648]{3,2,1,0:T(2,128)} %refs_5_, f32[12,160,2,648]{3,2,1,0:T(2,128)} %refs_5_, f32[12,160,2,648]{3,2,1,0:T(2,128)} %refs_5_, f32[12,160,2,648]{3,2,1,0:T(2,128)} %refs_5_, f32[12,160,2,648]{3,2,1,0:T(2,128)} %refs_5_), custom_call_target="tpu_custom_call" | custom-call | flops 999999995904 | bytes 10000000000 | tf_op jit(solution)/shard_map/lay_out/pallas_call | solution.py:125
  41.9 10.2 %collective-permute-done.2.refs_3_ = f32[4,160,512]{2,1,0:T(8,128)} collective-permute-done((f32[4,160,512]{2,1,0:T(8,128)}, f32[4,160,512]{2,1,0:T(8,128)}, u32[]{:S(2)}, u32[]{:S(2)}) %collective-permute-start.2) | collective-permute-done | bytes 1310752 | tf_op jit(solution)/shard_map/ppermute | solution.py:48
  52.1 14.2 %project.2 = (f32[4,976,256]{2,1,0:T(8,128)}, f32[1,976,256]{2,1,0:T(8,128)S(1)}, f32[1,976,256]{2,1,0:T(8,128)S(1)}, f32[1,976,256]{2,1,0:T(8,128)S(1)}, f32[1,976,256]{2,1,0:T(8,128)S(1)}) custom-call(s32[3]{0:T(128)S(1)} %pad_add_fusion.place_ref, s32[12]{0:T(128)S(1)} %copy-done.4, f32[2,160,512]{2,1,0:T(8,128)S(1)} %get-tuple-element.37.refs_0_, ...), custom_call_target="tpu_custom_call" | custom-call | flops 999999995904 | bytes 10000000000 | tf_op jit(solution)/shard_map/project/pallas_call | solution.py:215
  66.3 0.5 collective-permute-start.4
  66.8 0.5 collective-permute-start.6
  67.3 1.6 collective-permute-done.3
  68.9 1.4 collective-permute-done.4
  70.3 3.1 %add_bitcast_fusion.2 = (f32[976,256]{1,0:T(8,128)}, f32[976,256]{1,0:T(8,128)}) fusion(f32[1,976,256]{2,1,0:T(8,128)S(1)} %collective-permute-done.4, f32[4,976,256]{2,1,0:T(8,128)} %get-tuple-element.43.mine_ref, f32[1,976,256]{2,1,0:T(8,128)S(1)} %collective-permute-done.3), kind=kLoop, calls=%fused_computation.2 | loop fusion | flops 499712 | bytes 5996544 | tf_op jit(solution)/shard_map/add | solution.py:396
  73.4 3.1 %collective-permute-start.11 = (f32[976,256]{1,0:T(8,128)}, f32[976,256]{1,0:T(8,128)}, u32[]{:S(2)}, u32[]{:S(2)}) collective-permute-start(f32[976,256]{1,0:T(8,128)} %get-tuple-element.64), channel_id=1, source_target_pairs={{0,96},{16,112},{32,0},{48,16},{64,32},{80,48},{96,64},{112,80},{1... | collective-permute-start | bytes 2998280 | tf_op jit(solution)/shard_map/ppermute | solution.py:48
  76.5 17.7 %collective-permute-done.refs_1_ = f32[6,160,512]{2,1,0:T(8,128)} collective-permute-done((f32[6,160,512]{2,1,0:T(8,128)}, f32[6,160,512]{2,1,0:T(8,128)}, u32[]{:S(2)}, u32[]{:S(2)}) %collective-permute-start) | collective-permute-done | bytes 1966112 | tf_op jit(solution)/shard_map/ppermute | solution.py:48
  94.3 1.0 copy-done.2
  95.3 14.3 %project.3 = (f32[4,976,256]{2,1,0:T(8,128)}, f32[1,976,256]{2,1,0:T(8,128)S(1)}, f32[1,976,256]{2,1,0:T(8,128)S(1)}, f32[2,976,256]{2,1,0:T(8,128)}) custom-call(s32[3]{0:T(128)S(1)} %pad_add_fusion.place_ref, s32[12]{0:T(128)S(1)} %copy-done.4, f32[6,160,512]{2,1,0:T(8,128)S(1)} %get-tuple-element.35.refs_0_, f32[6,160,512]{2,1,0:T(8,128)} %collective-permute-done.refs_1_, ...), custom_call_target="tpu_custom_call" | custom-call | flops 999999995904 | bytes 10000000000 | tf_op jit(solution)/shard_map/project/pallas_call | solution.py:215
  109.7 0.5 collective-permute-start.9
  110.3 4.6 %collective-permute-done.11.near_down_ref = f32[976,256]{1,0:T(8,128)} collective-permute-done((f32[976,256]{1,0:T(8,128)}, f32[976,256]{1,0:T(8,128)}, u32[]{:S(2)}, u32[]{:S(2)}) %collective-permute-start.11) | collective-permute-done | bytes 999456 | tf_op jit(solution)/shard_map/ppermute | solution.py:48
  115.2 1.8 add_bitcast_fusion
  116.9 3.2 %collective-permute-start.14 = (f32[976,256]{1,0:T(8,128)S(1)}, f32[976,256]{1,0:T(8,128)S(1)}, u32[]{:S(2)}, u32[]{:S(2)}) collective-permute-start(f32[976,256]{1,0:T(8,128)S(1)} %get-tuple-element.62), channel_id=1, source_target_pairs={{0,96},{16,112},{32,0},{48,16},{64,32},{80,48},{96,64},{112,80},{1... | collective-permute-start | bytes 2998280 | tf_op jit(solution)/shard_map/ppermute | solution.py:48
  120.1 1.5 slice_add_fusion
  121.6 3.4 %collective-permute-start.17 = (f32[488,256]{1,0:T(8,128)S(1)}, f32[488,256]{1,0:T(8,128)S(1)}, u32[]{:S(2)}, u32[]{:S(2)}) collective-permute-start(f32[488,256]{1,0:T(8,128)S(1)} %get-tuple-element.60), channel_id=1, source_target_pairs={{0,96},{16,112},{32,0},{48,16},{64,32},{80,48},{96,64},{112,80},{1... | collective-permute-start | bytes 1499144 | tf_op jit(solution)/shard_map/ppermute | solution.py:48
  125.0 17.5 %collective-permute-done.14.near_down_ref = f32[976,256]{1,0:T(8,128)S(1)} collective-permute-done((f32[976,256]{1,0:T(8,128)S(1)}, f32[976,256]{1,0:T(8,128)S(1)}, u32[]{:S(2)}, u32[]{:S(2)}) %collective-permute-start.14) | collective-permute-done | bytes 999456 | tf_op jit(solution)/shard_map/ppermute | solution.py:48
  142.6 3.7 %collective-permute-done.12.near_up_ref = f32[976,256]{1,0:T(8,128)S(1)} collective-permute-done((f32[976,256]{1,0:T(8,128)S(1)}, f32[976,256]{1,0:T(8,128)S(1)}, u32[]{:S(2)}, u32[]{:S(2)}) %collective-permute-start.12) | collective-permute-done | bytes 999456 | tf_op jit(solution)/shard_map/ppermute | solution.py:48
  146.6 2.0 %collective-permute-start.13 = (f32[488,256]{1,0:T(8,128)S(1)}, f32[488,256]{1,0:T(8,128)S(1)}, u32[]{:S(2)}, u32[]{:S(2)}) collective-permute-start(f32[488,256]{1,0:T(8,128)S(1)} %get-tuple-element.59), channel_id=1, source_target_pairs={{0,32},{16,48},{32,64},{48,80},{64,96},{80,112},{96,0},{112,16},{1... | collective-permute-start | bytes 1499144 | tf_op jit(solution)/shard_map/ppermute | solution.py:48
  148.6 4.7 %collective-permute-done.17.far_down_ref = f32[488,256]{1,0:T(8,128)S(1)} collective-permute-done((f32[488,256]{1,0:T(8,128)S(1)}, f32[488,256]{1,0:T(8,128)S(1)}, u32[]{:S(2)}, u32[]{:S(2)}) %collective-permute-start.17) | collective-permute-done | bytes 499744 | tf_op jit(solution)/shard_map/ppermute | solution.py:48
  153.3 3.7 %collective-permute-done.16.far_up_ref = f32[488,256]{1,0:T(8,128)S(1)} collective-permute-done((f32[488,256]{1,0:T(8,128)S(1)}, f32[488,256]{1,0:T(8,128)S(1)}, u32[]{:S(2)}, u32[]{:S(2)}) %collective-permute-start.16) | collective-permute-done | bytes 499744 | tf_op jit(solution)/shard_map/ppermute | solution.py:48
  157.0 3.2 %place_run.2.refs_0_ = f32[12,2,4,64,81]{4,3,2,1,0:T(8,128)} custom-call(f32[4,976,256]{2,1,0:T(8,128)S(1)} %copy-done.1, f32[1,976,256]{2,1,0:T(8,128)S(1)} %copy-done.3, f32[488,256]{1,0:T(8,128)S(1)} %collective-permute-done.16.far_up_ref, f32[488,256]{1,0:T(8,128)S(1)} %collective-permute-done.17.far_down_ref, ...), custom_call_target="tpu_custom_call" | custom-call | flops 999424 | bytes 4997120 | tf_op jit(solution)/shard_map/place_run/pallas_call | solution.py:333
  160.2 2.9 %run_energy.2.so_far_ref = f32[16,128]{1,0:T(8,128)S(1)} custom-call(s32[3]{0:T(128)S(1)} %pad_add_fusion.place_ref, s32[12]{0:T(128)S(1)} %copy-done.4, f32[4,976,256]{2,1,0:T(8,128)S(1)} %copy-done.1, f32[1,976,256]{2,1,0:T(8,128)S(1)} %copy-done.3, f32[488,256]{1,0:T(8,128)S(1)} %collective-permute-done.16.far_up_ref, ...), custom_call_target="tpu_custom_call" | custom-call | flops 2498560 | bytes 3997696 | tf_op jit(solution)/shard_map/run_energy/pallas_call | solution.py:292
  163.2 3.4 %collective-permute-done.13.far_up_ref = f32[488,256]{1,0:T(8,128)S(1)} collective-permute-done((f32[488,256]{1,0:T(8,128)S(1)}, f32[488,256]{1,0:T(8,128)S(1)}, u32[]{:S(2)}, u32[]{:S(2)}) %collective-permute-start.13) | collective-permute-done | bytes 499744 | tf_op jit(solution)/shard_map/ppermute | solution.py:48
  166.6 1.4 run_energy.3
  168.0 1.2 collective-permute-done.18
  169.2 3.6 %collective-permute-done.19 = f32[16,128]{1,0:T(8,128)S(1)} collective-permute-done((f32[16,128]{1,0:T(8,128)S(1)}, f32[16,128]{1,0:T(8,128)S(1)}, u32[]{:S(2)}, u32[]{:S(2)}) %collective-permute-start.19) | collective-permute-done | bytes 8224 | tf_op jit(solution)/shard_map/ppermute | solution.py:349
  172.9 5.2 %collective-permute-done.20 = f32[16,128]{1,0:T(8,128)S(1)} collective-permute-done((f32[16,128]{1,0:T(8,128)S(1)}, f32[16,128]{1,0:T(8,128)S(1)}, u32[]{:S(2)}, u32[]{:S(2)}) %collective-permute-start.20) | collective-permute-done | bytes 8224 | tf_op jit(solution)/shard_map/ppermute | solution.py:349
  178.0 1.5 collective-permute-start.21
  179.5 2.2 %collective-permute-done.21 = f32[16,128]{1,0:T(8,128)S(1)} collective-permute-done((f32[16,128]{1,0:T(8,128)S(1)}, f32[16,128]{1,0:T(8,128)S(1)}, u32[]{:S(2)}, u32[]{:S(2)}) %collective-permute-start.21) | collective-permute-done | bytes 8224 | tf_op jit(solution)/shard_map/ppermute | solution.py:349
  181.7 3.1 %collective-permute-start.22 = (f32[16,128]{1,0:T(8,128)S(1)}, f32[16,128]{1,0:T(8,128)S(1)}, u32[]{:S(2)}, u32[]{:S(2)}) collective-permute-start(f32[16,128]{1,0:T(8,128)S(1)} %add.137), channel_id=1, source_target_pairs={{0,1},{1,0},{2,3},{3,2},{4,5},{5,4},{6,7},{7,6},{8,9},{9,8},{10,11... | collective-permute-start | bytes 24584 | tf_op jit(solution)/shard_map/ppermute | solution.py:349
  184.8 2.1 %collective-permute-done.22 = f32[16,128]{1,0:T(8,128)S(1)} collective-permute-done((f32[16,128]{1,0:T(8,128)S(1)}, f32[16,128]{1,0:T(8,128)S(1)}, u32[]{:S(2)}, u32[]{:S(2)}) %collective-permute-start.22) | collective-permute-done | bytes 8224 | tf_op jit(solution)/shard_map/ppermute | solution.py:349
  186.8 1.9 collective-permute-start.23
  188.7 1.8 collective-permute-done.23
  190.6 3.8 %collective-permute-start.24 = (f32[16,128]{1,0:T(8,128)S(1)}, f32[16,128]{1,0:T(8,128)S(1)}, u32[]{:S(2)}, u32[]{:S(2)}) collective-permute-start(f32[16,128]{1,0:T(8,128)S(1)} %add.139), channel_id=1, source_target_pairs={{0,8},{2,10},{4,12},{6,14},{8,0},{10,2},{12,4},{14,6},{1,9},{3,11}... | collective-permute-start | bytes 24584 | tf_op jit(solution)/shard_map/ppermute | solution.py:349
  194.3 1.7 place_run.3
  196.0 0.6 slice_log_fusion
  (51 shorter events, 1.3 us)
Async XLA Ops:
  1.4 3.1 %copy-start.8 = (s32[320,1]{0,1:T(1,128)}, s32[320,1]{0,1:T(1,128)S(1)}, u32[]{:S(2)}) copy-start(s32[320,1]{0,1:T(1,128)S(1)} %reshape.29) | copy-start | bytes 3844
  4.5 37.4 %collective-permute-start.1 = (f32[2,160,512]{2,1,0:T(8,128)}, f32[2,160,512]{2,1,0:T(8,128)}, u32[]{:S(2)}, u32[]{:S(2)}) collective-permute-start(f32[2,160,512]{2,1,0:T(8,128)} %get-tuple-element.30), channel_id=1, source_target_pairs={{0,64},{16,80},{32,96},{48,112},{64,0},{80,16},{96,32},{112,48},{1... | collective-permute-start | bytes 1966088 | tf_op jit(solution)/shard_map/ppermute | solution.py:48
  8.6 6.1 %copy-start.9 = (s32[320,1]{0,1:T(1,128)S(1)}, s32[320,1]{0,1:T(1,128)}, u32[]{:S(2)}) copy-start(s32[320,1]{0,1:T(1,128)} %copy-done.8) | copy-start | bytes 3844
  13.4 1.1 copy-start.5
  14.5 37.5 %collective-permute-start.2 = (f32[4,160,512]{2,1,0:T(8,128)}, f32[4,160,512]{2,1,0:T(8,128)}, u32[]{:S(2)}, u32[]{:S(2)}) collective-permute-start(f32[4,160,512]{2,1,0:T(8,128)} %get-tuple-element.33), channel_id=1, source_target_pairs={{0,64},{16,80},{32,96},{48,112},{64,0},{80,16},{96,32},{112,48},{1... | collective-permute-start | bytes 3932168 | tf_op jit(solution)/shard_map/ppermute | solution.py:48
  21.4 72.8 %collective-permute-start = (f32[6,160,512]{2,1,0:T(8,128)}, f32[6,160,512]{2,1,0:T(8,128)}, u32[]{:S(2)}, u32[]{:S(2)}) collective-permute-start(f32[6,160,512]{2,1,0:T(8,128)} %get-tuple-element.36), channel_id=1, source_target_pairs={{0,64},{16,80},{32,96},{48,112},{64,0},{80,16},{96,32},{112,48},{1... | collective-permute-start | bytes 5898248 | tf_op jit(solution)/shard_map/ppermute | solution.py:48
  24.7 27.3 %copy-start.4 = (s32[12]{0:T(128)S(1)}, s32[12]{0:T(128)}, u32[]{:S(2)}) copy-start(s32[12]{0:T(128)} %wave_ref.7) | copy-start | bytes 148
  66.3 2.6 %collective-permute-start.3 = (f32[1,976,256]{2,1,0:T(8,128)S(1)}, f32[1,976,256]{2,1,0:T(8,128)S(1)}, u32[]{:S(2)}, u32[]{:S(2)}) collective-permute-start(f32[1,976,256]{2,1,0:T(8,128)S(1)} %get-tuple-element.44), channel_id=1, source_target_pairs={{0,16},{16,0},{32,48},{48,32},{64,80},{80,64},{96,112},{112,96},{1... | collective-permute-start | bytes 2998280 | tf_op jit(solution)/shard_map/ppermute | solution.py:48
  66.3 4.0 %collective-permute-start.4 = (f32[1,976,256]{2,1,0:T(8,128)S(1)}, f32[1,976,256]{2,1,0:T(8,128)S(1)}, u32[]{:S(2)}, u32[]{:S(2)}) collective-permute-start(f32[1,976,256]{2,1,0:T(8,128)S(1)} %get-tuple-element.45), channel_id=1, source_target_pairs={{0,16},{16,0},{32,48},{48,32},{64,80},{80,64},{96,112},{112,96},{1... | collective-permute-start | bytes 2998280 | tf_op jit(solution)/shard_map/ppermute | solution.py:48
  66.8 27.4 %collective-permute-start.5 = (f32[1,976,256]{2,1,0:T(8,128)S(1)}, f32[1,976,256]{2,1,0:T(8,128)S(1)}, u32[]{:S(2)}, u32[]{:S(2)}) collective-permute-start(f32[1,976,256]{2,1,0:T(8,128)S(1)} %get-tuple-element.48), channel_id=1, source_target_pairs={{0,16},{16,0},{32,48},{48,32},{64,80},{80,64},{96,112},{112,96},{1... | collective-permute-start | bytes 2998280 | tf_op jit(solution)/shard_map/ppermute | solution.py:48
  66.8 27.4 %collective-permute-start.6 = (f32[1,976,256]{2,1,0:T(8,128)S(1)}, f32[1,976,256]{2,1,0:T(8,128)S(1)}, u32[]{:S(2)}, u32[]{:S(2)}) collective-permute-start(f32[1,976,256]{2,1,0:T(8,128)S(1)} %get-tuple-element.49), channel_id=1, source_target_pairs={{0,16},{16,0},{32,48},{48,32},{64,80},{80,64},{96,112},{112,96},{1... | collective-permute-start | bytes 2998280 | tf_op jit(solution)/shard_map/ppermute | solution.py:48
  73.4 41.5 %collective-permute-start.11 = (f32[976,256]{1,0:T(8,128)}, f32[976,256]{1,0:T(8,128)}, u32[]{:S(2)}, u32[]{:S(2)}) collective-permute-start(f32[976,256]{1,0:T(8,128)} %get-tuple-element.64), channel_id=1, source_target_pairs={{0,96},{16,112},{32,0},{48,16},{64,32},{80,48},{96,64},{112,80},{1... | collective-permute-start | bytes 2998280 | tf_op jit(solution)/shard_map/ppermute | solution.py:48
  76.5 38.4 %collective-permute-start.10 = (f32[976,256]{1,0:T(8,128)}, f32[976,256]{1,0:T(8,128)}, u32[]{:S(2)}, u32[]{:S(2)}) collective-permute-start(f32[976,256]{1,0:T(8,128)} %get-tuple-element.65), channel_id=1, source_target_pairs={{0,32},{16,48},{32,64},{48,80},{64,96},{80,112},{96,0},{112,16},{1... | collective-permute-start | bytes 2998280 | tf_op jit(solution)/shard_map/ppermute | solution.py:48
  94.2 15.4 %copy-start.6 = (f32[1,976,256]{2,1,0:T(8,128)}, f32[1,976,256]{2,1,0:T(8,128)S(1)}, u32[]{:S(2)}) copy-start(f32[1,976,256]{2,1,0:T(8,128)S(1)} %collective-permute-done.5) | copy-start | bytes 2998276
  94.2 1.0 copy-start.2
  109.6 10.5 %copy-start.1 = (f32[4,976,256]{2,1,0:T(8,128)S(1)}, f32[4,976,256]{2,1,0:T(8,128)}, u32[]{:S(2)}) copy-start(f32[4,976,256]{2,1,0:T(8,128)} %get-tuple-element.43.mine_ref) | copy-start | bytes 11993092
  109.6 10.5 %copy-start.7 = (f32[1,976,256]{2,1,0:T(8,128)S(1)}, f32[1,976,256]{2,1,0:T(8,128)}, u32[]{:S(2)}) copy-start(f32[1,976,256]{2,1,0:T(8,128)} %copy-done.6) | copy-start | bytes 2998276
  109.6 5.3 %collective-permute-start.8 = (f32[1,976,256]{2,1,0:T(8,128)S(1)}, f32[1,976,256]{2,1,0:T(8,128)S(1)}, u32[]{:S(2)}, u32[]{:S(2)}) collective-permute-start(f32[1,976,256]{2,1,0:T(8,128)S(1)} %get-tuple-element.53), channel_id=1, source_target_pairs={{0,16},{16,0},{32,48},{48,32},{64,80},{80,64},{96,112},{112,96},{1... | collective-permute-start | bytes 2998280 | tf_op jit(solution)/shard_map/ppermute | solution.py:48
  109.7 5.4 %collective-permute-start.9 = (f32[1,976,256]{2,1,0:T(8,128)S(1)}, f32[1,976,256]{2,1,0:T(8,128)S(1)}, u32[]{:S(2)}, u32[]{:S(2)}) collective-permute-start(f32[1,976,256]{2,1,0:T(8,128)S(1)} %get-tuple-element.54), channel_id=1, source_target_pairs={{0,16},{16,0},{32,48},{48,32},{64,80},{80,64},{96,112},{112,96},{1... | collective-permute-start | bytes 2998280 | tf_op jit(solution)/shard_map/ppermute | solution.py:48
  110.2 36.1 %collective-permute-start.7 = (f32[2,976,256]{2,1,0:T(8,128)}, f32[2,976,256]{2,1,0:T(8,128)S(1)}, u32[]{:S(2)}, u32[]{:S(2)}) collective-permute-start(f32[2,976,256]{2,1,0:T(8,128)} %get-tuple-element.52), channel_id=1, source_target_pairs={{0,16},{16,0},{32,48},{48,32},{64,80},{80,64},{96,112},{112,96},{1... | collective-permute-start | bytes 5996552 | tf_op jit(solution)/shard_map/ppermute | solution.py:48
  116.9 29.4 %copy-start = (f32[4,976,256]{2,1,0:T(8,128)S(1)}, f32[4,976,256]{2,1,0:T(8,128)}, u32[]{:S(2)}) copy-start(f32[4,976,256]{2,1,0:T(8,128)} %get-tuple-element.51.mine_ref) | copy-start | bytes 11993092
  116.9 25.6 %collective-permute-start.14 = (f32[976,256]{1,0:T(8,128)S(1)}, f32[976,256]{1,0:T(8,128)S(1)}, u32[]{:S(2)}, u32[]{:S(2)}) collective-permute-start(f32[976,256]{1,0:T(8,128)S(1)} %get-tuple-element.62), channel_id=1, source_target_pairs={{0,96},{16,112},{32,0},{48,16},{64,32},{80,48},{96,64},{112,80},{1... | collective-permute-start | bytes 2998280 | tf_op jit(solution)/shard_map/ppermute | solution.py:48
  120.1 36.9 %copy-start.3 = (f32[1,976,256]{2,1,0:T(8,128)S(1)}, f32[1,976,256]{2,1,0:T(8,128)}, u32[]{:S(2)}) copy-start(f32[1,976,256]{2,1,0:T(8,128)} %copy-done.2) | copy-start | bytes 2998276
  120.1 26.2 %collective-permute-start.12 = (f32[976,256]{1,0:T(8,128)S(1)}, f32[976,256]{1,0:T(8,128)S(1)}, u32[]{:S(2)}, u32[]{:S(2)}) collective-permute-start(f32[976,256]{1,0:T(8,128)S(1)} %get-tuple-element.63), channel_id=1, source_target_pairs={{0,32},{16,48},{32,64},{48,80},{64,96},{80,112},{96,0},{112,16},{1... | collective-permute-start | bytes 2998280 | tf_op jit(solution)/shard_map/ppermute | solution.py:48
  121.6 31.6 %collective-permute-start.17 = (f32[488,256]{1,0:T(8,128)S(1)}, f32[488,256]{1,0:T(8,128)S(1)}, u32[]{:S(2)}, u32[]{:S(2)}) collective-permute-start(f32[488,256]{1,0:T(8,128)S(1)} %get-tuple-element.60), channel_id=1, source_target_pairs={{0,96},{16,112},{32,0},{48,16},{64,32},{80,48},{96,64},{112,80},{1... | collective-permute-start | bytes 1499144 | tf_op jit(solution)/shard_map/ppermute | solution.py:48
  125.0 32.0 %collective-permute-start.16 = (f32[488,256]{1,0:T(8,128)S(1)}, f32[488,256]{1,0:T(8,128)S(1)}, u32[]{:S(2)}, u32[]{:S(2)}) collective-permute-start(f32[488,256]{1,0:T(8,128)S(1)} %get-tuple-element.61), channel_id=1, source_target_pairs={{0,32},{16,48},{32,64},{48,80},{64,96},{80,112},{96,0},{112,16},{1... | collective-permute-start | bytes 1499144 | tf_op jit(solution)/shard_map/ppermute | solution.py:48
  146.5 16.7 %collective-permute-start.15 = (f32[488,256]{1,0:T(8,128)S(1)}, f32[488,256]{1,0:T(8,128)S(1)}, u32[]{:S(2)}, u32[]{:S(2)}) collective-permute-start(f32[488,256]{1,0:T(8,128)S(1)} %get-tuple-element.58), channel_id=1, source_target_pairs={{0,96},{16,112},{32,0},{48,16},{64,32},{80,48},{96,64},{112,80},{1... | collective-permute-start | bytes 1499144 | tf_op jit(solution)/shard_map/ppermute | solution.py:48
  146.6 20.0 %collective-permute-start.13 = (f32[488,256]{1,0:T(8,128)S(1)}, f32[488,256]{1,0:T(8,128)S(1)}, u32[]{:S(2)}, u32[]{:S(2)}) collective-permute-start(f32[488,256]{1,0:T(8,128)S(1)} %get-tuple-element.59), channel_id=1, source_target_pairs={{0,32},{16,48},{32,64},{48,80},{64,96},{80,112},{96,0},{112,16},{1... | collective-permute-start | bytes 1499144 | tf_op jit(solution)/shard_map/ppermute | solution.py:48
  168.0 1.2 collective-permute-start.18
  169.2 3.7 %collective-permute-start.19 = (f32[16,128]{1,0:T(8,128)S(1)}, f32[16,128]{1,0:T(8,128)S(1)}, u32[]{:S(2)}, u32[]{:S(2)}) collective-permute-start(f32[16,128]{1,0:T(8,128)S(1)} %add.134), channel_id=1, source_target_pairs={{0,32},{16,48},{32,0},{48,16},{64,96},{80,112},{96,64},{112,80},{1... | collective-permute-start | bytes 24584 | tf_op jit(solution)/shard_map/ppermute | solution.py:349
  172.9 5.2 %collective-permute-start.20 = (f32[16,128]{1,0:T(8,128)S(1)}, f32[16,128]{1,0:T(8,128)S(1)}, u32[]{:S(2)}, u32[]{:S(2)}) collective-permute-start(f32[16,128]{1,0:T(8,128)S(1)} %add.135), channel_id=1, source_target_pairs={{0,64},{16,80},{32,96},{48,112},{64,0},{80,16},{96,32},{112,48},{1... | collective-permute-start | bytes 24584 | tf_op jit(solution)/shard_map/ppermute | solution.py:349
  178.0 3.7 %collective-permute-start.21 = (f32[16,128]{1,0:T(8,128)S(1)}, f32[16,128]{1,0:T(8,128)S(1)}, u32[]{:S(2)}, u32[]{:S(2)}) collective-permute-start(f32[16,128]{1,0:T(8,128)S(1)} %add.136), channel_id=1, source_target_pairs={{0,2},{2,0},{4,6},{6,4},{8,10},{10,8},{12,14},{14,12},{1,3},{3,1},... | collective-permute-start | bytes 24584 | tf_op jit(solution)/shard_map/ppermute | solution.py:349
  181.7 5.2 %collective-permute-start.22 = (f32[16,128]{1,0:T(8,128)S(1)}, f32[16,128]{1,0:T(8,128)S(1)}, u32[]{:S(2)}, u32[]{:S(2)}) collective-permute-start(f32[16,128]{1,0:T(8,128)S(1)} %add.137), channel_id=1, source_target_pairs={{0,1},{1,0},{2,3},{3,2},{4,5},{5,4},{6,7},{7,6},{8,9},{9,8},{10,11... | collective-permute-start | bytes 24584 | tf_op jit(solution)/shard_map/ppermute | solution.py:349
  186.8 3.7 %collective-permute-start.23 = (f32[16,128]{1,0:T(8,128)S(1)}, f32[16,128]{1,0:T(8,128)S(1)}, u32[]{:S(2)}, u32[]{:S(2)}) collective-permute-start(f32[16,128]{1,0:T(8,128)S(1)} %add.138), channel_id=1, source_target_pairs={{0,4},{2,6},{4,0},{6,2},{8,12},{10,14},{12,8},{14,10},{1,5},{3,7},... | collective-permute-start | bytes 24584 | tf_op jit(solution)/shard_map/ppermute | solution.py:349
  190.6 5.5 %collective-permute-start.24 = (f32[16,128]{1,0:T(8,128)S(1)}, f32[16,128]{1,0:T(8,128)S(1)}, u32[]{:S(2)}, u32[]{:S(2)}) collective-permute-start(f32[16,128]{1,0:T(8,128)S(1)} %add.139), channel_id=1, source_target_pairs={{0,8},{2,10},{4,12},{6,14},{8,0},{10,2},{12,4},{14,6},{1,9},{3,11}... | collective-permute-start | bytes 24584 | tf_op jit(solution)/shard_map/ppermute | solution.py:349

commit v5 on v4

--- a/solution.py
+++ b/solution.py
@@ -8,8 +8,8 @@
 from jax.sharding import PartitionSpec as P
 
 NDEG = 1280
-MESSAGES = (2, 4, 6)
-RUNS = ((0, 1), (2,))
+MESSAGES = (1, 2, 3, 6)
+RUNS = ((0, 1, 2), (3,))
 F32 = jnp.float32
 BF16 = jnp.bfloat16
 VMEM_LIMIT = 48 * 1024 * 1024
@@ -229,7 +229,7 @@
             ],
         ),
         out_shape=[jax.ShapeDtypeStruct((count, 2 * rows, width // 2), F32) for count in counts],
-        compiler_params=pltpu.CompilerParams(vmem_limit_bytes=VMEM_LIMIT),
+        compiler_params=pltpu.CompilerParams(vmem_limit_bytes=40 * 1024 * 1024),
         cost_estimate=pl.CostEstimate(flops=10**12, bytes_accessed=10**10, transcendentals=0),
         name="project",
     )(place, wave, *keeps, *recvs, table)

time: 198 us -> 195 us (0.985)
  other arithmetic: 7.45 us -> 4.4 us
  waiting for transfers between devices: 84.9 us -> 87.1 us
    pallas_call x2, Pallas kernels: 28.6 us -> 25.1 us  [project(): pl.pallas_call(functools.partial(project_kernel, share=share, first=first...]
    add x2, other arithmetic: 4.86 us -> 1.8 us  [send_early(): mine[run][spot] + other[0]]
    ppermute x18 -> x19, waiting for transfers between devices: 69 us -> 71.2 us  [send_along(): return lax.ppermute(x, 'band', pairs)]
    pallas_call x3 -> x4, Pallas kernels: 14.3 us -> 16 us  [pick_rows(): pl.pallas_call(pick_kernel, grid=(each,), in_specs=[pl.BlockSpec((count,...]
    ppermute x18 -> x19, starting transfers between devices: 20.2 us -> 19.1 us  [send_along(): return lax.ppermute(x, 'band', pairs)]
  transfers between devices with their start and end apart: 25 -> 26, of which waited for: 18 -> 17; matrix products, arithmetic and copies ran while one was open for 4% -> 2% of each run, Pallas kernels for 33% -> 33%
where the time goes in v5:
time: 195 us; the launch traced here: 194 us
  waiting for transfers between devices  87.1 us (45%)
  Pallas kernels  67.3 us (35%)
  starting transfers between devices  29.4 us (15%)
  local copies, waits for them, and re-layouts  4.79 us (2%)
  other arithmetic  4.4 us (2%)
    ppermute x19, waiting for transfers between devices, send_along(): return lax.ppermute(x, 'band', pairs)  71.2 us
    pallas_call x2, Pallas kernels, project(): pl.pallas_call(functools.partial(project_kernel, share=share, first=first...  25.1 us
    ppermute x19, starting transfers between devices, send_along(): return lax.ppermute(x, 'band', pairs)  19.1 us
    pallas_call x1, Pallas kernels, lay_out(): pl.pallas_call(functools.partial(layout_kernel, share=share), grid=(pairs...  17.1 us
    pallas_call x4, Pallas kernels, pick_rows(): pl.pallas_call(pick_kernel, grid=(each,), in_specs=[pl.BlockSpec((count,...  16 us
    ppermute x7, waiting for transfers between devices, all_sum(): x = x + lax.ppermute(x, axis, [(i, i ^ bit) for i in range(size)])  16 us
    ppermute x7, starting transfers between devices, all_sum(): x = x + lax.ppermute(x, axis, [(i, i ^ bit) for i in range(size)])  10.4 us
    pallas_call x2, Pallas kernels, place_run(): pl.pallas_call(functools.partial(place_kernel, share=share, ways=ways), g...  4.83 us
  transfers between devices with their start and end apart: 26, of which 17 were waited for; matrix products, arithmetic and copies ran while one was open for 2% of the time, Pallas kernels for 33%

profile of v5, /device:TPU:0, one launch (start us, length us, event | category | flops | bytes accessed | tf_op | source)
XLA Modules:
  0.0 193.9 jit_solution(791714620699410915)
XLA Ops:
  0.7 0.8 fusion.4
  1.6 2.3 %pick_rows.4 = (f32[1,160,512]{2,1,0:T(8,128)}, f32[1,160,512]{2,1,0:T(8,128)S(1)}) custom-call(s32[320,1]{1,0:T(8,128)S(1)} %copy.7.index_ref, f32[12,512,320]{2,1,0:T(8,128)} %bitcast.31), custom_call_target="tpu_custom_call" | custom-call | flops 999999995904 | bytes 10000000000 | tf_op jit(solution)/shard_map/pick_rows/pallas_call | solution.py:77
  3.9 3.3 %collective-permute-start.1 = (f32[1,160,512]{2,1,0:T(8,128)}, f32[1,160,512]{2,1,0:T(8,128)}, u32[]{:S(2)}, u32[]{:S(2)}) collective-permute-start(f32[1,160,512]{2,1,0:T(8,128)} %get-tuple-element.35), channel_id=1, source_target_pairs={{0,64},{16,80},{32,96},{48,112},{64,0},{80,16},{96,32},{112,48},{1... | collective-permute-start | bytes 983048 | tf_op jit(solution)/shard_map/ppermute | solution.py:48
  7.2 0.8 copy.8.index_ref
  8.0 3.0 %pick_rows.5 = (f32[2,160,512]{2,1,0:T(8,128)}, f32[2,160,512]{2,1,0:T(8,128)S(1)}) custom-call(s32[320,1]{1,0:T(8,128)S(1)} %copy.8.index_ref, f32[12,512,320]{2,1,0:T(8,128)} %bitcast.32), custom_call_target="tpu_custom_call" | custom-call | flops 999999995904 | bytes 10000000000 | tf_op jit(solution)/shard_map/pick_rows/pallas_call | solution.py:77
  11.0 0.8 copy-done.5
  12.2 4.2 %pick_rows.6 = (f32[3,160,512]{2,1,0:T(8,128)}, f32[3,160,512]{2,1,0:T(8,128)S(1)}) custom-call(s32[320,1]{1,0:T(8,128)S(1)} %copy.9.index_ref, f32[12,512,320]{2,1,0:T(8,128)} %bitcast.33), custom_call_target="tpu_custom_call" | custom-call | flops 999999995904 | bytes 10000000000 | tf_op jit(solution)/shard_map/pick_rows/pallas_call | solution.py:77
  16.4 3.3 %collective-permute-start.3 = (f32[3,160,512]{2,1,0:T(8,128)}, f32[3,160,512]{2,1,0:T(8,128)}, u32[]{:S(2)}, u32[]{:S(2)}) collective-permute-start(f32[3,160,512]{2,1,0:T(8,128)} %get-tuple-element.41), channel_id=1, source_target_pairs={{0,64},{16,80},{32,96},{48,112},{64,0},{80,16},{96,32},{112,48},{1... | collective-permute-start | bytes 2949128 | tf_op jit(solution)/shard_map/ppermute | solution.py:48
  19.8 6.5 %pick_rows.7 = (f32[6,160,512]{2,1,0:T(8,128)}, f32[6,160,512]{2,1,0:T(8,128)S(1)}) custom-call(s32[320,1]{1,0:T(8,128)S(1)} %copy.10.index_ref, f32[12,512,320]{2,1,0:T(8,128)} %bitcast.34), custom_call_target="tpu_custom_call" | custom-call | flops 999999995904 | bytes 10000000000 | tf_op jit(solution)/shard_map/pick_rows/pallas_call | solution.py:77
  26.6 17.1 %lay_out.1.refs_6_.refs_2_ = bf16[12,2,8,96,384]{4,3,2,1,0:T(8,128)(2,1)} custom-call(f32[12,160,2,648]{3,2,1,0:T(2,128)} %refs_5_, f32[12,160,2,648]{3,2,1,0:T(2,128)} %refs_5_, f32[12,160,2,648]{3,2,1,0:T(2,128)} %refs_5_, f32[12,160,2,648]{3,2,1,0:T(2,128)} %refs_5_, f32[12,160,2,648]{3,2,1,0:T(2,128)} %refs_5_, f32[12,160,2,648]{3,2,1,0:T(2,128)} %refs_5_), custom_call_target="tpu_custom_call" | custom-call | flops 999999995904 | bytes 10000000000 | tf_op jit(solution)/shard_map/lay_out/pallas_call | solution.py:125
  43.8 8.6 %collective-permute-done.3.refs_5_ = f32[3,160,512]{2,1,0:T(8,128)} collective-permute-done((f32[3,160,512]{2,1,0:T(8,128)}, f32[3,160,512]{2,1,0:T(8,128)}, u32[]{:S(2)}, u32[]{:S(2)}) %collective-permute-start.3) | collective-permute-done | bytes 983072 | tf_op jit(solution)/shard_map/ppermute | solution.py:48
  52.4 1.1 copy-done.6
  53.4 13.2 %project.2 = (f32[4,976,256]{2,1,0:T(8,128)S(1)}, f32[1,976,256]{2,1,0:T(8,128)S(1)}, f32[1,976,256]{2,1,0:T(8,128)S(1)}, f32[1,976,256]{2,1,0:T(8,128)S(1)}, f32[1,976,256]{2,1,0:T(8,128)S(1)}) custom-call(s32[3]{0:T(128)S(1)} %pad_add_fusion.place_ref, s32[12]{0:T(128)S(1)} %copy-done.4, f32[1,160,512]{2,1,0:T(8,128)S(1)} %get-tuple-element.45.refs_0_, ...), custom_call_target="tpu_custom_call" | custom-call | flops 999999995904 | bytes 10000000000 | tf_op jit(solution)/shard_map/project/pallas_call | solution.py:215
  66.8 0.5 collective-permute-start.5
  67.4 0.4 collective-permute-start.7
  67.8 1.6 collective-permute-done.4
  69.4 1.4 collective-permute-done.5
  70.8 1.5 add_bitcast_fusion.2
  72.3 2.2 %collective-permute-start.12 = (f32[976,256]{1,0:T(8,128)}, f32[976,256]{1,0:T(8,128)}, u32[]{:S(2)}, u32[]{:S(2)}) collective-permute-start(f32[976,256]{1,0:T(8,128)} %get-tuple-element.74), channel_id=1, source_target_pairs={{0,96},{16,112},{32,0},{48,16},{64,32},{80,48},{96,64},{112,80},{1... | collective-permute-start | bytes 2998280 | tf_op jit(solution)/shard_map/ppermute | solution.py:48
  74.5 20.0 %collective-permute-done.refs_1_ = f32[6,160,512]{2,1,0:T(8,128)} collective-permute-done((f32[6,160,512]{2,1,0:T(8,128)}, f32[6,160,512]{2,1,0:T(8,128)}, u32[]{:S(2)}, u32[]{:S(2)}) %collective-permute-start) | collective-permute-done | bytes 1966112 | tf_op jit(solution)/shard_map/ppermute | solution.py:48
  94.6 1.0 copy-done.2
  95.6 11.9 %project.3 = (f32[4,976,256]{2,1,0:T(8,128)S(1)}, f32[1,976,256]{2,1,0:T(8,128)S(1)}, f32[1,976,256]{2,1,0:T(8,128)S(1)}, f32[2,976,256]{2,1,0:T(8,128)S(1)}) custom-call(s32[3]{0:T(128)S(1)} %pad_add_fusion.place_ref, s32[12]{0:T(128)S(1)} %copy-done.4, f32[6,160,512]{2,1,0:T(8,128)S(1)} %get-tuple-element.43.refs_0_, ...), custom_call_target="tpu_custom_call" | custom-call | flops 999999995904 | bytes 10000000000 | tf_op jit(solution)/shard_map/project/pallas_call | solution.py:215
  107.6 0.5 collective-permute-start.10
  108.2 6.1 %collective-permute-done.12.near_down_ref = f32[976,256]{1,0:T(8,128)} collective-permute-done((f32[976,256]{1,0:T(8,128)}, f32[976,256]{1,0:T(8,128)}, u32[]{:S(2)}, u32[]{:S(2)}) %collective-permute-start.12) | collective-permute-done | bytes 999456 | tf_op jit(solution)/shard_map/ppermute | solution.py:48
  114.7 2.8 %collective-permute-start.15 = (f32[976,256]{1,0:T(8,128)S(1)}, f32[976,256]{1,0:T(8,128)S(1)}, u32[]{:S(2)}, u32[]{:S(2)}) collective-permute-start(f32[976,256]{1,0:T(8,128)S(1)} %get-tuple-element.72), channel_id=1, source_target_pairs={{0,96},{16,112},{32,0},{48,16},{64,32},{80,48},{96,64},{112,80},{1... | collective-permute-start | bytes 2998280 | tf_op jit(solution)/shard_map/ppermute | solution.py:48
  117.5 1.5 slice_add_fusion
  119.0 3.2 %collective-permute-start.18 = (f32[488,256]{1,0:T(8,128)S(1)}, f32[488,256]{1,0:T(8,128)S(1)}, u32[]{:S(2)}, u32[]{:S(2)}) collective-permute-start(f32[488,256]{1,0:T(8,128)S(1)} %get-tuple-element.70), channel_id=1, source_target_pairs={{0,96},{16,112},{32,0},{48,16},{64,32},{80,48},{96,64},{112,80},{1... | collective-permute-start | bytes 1499144 | tf_op jit(solution)/shard_map/ppermute | solution.py:48
  122.2 17.7 %collective-permute-done.15.near_down_ref = f32[976,256]{1,0:T(8,128)S(1)} collective-permute-done((f32[976,256]{1,0:T(8,128)S(1)}, f32[976,256]{1,0:T(8,128)S(1)}, u32[]{:S(2)}, u32[]{:S(2)}) %collective-permute-start.15) | collective-permute-done | bytes 999456 | tf_op jit(solution)/shard_map/ppermute | solution.py:48
  139.9 3.7 %collective-permute-done.13.near_up_ref = f32[976,256]{1,0:T(8,128)S(1)} collective-permute-done((f32[976,256]{1,0:T(8,128)S(1)}, f32[976,256]{1,0:T(8,128)S(1)}, u32[]{:S(2)}, u32[]{:S(2)}) %collective-permute-start.13) | collective-permute-done | bytes 999456 | tf_op jit(solution)/shard_map/ppermute | solution.py:48
  144.0 2.0 %collective-permute-start.14 = (f32[488,256]{1,0:T(8,128)S(1)}, f32[488,256]{1,0:T(8,128)S(1)}, u32[]{:S(2)}, u32[]{:S(2)}) collective-permute-start(f32[488,256]{1,0:T(8,128)S(1)} %get-tuple-element.69), channel_id=1, source_target_pairs={{0,32},{16,48},{32,64},{48,80},{64,96},{80,112},{96,0},{112,16},{1... | collective-permute-start | bytes 1499144 | tf_op jit(solution)/shard_map/ppermute | solution.py:48
  146.0 4.7 %collective-permute-done.18.far_down_ref = f32[488,256]{1,0:T(8,128)S(1)} collective-permute-done((f32[488,256]{1,0:T(8,128)S(1)}, f32[488,256]{1,0:T(8,128)S(1)}, u32[]{:S(2)}, u32[]{:S(2)}) %collective-permute-start.18) | collective-permute-done | bytes 499744 | tf_op jit(solution)/shard_map/ppermute | solution.py:48
  150.7 3.7 %collective-permute-done.17.far_up_ref = f32[488,256]{1,0:T(8,128)S(1)} collective-permute-done((f32[488,256]{1,0:T(8,128)S(1)}, f32[488,256]{1,0:T(8,128)S(1)}, u32[]{:S(2)}, u32[]{:S(2)}) %collective-permute-start.17) | collective-permute-done | bytes 499744 | tf_op jit(solution)/shard_map/ppermute | solution.py:48
  154.4 3.2 %place_run.2.refs_0_ = f32[12,2,4,64,81]{4,3,2,1,0:T(8,128)} custom-call(f32[4,976,256]{2,1,0:T(8,128)S(1)} %copy-done.1, f32[1,976,256]{2,1,0:T(8,128)S(1)} %copy-done.3, f32[488,256]{1,0:T(8,128)S(1)} %collective-permute-done.17.far_up_ref, f32[488,256]{1,0:T(8,128)S(1)} %collective-permute-done.18.far_down_ref, ...), custom_call_target="tpu_custom_call" | custom-call | flops 999424 | bytes 4997120 | tf_op jit(solution)/shard_map/place_run/pallas_call | solution.py:333
  157.6 2.9 %run_energy.2.so_far_ref = f32[16,128]{1,0:T(8,128)S(1)} custom-call(s32[3]{0:T(128)S(1)} %pad_add_fusion.place_ref, s32[12]{0:T(128)S(1)} %copy-done.4, f32[4,976,256]{2,1,0:T(8,128)S(1)} %copy-done.1, f32[1,976,256]{2,1,0:T(8,128)S(1)} %copy-done.3, f32[488,256]{1,0:T(8,128)S(1)} %collective-permute-done.17.far_up_ref, ...), custom_call_target="tpu_custom_call" | custom-call | flops 2498560 | bytes 3997696 | tf_op jit(solution)/shard_map/run_energy/pallas_call | solution.py:292
  160.4 3.4 %collective-permute-done.14.far_up_ref = f32[488,256]{1,0:T(8,128)S(1)} collective-permute-done((f32[488,256]{1,0:T(8,128)S(1)}, f32[488,256]{1,0:T(8,128)S(1)}, u32[]{:S(2)}, u32[]{:S(2)}) %collective-permute-start.14) | collective-permute-done | bytes 499744 | tf_op jit(solution)/shard_map/ppermute | solution.py:48
  163.9 1.4 run_energy.3
  165.3 1.2 collective-permute-done.19
  166.5 3.6 %collective-permute-done.20 = f32[16,128]{1,0:T(8,128)S(1)} collective-permute-done((f32[16,128]{1,0:T(8,128)S(1)}, f32[16,128]{1,0:T(8,128)S(1)}, u32[]{:S(2)}, u32[]{:S(2)}) %collective-permute-start.20) | collective-permute-done | bytes 8224 | tf_op jit(solution)/shard_map/ppermute | solution.py:349
  170.1 5.2 %collective-permute-done.21 = f32[16,128]{1,0:T(8,128)S(1)} collective-permute-done((f32[16,128]{1,0:T(8,128)S(1)}, f32[16,128]{1,0:T(8,128)S(1)}, u32[]{:S(2)}, u32[]{:S(2)}) %collective-permute-start.21) | collective-permute-done | bytes 8224 | tf_op jit(solution)/shard_map/ppermute | solution.py:349
  175.3 1.5 collective-permute-start.22
  176.8 2.2 %collective-permute-done.22 = f32[16,128]{1,0:T(8,128)S(1)} collective-permute-done((f32[16,128]{1,0:T(8,128)S(1)}, f32[16,128]{1,0:T(8,128)S(1)}, u32[]{:S(2)}, u32[]{:S(2)}) %collective-permute-start.22) | collective-permute-done | bytes 8224 | tf_op jit(solution)/shard_map/ppermute | solution.py:349
  178.9 3.1 %collective-permute-start.23 = (f32[16,128]{1,0:T(8,128)S(1)}, f32[16,128]{1,0:T(8,128)S(1)}, u32[]{:S(2)}, u32[]{:S(2)}) collective-permute-start(f32[16,128]{1,0:T(8,128)S(1)} %add.137), channel_id=1, source_target_pairs={{0,1},{1,0},{2,3},{3,2},{4,5},{5,4},{6,7},{7,6},{8,9},{9,8},{10,11... | collective-permute-start | bytes 24584 | tf_op jit(solution)/shard_map/ppermute | solution.py:349
  182.0 2.1 %collective-permute-done.23 = f32[16,128]{1,0:T(8,128)S(1)} collective-permute-done((f32[16,128]{1,0:T(8,128)S(1)}, f32[16,128]{1,0:T(8,128)S(1)}, u32[]{:S(2)}, u32[]{:S(2)}) %collective-permute-start.23) | collective-permute-done | bytes 8224 | tf_op jit(solution)/shard_map/ppermute | solution.py:349
  184.1 1.9 collective-permute-start.24
  186.0 1.8 collective-permute-done.24
  187.8 3.8 %collective-permute-start.25 = (f32[16,128]{1,0:T(8,128)S(1)}, f32[16,128]{1,0:T(8,128)S(1)}, u32[]{:S(2)}, u32[]{:S(2)}) collective-permute-start(f32[16,128]{1,0:T(8,128)S(1)} %add.139), channel_id=1, source_target_pairs={{0,8},{2,10},{4,12},{6,14},{8,0},{10,2},{12,4},{14,6},{1,9},{3,11}... | collective-permute-start | bytes 24584 | tf_op jit(solution)/shard_map/ppermute | solution.py:349
  191.6 1.7 place_run.3
  193.3 0.6 slice_log_fusion
  (59 shorter events, 2.2 us)
Async XLA Ops:
  1.4 2.5 %copy-start.9 = (s32[320,1]{0,1:T(1,128)}, s32[320,1]{0,1:T(1,128)S(1)}, u32[]{:S(2)}) copy-start(s32[320,1]{0,1:T(1,128)S(1)} %reshape.29) | copy-start | bytes 3844
  3.9 39.9 %collective-permute-start.1 = (f32[1,160,512]{2,1,0:T(8,128)}, f32[1,160,512]{2,1,0:T(8,128)}, u32[]{:S(2)}, u32[]{:S(2)}) collective-permute-start(f32[1,160,512]{2,1,0:T(8,128)} %get-tuple-element.35), channel_id=1, source_target_pairs={{0,64},{16,80},{32,96},{48,112},{64,0},{80,16},{96,32},{112,48},{1... | collective-permute-start | bytes 983048 | tf_op jit(solution)/shard_map/ppermute | solution.py:48
  8.0 4.1 %copy-start.10 = (s32[320,1]{0,1:T(1,128)S(1)}, s32[320,1]{0,1:T(1,128)}, u32[]{:S(2)}) copy-start(s32[320,1]{0,1:T(1,128)} %copy-done.9) | copy-start | bytes 3844
  11.0 0.8 copy-start.5
  11.8 32.0 %collective-permute-start.2 = (f32[2,160,512]{2,1,0:T(8,128)}, f32[2,160,512]{2,1,0:T(8,128)}, u32[]{:S(2)}, u32[]{:S(2)}) collective-permute-start(f32[2,160,512]{2,1,0:T(8,128)} %get-tuple-element.38), channel_id=1, source_target_pairs={{0,64},{16,80},{32,96},{48,112},{64,0},{80,16},{96,32},{112,48},{1... | collective-permute-start | bytes 1966088 | tf_op jit(solution)/shard_map/ppermute | solution.py:48
  12.2 7.5 %copy-start.11 = (s32[320,1]{0,1:T(1,128)S(1)}, s32[320,1]{0,1:T(1,128)}, u32[]{:S(2)}) copy-start(s32[320,1]{0,1:T(1,128)} %copy-done.9) | copy-start | bytes 3844
  16.4 36.0 %collective-permute-start.3 = (f32[3,160,512]{2,1,0:T(8,128)}, f32[3,160,512]{2,1,0:T(8,128)}, u32[]{:S(2)}, u32[]{:S(2)}) collective-permute-start(f32[3,160,512]{2,1,0:T(8,128)} %get-tuple-element.41), channel_id=1, source_target_pairs={{0,64},{16,80},{32,96},{48,112},{64,0},{80,16},{96,32},{112,48},{1... | collective-permute-start | bytes 2949128 | tf_op jit(solution)/shard_map/ppermute | solution.py:48
  26.3 68.2 %collective-permute-start = (f32[6,160,512]{2,1,0:T(8,128)}, f32[6,160,512]{2,1,0:T(8,128)}, u32[]{:S(2)}, u32[]{:S(2)}) collective-permute-start(f32[6,160,512]{2,1,0:T(8,128)} %get-tuple-element.44), channel_id=1, source_target_pairs={{0,64},{16,80},{32,96},{48,112},{64,0},{80,16},{96,32},{112,48},{1... | collective-permute-start | bytes 5898248 | tf_op jit(solution)/shard_map/ppermute | solution.py:48
  26.6 25.8 %copy-start.4 = (s32[12]{0:T(128)S(1)}, s32[12]{0:T(128)}, u32[]{:S(2)}) copy-start(s32[12]{0:T(128)} %wave_ref.7) | copy-start | bytes 148
  52.4 1.1 copy-start.6
  66.7 27.8 %copy-start = (f32[4,976,256]{2,1,0:T(8,128)}, f32[4,976,256]{2,1,0:T(8,128)S(1)}, u32[]{:S(2)}) copy-start(f32[4,976,256]{2,1,0:T(8,128)S(1)} %get-tuple-element.53.mine_ref) | copy-start | bytes 11993092
  66.7 2.7 %collective-permute-start.4 = (f32[1,976,256]{2,1,0:T(8,128)S(1)}, f32[1,976,256]{2,1,0:T(8,128)S(1)}, u32[]{:S(2)}, u32[]{:S(2)}) collective-permute-start(f32[1,976,256]{2,1,0:T(8,128)S(1)} %get-tuple-element.54), channel_id=1, source_target_pairs={{0,16},{16,0},{32,48},{48,32},{64,80},{80,64},{96,112},{112,96},{1... | collective-permute-start | bytes 2998280 | tf_op jit(solution)/shard_map/ppermute | solution.py:48
  66.8 4.0 %collective-permute-start.5 = (f32[1,976,256]{2,1,0:T(8,128)S(1)}, f32[1,976,256]{2,1,0:T(8,128)S(1)}, u32[]{:S(2)}, u32[]{:S(2)}) collective-permute-start(f32[1,976,256]{2,1,0:T(8,128)S(1)} %get-tuple-element.55), channel_id=1, source_target_pairs={{0,16},{16,0},{32,48},{48,32},{64,80},{80,64},{96,112},{112,96},{1... | collective-permute-start | bytes 2998280 | tf_op jit(solution)/shard_map/ppermute | solution.py:48
  67.3 27.2 %collective-permute-start.6 = (f32[1,976,256]{2,1,0:T(8,128)S(1)}, f32[1,976,256]{2,1,0:T(8,128)S(1)}, u32[]{:S(2)}, u32[]{:S(2)}) collective-permute-start(f32[1,976,256]{2,1,0:T(8,128)S(1)} %get-tuple-element.58), channel_id=1, source_target_pairs={{0,16},{16,0},{32,48},{48,32},{64,80},{80,64},{96,112},{112,96},{1... | collective-permute-start | bytes 2998280 | tf_op jit(solution)/shard_map/ppermute | solution.py:48
  67.4 27.1 %collective-permute-start.7 = (f32[1,976,256]{2,1,0:T(8,128)S(1)}, f32[1,976,256]{2,1,0:T(8,128)S(1)}, u32[]{:S(2)}, u32[]{:S(2)}) collective-permute-start(f32[1,976,256]{2,1,0:T(8,128)S(1)} %get-tuple-element.59), channel_id=1, source_target_pairs={{0,16},{16,0},{32,48},{48,32},{64,80},{80,64},{96,112},{112,96},{1... | collective-permute-start | bytes 2998280 | tf_op jit(solution)/shard_map/ppermute | solution.py:48
  72.3 42.0 %collective-permute-start.12 = (f32[976,256]{1,0:T(8,128)}, f32[976,256]{1,0:T(8,128)}, u32[]{:S(2)}, u32[]{:S(2)}) collective-permute-start(f32[976,256]{1,0:T(8,128)} %get-tuple-element.74), channel_id=1, source_target_pairs={{0,96},{16,112},{32,0},{48,16},{64,32},{80,48},{96,64},{112,80},{1... | collective-permute-start | bytes 2998280 | tf_op jit(solution)/shard_map/ppermute | solution.py:48
  74.5 39.9 %collective-permute-start.11 = (f32[976,256]{1,0:T(8,128)}, f32[976,256]{1,0:T(8,128)}, u32[]{:S(2)}, u32[]{:S(2)}) collective-permute-start(f32[976,256]{1,0:T(8,128)} %get-tuple-element.75), channel_id=1, source_target_pairs={{0,32},{16,48},{32,64},{48,80},{64,96},{80,112},{96,0},{112,16},{1... | collective-permute-start | bytes 2998280 | tf_op jit(solution)/shard_map/ppermute | solution.py:48
  94.5 12.9 %copy-start.7 = (f32[1,976,256]{2,1,0:T(8,128)}, f32[1,976,256]{2,1,0:T(8,128)S(1)}, u32[]{:S(2)}) copy-start(f32[1,976,256]{2,1,0:T(8,128)S(1)} %collective-permute-done.6) | copy-start | bytes 2998276
  94.5 1.0 copy-start.2
  107.5 10.0 %copy-start.1 = (f32[4,976,256]{2,1,0:T(8,128)S(1)}, f32[4,976,256]{2,1,0:T(8,128)}, u32[]{:S(2)}) copy-start(f32[4,976,256]{2,1,0:T(8,128)} %copy-done) | copy-start | bytes 11993092
  107.5 10.0 %copy-start.8 = (f32[1,976,256]{2,1,0:T(8,128)S(1)}, f32[1,976,256]{2,1,0:T(8,128)}, u32[]{:S(2)}) copy-start(f32[1,976,256]{2,1,0:T(8,128)} %copy-done.7) | copy-start | bytes 2998276
  107.5 7.0 %collective-permute-start.9 = (f32[1,976,256]{2,1,0:T(8,128)S(1)}, f32[1,976,256]{2,1,0:T(8,128)S(1)}, u32[]{:S(2)}, u32[]{:S(2)}) collective-permute-start(f32[1,976,256]{2,1,0:T(8,128)S(1)} %get-tuple-element.63), channel_id=1, source_target_pairs={{0,16},{16,0},{32,48},{48,32},{64,80},{80,64},{96,112},{112,96},{1... | collective-permute-start | bytes 2998280 | tf_op jit(solution)/shard_map/ppermute | solution.py:48
  107.6 6.9 %collective-permute-start.10 = (f32[1,976,256]{2,1,0:T(8,128)S(1)}, f32[1,976,256]{2,1,0:T(8,128)S(1)}, u32[]{:S(2)}, u32[]{:S(2)}) collective-permute-start(f32[1,976,256]{2,1,0:T(8,128)S(1)} %get-tuple-element.64), channel_id=1, source_target_pairs={{0,16},{16,0},{32,48},{48,32},{64,80},{80,64},{96,112},{112,96},{1... | collective-permute-start | bytes 2998280 | tf_op jit(solution)/shard_map/ppermute | solution.py:48
  108.1 35.6 %collective-permute-start.8 = (f32[2,976,256]{2,1,0:T(8,128)S(1)}, f32[2,976,256]{2,1,0:T(8,128)S(1)}, u32[]{:S(2)}, u32[]{:S(2)}) collective-permute-start(f32[2,976,256]{2,1,0:T(8,128)S(1)} %get-tuple-element.62), channel_id=1, source_target_pairs={{0,16},{16,0},{32,48},{48,32},{64,80},{80,64},{96,112},{112,96},{1... | collective-permute-start | bytes 5996552 | tf_op jit(solution)/shard_map/ppermute | solution.py:48
  114.7 25.2 %collective-permute-start.15 = (f32[976,256]{1,0:T(8,128)S(1)}, f32[976,256]{1,0:T(8,128)S(1)}, u32[]{:S(2)}, u32[]{:S(2)}) collective-permute-start(f32[976,256]{1,0:T(8,128)S(1)} %get-tuple-element.72), channel_id=1, source_target_pairs={{0,96},{16,112},{32,0},{48,16},{64,32},{80,48},{96,64},{112,80},{1... | collective-permute-start | bytes 2998280 | tf_op jit(solution)/shard_map/ppermute | solution.py:48
  117.5 36.9 %copy-start.3 = (f32[1,976,256]{2,1,0:T(8,128)S(1)}, f32[1,976,256]{2,1,0:T(8,128)}, u32[]{:S(2)}) copy-start(f32[1,976,256]{2,1,0:T(8,128)} %copy-done.2) | copy-start | bytes 2998276
  117.5 26.2 %collective-permute-start.13 = (f32[976,256]{1,0:T(8,128)S(1)}, f32[976,256]{1,0:T(8,128)S(1)}, u32[]{:S(2)}, u32[]{:S(2)}) collective-permute-start(f32[976,256]{1,0:T(8,128)S(1)} %get-tuple-element.73), channel_id=1, source_target_pairs={{0,32},{16,48},{32,64},{48,80},{64,96},{80,112},{96,0},{112,16},{1... | collective-permute-start | bytes 2998280 | tf_op jit(solution)/shard_map/ppermute | solution.py:48
  119.0 31.7 %collective-permute-start.18 = (f32[488,256]{1,0:T(8,128)S(1)}, f32[488,256]{1,0:T(8,128)S(1)}, u32[]{:S(2)}, u32[]{:S(2)}) collective-permute-start(f32[488,256]{1,0:T(8,128)S(1)} %get-tuple-element.70), channel_id=1, source_target_pairs={{0,96},{16,112},{32,0},{48,16},{64,32},{80,48},{96,64},{112,80},{1... | collective-permute-start | bytes 1499144 | tf_op jit(solution)/shard_map/ppermute | solution.py:48
  122.2 32.2 %collective-permute-start.17 = (f32[488,256]{1,0:T(8,128)S(1)}, f32[488,256]{1,0:T(8,128)S(1)}, u32[]{:S(2)}, u32[]{:S(2)}) collective-permute-start(f32[488,256]{1,0:T(8,128)S(1)} %get-tuple-element.71), channel_id=1, source_target_pairs={{0,32},{16,48},{32,64},{48,80},{64,96},{80,112},{96,0},{112,16},{1... | collective-permute-start | bytes 1499144 | tf_op jit(solution)/shard_map/ppermute | solution.py:48
  143.9 16.6 %collective-permute-start.16 = (f32[488,256]{1,0:T(8,128)S(1)}, f32[488,256]{1,0:T(8,128)S(1)}, u32[]{:S(2)}, u32[]{:S(2)}) collective-permute-start(f32[488,256]{1,0:T(8,128)S(1)} %get-tuple-element.68), channel_id=1, source_target_pairs={{0,96},{16,112},{32,0},{48,16},{64,32},{80,48},{96,64},{112,80},{1... | collective-permute-start | bytes 1499144 | tf_op jit(solution)/shard_map/ppermute | solution.py:48
  144.0 19.9 %collective-permute-start.14 = (f32[488,256]{1,0:T(8,128)S(1)}, f32[488,256]{1,0:T(8,128)S(1)}, u32[]{:S(2)}, u32[]{:S(2)}) collective-permute-start(f32[488,256]{1,0:T(8,128)S(1)} %get-tuple-element.69), channel_id=1, source_target_pairs={{0,32},{16,48},{32,64},{48,80},{64,96},{80,112},{96,0},{112,16},{1... | collective-permute-start | bytes 1499144 | tf_op jit(solution)/shard_map/ppermute | solution.py:48
  165.2 1.2 collective-permute-start.19
  166.5 3.7 %collective-permute-start.20 = (f32[16,128]{1,0:T(8,128)S(1)}, f32[16,128]{1,0:T(8,128)S(1)}, u32[]{:S(2)}, u32[]{:S(2)}) collective-permute-start(f32[16,128]{1,0:T(8,128)S(1)} %add.134), channel_id=1, source_target_pairs={{0,32},{16,48},{32,0},{48,16},{64,96},{80,112},{96,64},{112,80},{1... | collective-permute-start | bytes 24584 | tf_op jit(solution)/shard_map/ppermute | solution.py:349
  170.1 5.2 %collective-permute-start.21 = (f32[16,128]{1,0:T(8,128)S(1)}, f32[16,128]{1,0:T(8,128)S(1)}, u32[]{:S(2)}, u32[]{:S(2)}) collective-permute-start(f32[16,128]{1,0:T(8,128)S(1)} %add.135), channel_id=1, source_target_pairs={{0,64},{16,80},{32,96},{48,112},{64,0},{80,16},{96,32},{112,48},{1... | collective-permute-start | bytes 24584 | tf_op jit(solution)/shard_map/ppermute | solution.py:349
  175.3 3.7 %collective-permute-start.22 = (f32[16,128]{1,0:T(8,128)S(1)}, f32[16,128]{1,0:T(8,128)S(1)}, u32[]{:S(2)}, u32[]{:S(2)}) collective-permute-start(f32[16,128]{1,0:T(8,128)S(1)} %add.136), channel_id=1, source_target_pairs={{0,2},{2,0},{4,6},{6,4},{8,10},{10,8},{12,14},{14,12},{1,3},{3,1},... | collective-permute-start | bytes 24584 | tf_op jit(solution)/shard_map/ppermute | solution.py:349
  178.9 5.2 %collective-permute-start.23 = (f32[16,128]{1,0:T(8,128)S(1)}, f32[16,128]{1,0:T(8,128)S(1)}, u32[]{:S(2)}, u32[]{:S(2)}) collective-permute-start(f32[16,128]{1,0:T(8,128)S(1)} %add.137), channel_id=1, source_target_pairs={{0,1},{1,0},{2,3},{3,2},{4,5},{5,4},{6,7},{7,6},{8,9},{9,8},{10,11... | collective-permute-start | bytes 24584 | tf_op jit(solution)/shard_map/ppermute | solution.py:349
  184.1 3.7 %collective-permute-start.24 = (f32[16,128]{1,0:T(8,128)S(1)}, f32[16,128]{1,0:T(8,128)S(1)}, u32[]{:S(2)}, u32[]{:S(2)}) collective-permute-start(f32[16,128]{1,0:T(8,128)S(1)} %add.138), channel_id=1, source_target_pairs={{0,4},{2,6},{4,0},{6,2},{8,12},{10,14},{12,8},{14,10},{1,5},{3,7},... | collective-permute-start | bytes 24584 | tf_op jit(solution)/shard_map/ppermute | solution.py:349
  187.8 5.5 %collective-permute-start.25 = (f32[16,128]{1,0:T(8,128)S(1)}, f32[16,128]{1,0:T(8,128)S(1)}, u32[]{:S(2)}, u32[]{:S(2)}) collective-permute-start(f32[16,128]{1,0:T(8,128)S(1)} %add.139), channel_id=1, source_target_pairs={{0,8},{2,10},{4,12},{6,14},{8,0},{10,2},{12,4},{14,6},{1,9},{3,11}... | collective-permute-start | bytes 24584 | tf_op jit(solution)/shard_map/ppermute | solution.py:349

commit v6 on v5

--- a/solution.py
+++ b/solution.py
@@ -240,17 +240,12 @@
 
 
 def energy_kernel(
-    place_ref, wave_ref, mine_ref, cross_ref, far_up_ref, far_down_ref, near_up_ref, near_down_ref, so_far_ref, out_ref,
-    *, share, first, ways,
+    place_ref, wave_ref, low_ref, high_ref, far_up_ref, far_down_ref, so_far_ref, out_ref, *, share, first, ways
 ):
-    low = far_up_ref.shape[0]
     lanes = out_ref.shape[1]
     halves = []
-    for rows, far_ref, near_ref in (
-        (slice(None, low), far_up_ref, near_down_ref),
-        (slice(low, None), far_down_ref, near_up_ref),
-    ):
-        value = (mine_ref[0, rows, :] + cross_ref[0, rows, :]) + (far_ref[...] + near_ref[rows, :])
+    for held_ref, far_ref in ((low_ref, far_up_ref), (high_ref, far_down_ref)):
+        value = held_ref[...] + far_ref[...]
         squares = value * value
         halves.append(squares[:, :lanes] + squares[:, lanes:])
     squares = jnp.concatenate(halves, 0)
@@ -288,7 +283,7 @@
 
 
 def run_energy(place, wave, parts, so_far, share, first, ways):
-    _, rows, width = parts[0].shape
+    rows, width = parts[0].shape
     return pl.pallas_call(
         functools.partial(energy_kernel, share=share, first=first, ways=ways),
         grid_spec=pltpu.PrefetchScalarGridSpec(
@@ -305,31 +300,24 @@
 
 
 def own_parts(parts):
-    _, rows, width = parts[0].shape
-    return [
-        pl.BlockSpec((1, rows, width), lambda step, *_: (parts[0].shape[0] - 1, 0, 0)),
-        pl.BlockSpec((1, rows, width), lambda step, *_: (parts[1].shape[0] - 1, 0, 0)),
-    ] + [pl.BlockSpec(part.shape, lambda step, *_: (0, 0)) for part in parts[2:]]
-
-
-def place_kernel(mine_ref, cross_ref, far_up_ref, far_down_ref, near_up_ref, near_down_ref, *refs, share, ways):
+    return [pl.BlockSpec(part.shape, lambda step, *_: (0, 0)) for part in parts]
+
+
+def place_kernel(low_ref, high_ref, far_up_ref, far_down_ref, *refs, share, ways):
     out_ref = refs[-1]
-    low = far_up_ref.shape[0]
+    low = low_ref.shape[0]
     for pair, at in enumerate(ways):
         for parity in range(2):
             begin = at + parity * share
-            rows = slice(begin, begin + share)
-            if begin < low:
-                arrived = far_up_ref[rows, :] + near_down_ref[rows, :]
-            else:
-                arrived = far_down_ref[begin - low : begin - low + share, :] + near_up_ref[rows, :]
-            value = ((mine_ref[0, rows, :] + cross_ref[0, rows, :]) + arrived).T
+            held_ref, far_ref = (low_ref, far_up_ref) if begin < low else (high_ref, far_down_ref)
+            rows = slice(begin % low, begin % low + share)
+            value = (held_ref[rows, :] + far_ref[rows, :]).T
             out_ref[pair, parity] = value.reshape(out_ref.shape[2:])
 
 
 def place_run(parts, held, shape, share, first, ways):
     each = len(ways)
-    _, rows, width = parts[0].shape
+    rows, width = parts[0].shape
     return pl.pallas_call(
         functools.partial(place_kernel, share=share, ways=ways),
         grid=(1,),
@@ -416,7 +404,13 @@
     held = []
     total = jnp.zeros((16, 128), F32)
     for run in range(len(RUNS)):
-        parts = [mine[run], cross[run][-1]] + far[run] + near[run]
+        own, other = mine[run][3], cross[run][-1][-1]
+        low = own.shape[0] // 2
+        parts = [
+            own[:low] + other[:low] + near[run][1][:low],
+            own[low:] + other[low:] + near[run][0][low:],
+            *far[run],
+        ]
         total = run_energy(place, pair_m, parts, behind(total, held), share, firsts[run], ways[run])
         held = [place_run(parts, held, shape, share, firsts[run], ways[run])]
     total = all_sum(total)

time: 195 us -> 192 us (0.985)
  starting transfers between devices: 29.4 us -> 33.9 us
  waiting for transfers between devices: 87.1 us -> 83.5 us
  Pallas kernels: 67.3 us -> 64.5 us
    ppermute x7, waiting for transfers between devices: 16 us -> 12.3 us  [all_sum(): x = x + lax.ppermute(x, axis, [(i, i ^ bit) for i in range(size)])]
    ppermute x7, starting transfers between devices: 10.4 us -> 14 us  [all_sum(): x = x + lax.ppermute(x, axis, [(i, i ^ bit) for i in range(size)])]
  transfers between devices with their start and end apart: 26 -> 26, of which waited for: 17 -> 17; matrix products, arithmetic and copies ran while one was open for 2% -> 3% of each run, Pallas kernels for 33% -> 32%
where the time goes in v6:
time: 192 us
  waiting for transfers between devices  83.5 us (43%)
  Pallas kernels  64.5 us (34%)
  starting transfers between devices  33.9 us (18%)
  other arithmetic  5 us (3%)
  local copies, waits for them, and re-layouts  3.8 us (2%)
    ppermute x19, waiting for transfers between devices, send_along(): return lax.ppermute(x, 'band', pairs)  71.2 us
    pallas_call x2, Pallas kernels, project(): pl.pallas_call(functools.partial(project_kernel, share=share, first=first...  25.7 us
    ppermute x19, starting transfers between devices, send_along(): return lax.ppermute(x, 'band', pairs)  19.9 us
    pallas_call x1, Pallas kernels, lay_out(): pl.pallas_call(functools.partial(layout_kernel, share=share), grid=(pairs...  17.1 us
    pallas_call x4, Pallas kernels, pick_rows(): pl.pallas_call(pick_kernel, grid=(each,), in_specs=[pl.BlockSpec((count,...  16 us
    ppermute x7, starting transfers between devices, all_sum(): x = x + lax.ppermute(x, axis, [(i, i ^ bit) for i in range(size)])  14 us
    ppermute x7, waiting for transfers between devices, all_sum(): x = x + lax.ppermute(x, axis, [(i, i ^ bit) for i in range(size)])  12.3 us
  transfers between devices with their start and end apart: 26, of which 17 were waited for; matrix products, arithmetic and copies ran while one was open for 3% of the time, Pallas kernels for 32%

profile of v6, /device:TPU:0, one launch (start us, length us, event | category | flops | bytes accessed | tf_op | source)
XLA Modules:
  0.0 191.5 jit_solution(9987922882118522734)
XLA Ops:
  0.7 0.8 fusion.8
  1.6 2.3 %pick_rows.4 = (f32[1,160,512]{2,1,0:T(8,128)}, f32[1,160,512]{2,1,0:T(8,128)S(1)}) custom-call(s32[320,1]{1,0:T(8,128)S(1)} %copy.7.index_ref, f32[12,512,320]{2,1,0:T(8,128)} %bitcast.47), custom_call_target="tpu_custom_call" | custom-call | flops 999999995904 | bytes 10000000000 | tf_op jit(solution)/shard_map/pick_rows/pallas_call | solution.py:77
  3.9 3.3 %collective-permute-start.1 = (f32[1,160,512]{2,1,0:T(8,128)}, f32[1,160,512]{2,1,0:T(8,128)}, u32[]{:S(2)}, u32[]{:S(2)}) collective-permute-start(f32[1,160,512]{2,1,0:T(8,128)} %get-tuple-element.35), channel_id=1, source_target_pairs={{0,64},{16,80},{32,96},{48,112},{64,0},{80,16},{96,32},{112,48},{1... | collective-permute-start | bytes 983048 | tf_op jit(solution)/shard_map/ppermute | solution.py:48
  7.2 0.8 copy.8.index_ref
  8.0 3.0 %pick_rows.5 = (f32[2,160,512]{2,1,0:T(8,128)}, f32[2,160,512]{2,1,0:T(8,128)S(1)}) custom-call(s32[320,1]{1,0:T(8,128)S(1)} %copy.8.index_ref, f32[12,512,320]{2,1,0:T(8,128)} %bitcast.48), custom_call_target="tpu_custom_call" | custom-call | flops 999999995904 | bytes 10000000000 | tf_op jit(solution)/shard_map/pick_rows/pallas_call | solution.py:77
  11.0 0.8 copy-done.3
  12.2 4.2 %pick_rows.6 = (f32[3,160,512]{2,1,0:T(8,128)}, f32[3,160,512]{2,1,0:T(8,128)S(1)}) custom-call(s32[320,1]{1,0:T(8,128)S(1)} %copy.9.index_ref, f32[12,512,320]{2,1,0:T(8,128)} %bitcast.49), custom_call_target="tpu_custom_call" | custom-call | flops 999999995904 | bytes 10000000000 | tf_op jit(solution)/shard_map/pick_rows/pallas_call | solution.py:77
  16.4 3.3 %collective-permute-start.3 = (f32[3,160,512]{2,1,0:T(8,128)}, f32[3,160,512]{2,1,0:T(8,128)}, u32[]{:S(2)}, u32[]{:S(2)}) collective-permute-start(f32[3,160,512]{2,1,0:T(8,128)} %get-tuple-element.41), channel_id=1, source_target_pairs={{0,64},{16,80},{32,96},{48,112},{64,0},{80,16},{96,32},{112,48},{1... | collective-permute-start | bytes 2949128 | tf_op jit(solution)/shard_map/ppermute | solution.py:48
  19.8 6.5 %pick_rows.7 = (f32[6,160,512]{2,1,0:T(8,128)}, f32[6,160,512]{2,1,0:T(8,128)S(1)}) custom-call(s32[320,1]{1,0:T(8,128)S(1)} %copy.10.index_ref, f32[12,512,320]{2,1,0:T(8,128)} %bitcast.50), custom_call_target="tpu_custom_call" | custom-call | flops 999999995904 | bytes 10000000000 | tf_op jit(solution)/shard_map/pick_rows/pallas_call | solution.py:77
  26.6 17.1 %lay_out.1.refs_6_.refs_2_ = bf16[12,2,8,96,384]{4,3,2,1,0:T(8,128)(2,1)} custom-call(f32[12,160,2,648]{3,2,1,0:T(2,128)} %refs_5_, f32[12,160,2,648]{3,2,1,0:T(2,128)} %refs_5_, f32[12,160,2,648]{3,2,1,0:T(2,128)} %refs_5_, f32[12,160,2,648]{3,2,1,0:T(2,128)} %refs_5_, f32[12,160,2,648]{3,2,1,0:T(2,128)} %refs_5_, f32[12,160,2,648]{3,2,1,0:T(2,128)} %refs_5_), custom_call_target="tpu_custom_call" | custom-call | flops 999999995904 | bytes 10000000000 | tf_op jit(solution)/shard_map/lay_out/pallas_call | solution.py:125
  43.8 8.6 %collective-permute-done.3.refs_5_ = f32[3,160,512]{2,1,0:T(8,128)} collective-permute-done((f32[3,160,512]{2,1,0:T(8,128)}, f32[3,160,512]{2,1,0:T(8,128)}, u32[]{:S(2)}, u32[]{:S(2)}) %collective-permute-start.3) | collective-permute-done | bytes 983072 | tf_op jit(solution)/shard_map/ppermute | solution.py:48
  52.4 1.1 copy-done.4
  53.4 13.2 %project.2 = (f32[4,976,256]{2,1,0:T(8,128)S(1)}, f32[1,976,256]{2,1,0:T(8,128)S(1)}, f32[1,976,256]{2,1,0:T(8,128)S(1)}, f32[1,976,256]{2,1,0:T(8,128)S(1)}, f32[1,976,256]{2,1,0:T(8,128)S(1)}) custom-call(s32[3]{0:T(128)S(1)} %pad_add_fusion.place_ref, s32[12]{0:T(128)S(1)} %copy-done.2, f32[1,160,512]{2,1,0:T(8,128)S(1)} %get-tuple-element.45.refs_0_, ...), custom_call_target="tpu_custom_call" | custom-call | flops 999999995904 | bytes 10000000000 | tf_op jit(solution)/shard_map/project/pallas_call | solution.py:215
  66.8 0.5 collective-permute-start.5
  67.8 1.6 collective-permute-done.4
  69.4 1.4 collective-permute-done.5
  70.8 1.5 add_bitcast_fusion.2
  72.3 2.2 %collective-permute-start.12 = (f32[976,256]{1,0:T(8,128)}, f32[976,256]{1,0:T(8,128)}, u32[]{:S(2)}, u32[]{:S(2)}) collective-permute-start(f32[976,256]{1,0:T(8,128)} %get-tuple-element.80), channel_id=1, source_target_pairs={{0,96},{16,112},{32,0},{48,16},{64,32},{80,48},{96,64},{112,80},{1... | collective-permute-start | bytes 2998280 | tf_op jit(solution)/shard_map/ppermute | solution.py:48
  74.5 20.0 %collective-permute-done.refs_1_ = f32[6,160,512]{2,1,0:T(8,128)} collective-permute-done((f32[6,160,512]{2,1,0:T(8,128)}, f32[6,160,512]{2,1,0:T(8,128)}, u32[]{:S(2)}, u32[]{:S(2)}) %collective-permute-start) | collective-permute-done | bytes 1966112 | tf_op jit(solution)/shard_map/ppermute | solution.py:48
  94.5 12.4 %project.3 = (f32[4,976,256]{2,1,0:T(8,128)S(1)}, f32[1,976,256]{2,1,0:T(8,128)S(1)}, f32[1,976,256]{2,1,0:T(8,128)S(1)}, f32[2,976,256]{2,1,0:T(8,128)S(1)}) custom-call(s32[3]{0:T(128)S(1)} %pad_add_fusion.place_ref, s32[12]{0:T(128)S(1)} %copy-done.2, f32[6,160,512]{2,1,0:T(8,128)S(1)} %get-tuple-element.43.refs_0_, ...), custom_call_target="tpu_custom_call" | custom-call | flops 999999995904 | bytes 10000000000 | tf_op jit(solution)/shard_map/project/pallas_call | solution.py:215
  107.1 0.5 collective-permute-start.10
  107.7 6.6 %collective-permute-done.12 = f32[976,256]{1,0:T(8,128)} collective-permute-done((f32[976,256]{1,0:T(8,128)}, f32[976,256]{1,0:T(8,128)}, u32[]{:S(2)}, u32[]{:S(2)}) %collective-permute-start.12) | collective-permute-done | bytes 999456 | tf_op jit(solution)/shard_map/ppermute | solution.py:48
  114.8 1.5 collective-permute-start.14
  116.2 2.0 %collective-permute-start.13 = (f32[976,256]{1,0:T(8,128)S(1)}, f32[976,256]{1,0:T(8,128)S(1)}, u32[]{:S(2)}, u32[]{:S(2)}) collective-permute-start(f32[976,256]{1,0:T(8,128)S(1)} %get-tuple-element.79), channel_id=1, source_target_pairs={{0,96},{16,112},{32,0},{48,16},{64,32},{80,48},{96,64},{112,80},{1... | collective-permute-start | bytes 2998280 | tf_op jit(solution)/shard_map/ppermute | solution.py:48
  118.3 1.9 slice_add_fusion
  120.1 1.4 collective-permute-start.18
  121.5 0.7 collective-permute-start.17
  122.2 19.0 %collective-permute-done.14 = f32[976,256]{1,0:T(8,128)S(1)} collective-permute-done((f32[976,256]{1,0:T(8,128)S(1)}, f32[976,256]{1,0:T(8,128)S(1)}, u32[]{:S(2)}, u32[]{:S(2)}) %collective-permute-start.14) | collective-permute-done | bytes 999456 | tf_op jit(solution)/shard_map/ppermute | solution.py:48
  141.7 3.3 %collective-permute-start.16 = (f32[488,256]{1,0:T(8,128)S(1)}, f32[488,256]{1,0:T(8,128)S(1)}, u32[]{:S(2)}, u32[]{:S(2)}) collective-permute-start(f32[488,256]{1,0:T(8,128)S(1)} %get-tuple-element.68), channel_id=1, source_target_pairs={{0,96},{16,112},{32,0},{48,16},{64,32},{80,48},{96,64},{112,80},{1... | collective-permute-start | bytes 1499144 | tf_op jit(solution)/shard_map/ppermute | solution.py:48
  144.9 7.0 %collective-permute-done.18.far_down_ref = f32[488,256]{1,0:T(8,128)S(1)} collective-permute-done((f32[488,256]{1,0:T(8,128)S(1)}, f32[488,256]{1,0:T(8,128)S(1)}, u32[]{:S(2)}, u32[]{:S(2)}) %collective-permute-start.18) | collective-permute-done | bytes 499744 | tf_op jit(solution)/shard_map/ppermute | solution.py:48
  152.0 1.6 place_run.2.refs_0_
  153.6 1.2 run_energy.2.so_far_ref
  154.8 6.4 %collective-permute-done.16.far_down_ref = f32[488,256]{1,0:T(8,128)S(1)} collective-permute-done((f32[488,256]{1,0:T(8,128)S(1)}, f32[488,256]{1,0:T(8,128)S(1)}, u32[]{:S(2)}, u32[]{:S(2)}) %collective-permute-start.16) | collective-permute-done | bytes 499744 | tf_op jit(solution)/shard_map/ppermute | solution.py:48
  161.7 1.2 run_energy.3
  163.0 1.2 collective-permute-done.19
  164.1 1.1 collective-permute-start.20
  165.3 2.5 %collective-permute-done.20 = f32[16,128]{1,0:T(8,128)S(1)} collective-permute-done((f32[16,128]{1,0:T(8,128)S(1)}, f32[16,128]{1,0:T(8,128)S(1)}, u32[]{:S(2)}, u32[]{:S(2)}) %collective-permute-start.20) | collective-permute-done | bytes 8224 | tf_op jit(solution)/shard_map/ppermute | solution.py:337
  167.8 2.5 %collective-permute-start.21 = (f32[16,128]{1,0:T(8,128)S(1)}, f32[16,128]{1,0:T(8,128)S(1)}, u32[]{:S(2)}, u32[]{:S(2)}) collective-permute-start(f32[16,128]{1,0:T(8,128)S(1)} %add.183), channel_id=1, source_target_pairs={{0,64},{16,80},{32,96},{48,112},{64,0},{80,16},{96,32},{112,48},{1... | collective-permute-start | bytes 24584 | tf_op jit(solution)/shard_map/ppermute | solution.py:337
  170.3 2.7 %collective-permute-done.21 = f32[16,128]{1,0:T(8,128)S(1)} collective-permute-done((f32[16,128]{1,0:T(8,128)S(1)}, f32[16,128]{1,0:T(8,128)S(1)}, u32[]{:S(2)}, u32[]{:S(2)}) %collective-permute-start.21) | collective-permute-done | bytes 8224 | tf_op jit(solution)/shard_map/ppermute | solution.py:337
  173.0 1.5 collective-permute-start.22
  174.4 2.2 %collective-permute-done.22 = f32[16,128]{1,0:T(8,128)S(1)} collective-permute-done((f32[16,128]{1,0:T(8,128)S(1)}, f32[16,128]{1,0:T(8,128)S(1)}, u32[]{:S(2)}, u32[]{:S(2)}) %collective-permute-start.22) | collective-permute-done | bytes 8224 | tf_op jit(solution)/shard_map/ppermute | solution.py:337
  176.6 3.1 %collective-permute-start.23 = (f32[16,128]{1,0:T(8,128)S(1)}, f32[16,128]{1,0:T(8,128)S(1)}, u32[]{:S(2)}, u32[]{:S(2)}) collective-permute-start(f32[16,128]{1,0:T(8,128)S(1)} %add.185), channel_id=1, source_target_pairs={{0,1},{1,0},{2,3},{3,2},{4,5},{5,4},{6,7},{7,6},{8,9},{9,8},{10,11... | collective-permute-start | bytes 24584 | tf_op jit(solution)/shard_map/ppermute | solution.py:337
  179.7 2.1 %collective-permute-done.23 = f32[16,128]{1,0:T(8,128)S(1)} collective-permute-done((f32[16,128]{1,0:T(8,128)S(1)}, f32[16,128]{1,0:T(8,128)S(1)}, u32[]{:S(2)}, u32[]{:S(2)}) %collective-permute-start.23) | collective-permute-done | bytes 8224 | tf_op jit(solution)/shard_map/ppermute | solution.py:337
  181.8 1.9 collective-permute-start.24
  183.7 1.8 collective-permute-done.24
  185.5 3.8 %collective-permute-start.25 = (f32[16,128]{1,0:T(8,128)S(1)}, f32[16,128]{1,0:T(8,128)S(1)}, u32[]{:S(2)}, u32[]{:S(2)}) collective-permute-start(f32[16,128]{1,0:T(8,128)S(1)} %add.187), channel_id=1, source_target_pairs={{0,8},{2,10},{4,12},{6,14},{8,0},{10,2},{12,4},{14,6},{1,9},{3,11}... | collective-permute-start | bytes 24584 | tf_op jit(solution)/shard_map/ppermute | solution.py:337
  189.3 1.6 place_run.3
  190.9 0.6 slice_log_fusion
  (59 shorter events, 3.2 us)
Async XLA Ops:
  1.4 2.5 %copy-start.9 = (s32[320,1]{0,1:T(1,128)}, s32[320,1]{0,1:T(1,128)S(1)}, u32[]{:S(2)}) copy-start(s32[320,1]{0,1:T(1,128)S(1)} %reshape.41) | copy-start | bytes 3844
  3.9 39.9 %collective-permute-start.1 = (f32[1,160,512]{2,1,0:T(8,128)}, f32[1,160,512]{2,1,0:T(8,128)}, u32[]{:S(2)}, u32[]{:S(2)}) collective-permute-start(f32[1,160,512]{2,1,0:T(8,128)} %get-tuple-element.35), channel_id=1, source_target_pairs={{0,64},{16,80},{32,96},{48,112},{64,0},{80,16},{96,32},{112,48},{1... | collective-permute-start | bytes 983048 | tf_op jit(solution)/shard_map/ppermute | solution.py:48
  8.0 4.1 %copy-start.10 = (s32[320,1]{0,1:T(1,128)S(1)}, s32[320,1]{0,1:T(1,128)}, u32[]{:S(2)}) copy-start(s32[320,1]{0,1:T(1,128)} %copy-done.9) | copy-start | bytes 3844
  11.0 0.8 copy-start.3
  11.8 32.0 %collective-permute-start.2 = (f32[2,160,512]{2,1,0:T(8,128)}, f32[2,160,512]{2,1,0:T(8,128)}, u32[]{:S(2)}, u32[]{:S(2)}) collective-permute-start(f32[2,160,512]{2,1,0:T(8,128)} %get-tuple-element.38), channel_id=1, source_target_pairs={{0,64},{16,80},{32,96},{48,112},{64,0},{80,16},{96,32},{112,48},{1... | collective-permute-start | bytes 1966088 | tf_op jit(solution)/shard_map/ppermute | solution.py:48
  12.2 7.5 %copy-start.11 = (s32[320,1]{0,1:T(1,128)S(1)}, s32[320,1]{0,1:T(1,128)}, u32[]{:S(2)}) copy-start(s32[320,1]{0,1:T(1,128)} %copy-done.9) | copy-start | bytes 3844
  16.4 36.0 %collective-permute-start.3 = (f32[3,160,512]{2,1,0:T(8,128)}, f32[3,160,512]{2,1,0:T(8,128)}, u32[]{:S(2)}, u32[]{:S(2)}) collective-permute-start(f32[3,160,512]{2,1,0:T(8,128)} %get-tuple-element.41), channel_id=1, source_target_pairs={{0,64},{16,80},{32,96},{48,112},{64,0},{80,16},{96,32},{112,48},{1... | collective-permute-start | bytes 2949128 | tf_op jit(solution)/shard_map/ppermute | solution.py:48
  26.3 68.2 %collective-permute-start = (f32[6,160,512]{2,1,0:T(8,128)}, f32[6,160,512]{2,1,0:T(8,128)}, u32[]{:S(2)}, u32[]{:S(2)}) collective-permute-start(f32[6,160,512]{2,1,0:T(8,128)} %get-tuple-element.44), channel_id=1, source_target_pairs={{0,64},{16,80},{32,96},{48,112},{64,0},{80,16},{96,32},{112,48},{1... | collective-permute-start | bytes 5898248 | tf_op jit(solution)/shard_map/ppermute | solution.py:48
  26.6 25.8 %copy-start.2 = (s32[12]{0:T(128)S(1)}, s32[12]{0:T(128)}, u32[]{:S(2)}) copy-start(s32[12]{0:T(128)} %wave_ref.7) | copy-start | bytes 148
  52.4 1.1 copy-start.4
  66.7 4.1 %copy-start = (f32[4,976,256]{2,1,0:T(8,128)}, f32[4,976,256]{2,1,0:T(8,128)S(1)}, u32[]{:S(2)}) copy-start(f32[4,976,256]{2,1,0:T(8,128)S(1)} %get-tuple-element.53) | copy-start | bytes 11993092
  66.7 2.7 %collective-permute-start.4 = (f32[1,976,256]{2,1,0:T(8,128)S(1)}, f32[1,976,256]{2,1,0:T(8,128)S(1)}, u32[]{:S(2)}, u32[]{:S(2)}) collective-permute-start(f32[1,976,256]{2,1,0:T(8,128)S(1)} %get-tuple-element.54), channel_id=1, source_target_pairs={{0,16},{16,0},{32,48},{48,32},{64,80},{80,64},{96,112},{112,96},{1... | collective-permute-start | bytes 2998280 | tf_op jit(solution)/shard_map/ppermute | solution.py:48
  66.8 4.0 %collective-permute-start.5 = (f32[1,976,256]{2,1,0:T(8,128)S(1)}, f32[1,976,256]{2,1,0:T(8,128)S(1)}, u32[]{:S(2)}, u32[]{:S(2)}) collective-permute-start(f32[1,976,256]{2,1,0:T(8,128)S(1)} %get-tuple-element.55), channel_id=1, source_target_pairs={{0,16},{16,0},{32,48},{48,32},{64,80},{80,64},{96,112},{112,96},{1... | collective-permute-start | bytes 2998280 | tf_op jit(solution)/shard_map/ppermute | solution.py:48
  67.3 27.2 %collective-permute-start.6 = (f32[1,976,256]{2,1,0:T(8,128)S(1)}, f32[1,976,256]{2,1,0:T(8,128)S(1)}, u32[]{:S(2)}, u32[]{:S(2)}) collective-permute-start(f32[1,976,256]{2,1,0:T(8,128)S(1)} %get-tuple-element.58), channel_id=1, source_target_pairs={{0,16},{16,0},{32,48},{48,32},{64,80},{80,64},{96,112},{112,96},{1... | collective-permute-start | bytes 2998280 | tf_op jit(solution)/shard_map/ppermute | solution.py:48
  67.4 27.1 %collective-permute-start.7 = (f32[1,976,256]{2,1,0:T(8,128)S(1)}, f32[1,976,256]{2,1,0:T(8,128)S(1)}, u32[]{:S(2)}, u32[]{:S(2)}) collective-permute-start(f32[1,976,256]{2,1,0:T(8,128)S(1)} %get-tuple-element.59), channel_id=1, source_target_pairs={{0,16},{16,0},{32,48},{48,32},{64,80},{80,64},{96,112},{112,96},{1... | collective-permute-start | bytes 2998280 | tf_op jit(solution)/shard_map/ppermute | solution.py:48
  72.3 42.0 %collective-permute-start.12 = (f32[976,256]{1,0:T(8,128)}, f32[976,256]{1,0:T(8,128)}, u32[]{:S(2)}, u32[]{:S(2)}) collective-permute-start(f32[976,256]{1,0:T(8,128)} %get-tuple-element.80), channel_id=1, source_target_pairs={{0,96},{16,112},{32,0},{48,16},{64,32},{80,48},{96,64},{112,80},{1... | collective-permute-start | bytes 2998280 | tf_op jit(solution)/shard_map/ppermute | solution.py:48
  74.5 39.9 %collective-permute-start.11 = (f32[976,256]{1,0:T(8,128)}, f32[976,256]{1,0:T(8,128)}, u32[]{:S(2)}, u32[]{:S(2)}) collective-permute-start(f32[976,256]{1,0:T(8,128)} %get-tuple-element.81), channel_id=1, source_target_pairs={{0,32},{16,48},{32,64},{48,80},{64,96},{80,112},{96,0},{112,16},{1... | collective-permute-start | bytes 2998280 | tf_op jit(solution)/shard_map/ppermute | solution.py:48
  94.5 12.5 %copy-start.5 = (f32[1,976,256]{2,1,0:T(8,128)}, f32[1,976,256]{2,1,0:T(8,128)S(1)}, u32[]{:S(2)}) copy-start(f32[1,976,256]{2,1,0:T(8,128)S(1)} %collective-permute-done.6) | copy-start | bytes 2998276
  94.5 12.5 %copy-start.7 = (f32[1,976,256]{2,1,0:T(8,128)}, f32[1,976,256]{2,1,0:T(8,128)S(1)}, u32[]{:S(2)}) copy-start(f32[1,976,256]{2,1,0:T(8,128)S(1)} %collective-permute-done.7) | copy-start | bytes 2998276
  107.0 11.2 %copy-start.1 = (f32[4,976,256]{2,1,0:T(8,128)S(1)}, f32[4,976,256]{2,1,0:T(8,128)}, u32[]{:S(2)}) copy-start(f32[4,976,256]{2,1,0:T(8,128)} %copy-done) | copy-start | bytes 11993092
  107.0 11.2 %copy-start.6 = (f32[1,976,256]{2,1,0:T(8,128)S(1)}, f32[1,976,256]{2,1,0:T(8,128)}, u32[]{:S(2)}) copy-start(f32[1,976,256]{2,1,0:T(8,128)} %copy-done.5) | copy-start | bytes 2998276
  107.0 11.2 %copy-start.8 = (f32[1,976,256]{2,1,0:T(8,128)S(1)}, f32[1,976,256]{2,1,0:T(8,128)}, u32[]{:S(2)}) copy-start(f32[1,976,256]{2,1,0:T(8,128)} %copy-done.7) | copy-start | bytes 2998276
  107.1 7.4 %collective-permute-start.9 = (f32[1,976,256]{2,1,0:T(8,128)S(1)}, f32[1,976,256]{2,1,0:T(8,128)S(1)}, u32[]{:S(2)}, u32[]{:S(2)}) collective-permute-start(f32[1,976,256]{2,1,0:T(8,128)S(1)} %get-tuple-element.63), channel_id=1, source_target_pairs={{0,16},{16,0},{32,48},{48,32},{64,80},{80,64},{96,112},{112,96},{1... | collective-permute-start | bytes 2998280 | tf_op jit(solution)/shard_map/ppermute | solution.py:48
  107.1 7.3 %collective-permute-start.10 = (f32[1,976,256]{2,1,0:T(8,128)S(1)}, f32[1,976,256]{2,1,0:T(8,128)S(1)}, u32[]{:S(2)}, u32[]{:S(2)}) collective-permute-start(f32[1,976,256]{2,1,0:T(8,128)S(1)} %get-tuple-element.64), channel_id=1, source_target_pairs={{0,16},{16,0},{32,48},{48,32},{64,80},{80,64},{96,112},{112,96},{1... | collective-permute-start | bytes 2998280 | tf_op jit(solution)/shard_map/ppermute | solution.py:48
  107.6 33.6 %collective-permute-start.8 = (f32[2,976,256]{2,1,0:T(8,128)S(1)}, f32[2,976,256]{2,1,0:T(8,128)S(1)}, u32[]{:S(2)}, u32[]{:S(2)}) collective-permute-start(f32[2,976,256]{2,1,0:T(8,128)S(1)} %get-tuple-element.62), channel_id=1, source_target_pairs={{0,16},{16,0},{32,48},{48,32},{64,80},{80,64},{96,112},{112,96},{1... | collective-permute-start | bytes 5996552 | tf_op jit(solution)/shard_map/ppermute | solution.py:48
  114.8 26.4 %collective-permute-start.14 = (f32[976,256]{1,0:T(8,128)S(1)}, f32[976,256]{1,0:T(8,128)S(1)}, u32[]{:S(2)}, u32[]{:S(2)}) collective-permute-start(f32[976,256]{1,0:T(8,128)S(1)} %get-tuple-element.78), channel_id=1, source_target_pairs={{0,32},{16,48},{32,64},{48,80},{64,96},{80,112},{96,0},{112,16},{1... | collective-permute-start | bytes 2998280 | tf_op jit(solution)/shard_map/ppermute | solution.py:48
  116.2 25.0 %collective-permute-start.13 = (f32[976,256]{1,0:T(8,128)S(1)}, f32[976,256]{1,0:T(8,128)S(1)}, u32[]{:S(2)}, u32[]{:S(2)}) collective-permute-start(f32[976,256]{1,0:T(8,128)S(1)} %get-tuple-element.79), channel_id=1, source_target_pairs={{0,96},{16,112},{32,0},{48,16},{64,32},{80,48},{96,64},{112,80},{1... | collective-permute-start | bytes 2998280 | tf_op jit(solution)/shard_map/ppermute | solution.py:48
  120.1 31.8 %collective-permute-start.18 = (f32[488,256]{1,0:T(8,128)S(1)}, f32[488,256]{1,0:T(8,128)S(1)}, u32[]{:S(2)}, u32[]{:S(2)}) collective-permute-start(f32[488,256]{1,0:T(8,128)S(1)} %get-tuple-element.74), channel_id=1, source_target_pairs={{0,96},{16,112},{32,0},{48,16},{64,32},{80,48},{96,64},{112,80},{1... | collective-permute-start | bytes 1499144 | tf_op jit(solution)/shard_map/ppermute | solution.py:48
  121.5 30.5 %collective-permute-start.17 = (f32[488,256]{1,0:T(8,128)S(1)}, f32[488,256]{1,0:T(8,128)S(1)}, u32[]{:S(2)}, u32[]{:S(2)}) collective-permute-start(f32[488,256]{1,0:T(8,128)S(1)} %get-tuple-element.75), channel_id=1, source_target_pairs={{0,32},{16,48},{32,64},{48,80},{64,96},{80,112},{96,0},{112,16},{1... | collective-permute-start | bytes 1499144 | tf_op jit(solution)/shard_map/ppermute | solution.py:48
  141.7 19.6 %collective-permute-start.16 = (f32[488,256]{1,0:T(8,128)S(1)}, f32[488,256]{1,0:T(8,128)S(1)}, u32[]{:S(2)}, u32[]{:S(2)}) collective-permute-start(f32[488,256]{1,0:T(8,128)S(1)} %get-tuple-element.68), channel_id=1, source_target_pairs={{0,96},{16,112},{32,0},{48,16},{64,32},{80,48},{96,64},{112,80},{1... | collective-permute-start | bytes 1499144 | tf_op jit(solution)/shard_map/ppermute | solution.py:48
  144.9 16.7 %collective-permute-start.15 = (f32[488,256]{1,0:T(8,128)S(1)}, f32[488,256]{1,0:T(8,128)S(1)}, u32[]{:S(2)}, u32[]{:S(2)}) collective-permute-start(f32[488,256]{1,0:T(8,128)S(1)} %get-tuple-element.73), channel_id=1, source_target_pairs={{0,32},{16,48},{32,64},{48,80},{64,96},{80,112},{96,0},{112,16},{1... | collective-permute-start | bytes 1499144 | tf_op jit(solution)/shard_map/ppermute | solution.py:48
  162.9 1.2 collective-permute-start.19
  164.1 3.7 %collective-permute-start.20 = (f32[16,128]{1,0:T(8,128)S(1)}, f32[16,128]{1,0:T(8,128)S(1)}, u32[]{:S(2)}, u32[]{:S(2)}) collective-permute-start(f32[16,128]{1,0:T(8,128)S(1)} %add.182), channel_id=1, source_target_pairs={{0,32},{16,48},{32,0},{48,16},{64,96},{80,112},{96,64},{112,80},{1... | collective-permute-start | bytes 24584 | tf_op jit(solution)/shard_map/ppermute | solution.py:337
  167.8 5.2 %collective-permute-start.21 = (f32[16,128]{1,0:T(8,128)S(1)}, f32[16,128]{1,0:T(8,128)S(1)}, u32[]{:S(2)}, u32[]{:S(2)}) collective-permute-start(f32[16,128]{1,0:T(8,128)S(1)} %add.183), channel_id=1, source_target_pairs={{0,64},{16,80},{32,96},{48,112},{64,0},{80,16},{96,32},{112,48},{1... | collective-permute-start | bytes 24584 | tf_op jit(solution)/shard_map/ppermute | solution.py:337
  173.0 3.7 %collective-permute-start.22 = (f32[16,128]{1,0:T(8,128)S(1)}, f32[16,128]{1,0:T(8,128)S(1)}, u32[]{:S(2)}, u32[]{:S(2)}) collective-permute-start(f32[16,128]{1,0:T(8,128)S(1)} %add.184), channel_id=1, source_target_pairs={{0,2},{2,0},{4,6},{6,4},{8,10},{10,8},{12,14},{14,12},{1,3},{3,1},... | collective-permute-start | bytes 24584 | tf_op jit(solution)/shard_map/ppermute | solution.py:337
  176.6 5.2 %collective-permute-start.23 = (f32[16,128]{1,0:T(8,128)S(1)}, f32[16,128]{1,0:T(8,128)S(1)}, u32[]{:S(2)}, u32[]{:S(2)}) collective-permute-start(f32[16,128]{1,0:T(8,128)S(1)} %add.185), channel_id=1, source_target_pairs={{0,1},{1,0},{2,3},{3,2},{4,5},{5,4},{6,7},{7,6},{8,9},{9,8},{10,11... | collective-permute-start | bytes 24584 | tf_op jit(solution)/shard_map/ppermute | solution.py:337
  181.8 3.7 %collective-permute-start.24 = (f32[16,128]{1,0:T(8,128)S(1)}, f32[16,128]{1,0:T(8,128)S(1)}, u32[]{:S(2)}, u32[]{:S(2)}) collective-permute-start(f32[16,128]{1,0:T(8,128)S(1)} %add.186), channel_id=1, source_target_pairs={{0,4},{2,6},{4,0},{6,2},{8,12},{10,14},{12,8},{14,10},{1,5},{3,7},... | collective-permute-start | bytes 24584 | tf_op jit(solution)/shard_map/ppermute | solution.py:337
  185.5 5.4 %collective-permute-start.25 = (f32[16,128]{1,0:T(8,128)S(1)}, f32[16,128]{1,0:T(8,128)S(1)}, u32[]{:S(2)}, u32[]{:S(2)}) collective-permute-start(f32[16,128]{1,0:T(8,128)S(1)} %add.187), channel_id=1, source_target_pairs={{0,8},{2,10},{4,12},{6,14},{8,0},{10,2},{12,4},{14,6},{1,9},{3,11}... | collective-permute-start | bytes 24584 | tf_op jit(solution)/shard_map/ppermute | solution.py:337

commit v7 on v6

--- a/solution.py
+++ b/solution.py
@@ -12,8 +12,8 @@
 RUNS = ((0, 1, 2), (3,))
 F32 = jnp.float32
 BF16 = jnp.bfloat16
-VMEM_LIMIT = 48 * 1024 * 1024
-VMEM_SMALL = 16 * 1024 * 1024
+VMEM_LIMIT = 52 * 1024 * 1024
+VMEM_SMALL = 32 * 1024 * 1024
 
 
 def behind(x, after):

time: 192 us -> 192 us (level)
  transfers between devices with their start and end apart: 26 -> 26, of which waited for: 17 -> 15; matrix products, arithmetic and copies ran while one was open for 3% -> 3% of each run, Pallas kernels for 32% -> 32%
where the time goes in v7:
time: 192 us; the launch traced here: 191 us
  waiting for transfers between devices  81.7 us (43%)
  Pallas kernels  65.2 us (34%)
  starting transfers between devices  35.4 us (18%)
  other arithmetic  5.02 us (3%)
  local copies, waits for them, and re-layouts  2.83 us (1%)
    ppermute x19, waiting for transfers between devices, send_along(): return lax.ppermute(x, 'band', pairs)  70.2 us
    pallas_call x2, Pallas kernels, project(): pl.pallas_call(functools.partial(project_kernel, share=share, first=first...  25.8 us
    ppermute x19, starting transfers between devices, send_along(): return lax.ppermute(x, 'band', pairs)  20.6 us
    pallas_call x1, Pallas kernels, lay_out(): pl.pallas_call(functools.partial(layout_kernel, share=share), grid=(pairs...  17.2 us
    pallas_call x4, Pallas kernels, pick_rows(): pl.pallas_call(pick_kernel, grid=(each,), in_specs=[pl.BlockSpec((count,...  16.5 us
    ppermute x7, starting transfers between devices, all_sum(): x = x + lax.ppermute(x, axis, [(i, i ^ bit) for i in range(size)])  14.8 us
    ppermute x7, waiting for transfers between devices, all_sum(): x = x + lax.ppermute(x, axis, [(i, i ^ bit) for i in range(size)])  11.5 us
  transfers between devices with their start and end apart: 26, of which 15 were waited for; matrix products, arithmetic and copies ran while one was open for 3% of the time, Pallas kernels for 32%

profile of v7, /device:TPU:0, one launch (start us, length us, event | category | flops | bytes accessed | tf_op | source)
XLA Modules:
  0.0 191.1 jit_solution(5077744394993293119)
XLA Ops:
  0.7 0.8 fusion.8
  1.6 2.3 %pick_rows.4 = (f32[1,160,512]{2,1,0:T(8,128)}, f32[1,160,512]{2,1,0:T(8,128)S(1)}) custom-call(s32[320,1]{1,0:T(8,128)S(1)} %copy.7.index_ref, f32[12,512,320]{2,1,0:T(8,128)} %bitcast.47), custom_call_target="tpu_custom_call" | custom-call | flops 999999995904 | bytes 10000000000 | tf_op jit(solution)/shard_map/pick_rows/pallas_call | solution.py:77
  3.9 3.3 %collective-permute-start.1 = (f32[1,160,512]{2,1,0:T(8,128)}, f32[1,160,512]{2,1,0:T(8,128)}, u32[]{:S(2)}, u32[]{:S(2)}) collective-permute-start(f32[1,160,512]{2,1,0:T(8,128)} %get-tuple-element.35), channel_id=1, source_target_pairs={{0,64},{16,80},{32,96},{48,112},{64,0},{80,16},{96,32},{112,48},{1... | collective-permute-start | bytes 983048 | tf_op jit(solution)/shard_map/ppermute | solution.py:48
  7.2 0.8 copy.8.index_ref
  8.0 2.9 %pick_rows.5 = (f32[2,160,512]{2,1,0:T(8,128)}, f32[2,160,512]{2,1,0:T(8,128)S(1)}) custom-call(s32[320,1]{1,0:T(8,128)S(1)} %copy.8.index_ref, f32[12,512,320]{2,1,0:T(8,128)} %bitcast.48), custom_call_target="tpu_custom_call" | custom-call | flops 999999995904 | bytes 10000000000 | tf_op jit(solution)/shard_map/pick_rows/pallas_call | solution.py:77
  11.4 4.4 %pick_rows.6 = (f32[3,160,512]{2,1,0:T(8,128)}, f32[3,160,512]{2,1,0:T(8,128)}) custom-call(s32[320,1]{1,0:T(8,128)S(1)} %copy.9.index_ref, f32[12,512,320]{2,1,0:T(8,128)} %bitcast.49), custom_call_target="tpu_custom_call" | custom-call | flops 999999995904 | bytes 10000000000 | tf_op jit(solution)/shard_map/pick_rows/pallas_call | solution.py:77
  15.8 3.3 %collective-permute-start.3 = (f32[3,160,512]{2,1,0:T(8,128)}, f32[3,160,512]{2,1,0:T(8,128)}, u32[]{:S(2)}, u32[]{:S(2)}) collective-permute-start(f32[3,160,512]{2,1,0:T(8,128)} %get-tuple-element.41), channel_id=1, source_target_pairs={{0,64},{16,80},{32,96},{48,112},{64,0},{80,16},{96,32},{112,48},{1... | collective-permute-start | bytes 2949128 | tf_op jit(solution)/shard_map/ppermute | solution.py:48
  19.2 6.9 %pick_rows.7 = (f32[6,160,512]{2,1,0:T(8,128)}, f32[6,160,512]{2,1,0:T(8,128)}) custom-call(s32[320,1]{1,0:T(8,128)S(1)} %copy.10.index_ref, f32[12,512,320]{2,1,0:T(8,128)} %bitcast.50), custom_call_target="tpu_custom_call" | custom-call | flops 999999995904 | bytes 10000000000 | tf_op jit(solution)/shard_map/pick_rows/pallas_call | solution.py:77
  26.3 17.2 %lay_out.1.refs_6_.refs_2_ = bf16[12,2,8,96,384]{4,3,2,1,0:T(8,128)(2,1)} custom-call(f32[12,160,2,648]{3,2,1,0:T(2,128)} %refs_5_, f32[12,160,2,648]{3,2,1,0:T(2,128)} %refs_5_, f32[12,160,2,648]{3,2,1,0:T(2,128)} %refs_5_, f32[12,160,2,648]{3,2,1,0:T(2,128)} %refs_5_, f32[12,160,2,648]{3,2,1,0:T(2,128)} %refs_5_, f32[12,160,2,648]{3,2,1,0:T(2,128)} %refs_5_), custom_call_target="tpu_custom_call" | custom-call | flops 999999995904 | bytes 10000000000 | tf_op jit(solution)/shard_map/lay_out/pallas_call | solution.py:125
  43.5 8.0 %collective-permute-done.3.refs_5_ = f32[3,160,512]{2,1,0:T(8,128)} collective-permute-done((f32[3,160,512]{2,1,0:T(8,128)}, f32[3,160,512]{2,1,0:T(8,128)}, u32[]{:S(2)}, u32[]{:S(2)}) %collective-permute-start.3) | collective-permute-done | bytes 983072 | tf_op jit(solution)/shard_map/ppermute | solution.py:48
  51.5 13.5 %project.2 = (f32[4,976,256]{2,1,0:T(8,128)S(1)}, f32[1,976,256]{2,1,0:T(8,128)S(1)}, f32[1,976,256]{2,1,0:T(8,128)S(1)}, f32[1,976,256]{2,1,0:T(8,128)S(1)}, f32[1,976,256]{2,1,0:T(8,128)S(1)}) custom-call(s32[3]{0:T(128)S(1)} %pad_add_fusion.place_ref, s32[12]{0:T(128)S(1)} %copy-done.2, f32[1,160,512]{2,1,0:T(8,128)S(1)} %get-tuple-element.45.refs_0_, ...), custom_call_target="tpu_custom_call" | custom-call | flops 999999995904 | bytes 10000000000 | tf_op jit(solution)/shard_map/project/pallas_call | solution.py:215
  65.1 0.5 collective-permute-start.5
  65.7 0.4 collective-permute-start.7
  66.1 1.6 collective-permute-done.4
  67.7 1.4 collective-permute-done.5
  69.1 1.6 add_bitcast_fusion.2
  70.7 3.0 %collective-permute-start.12 = (f32[976,256]{1,0:T(8,128)}, f32[976,256]{1,0:T(8,128)}, u32[]{:S(2)}, u32[]{:S(2)}) collective-permute-start(f32[976,256]{1,0:T(8,128)} %get-tuple-element.80), channel_id=1, source_target_pairs={{0,96},{16,112},{32,0},{48,16},{64,32},{80,48},{96,64},{112,80},{1... | collective-permute-start | bytes 2998280 | tf_op jit(solution)/shard_map/ppermute | solution.py:48
  73.7 19.9 %collective-permute-done.refs_1_ = f32[6,160,512]{2,1,0:T(8,128)} collective-permute-done((f32[6,160,512]{2,1,0:T(8,128)}, f32[6,160,512]{2,1,0:T(8,128)}, u32[]{:S(2)}, u32[]{:S(2)}) %collective-permute-start) | collective-permute-done | bytes 1966112 | tf_op jit(solution)/shard_map/ppermute | solution.py:48
  93.7 0.9 copy-done.5
  94.6 12.4 %project.3 = (f32[4,976,256]{2,1,0:T(8,128)S(1)}, f32[1,976,256]{2,1,0:T(8,128)S(1)}, f32[1,976,256]{2,1,0:T(8,128)S(1)}, f32[2,976,256]{2,1,0:T(8,128)S(1)}) custom-call(s32[3]{0:T(128)S(1)} %pad_add_fusion.place_ref, s32[12]{0:T(128)S(1)} %copy-done.2, f32[6,160,512]{2,1,0:T(8,128)S(1)} %copy-done.3, f32[6,160,512]{2,1,0:T(8,128)} %collective-permute-done.refs_1_, ...), custom_call_target="tpu_custom_call" | custom-call | flops 999999995904 | bytes 10000000000 | tf_op jit(solution)/shard_map/project/pallas_call | solution.py:215
  107.1 0.5 collective-permute-start.10
  107.7 6.6 %collective-permute-done.12 = f32[976,256]{1,0:T(8,128)} collective-permute-done((f32[976,256]{1,0:T(8,128)}, f32[976,256]{1,0:T(8,128)}, u32[]{:S(2)}, u32[]{:S(2)}) %collective-permute-start.12) | collective-permute-done | bytes 999456 | tf_op jit(solution)/shard_map/ppermute | solution.py:48
  114.6 1.6 collective-permute-start.14
  116.2 1.9 collective-permute-start.13
  118.1 1.9 slice_add_fusion
  120.0 1.5 collective-permute-start.18
  121.5 0.6 collective-permute-start.17
  122.1 19.0 %collective-permute-done.14 = f32[976,256]{1,0:T(8,128)S(1)} collective-permute-done((f32[976,256]{1,0:T(8,128)S(1)}, f32[976,256]{1,0:T(8,128)S(1)}, u32[]{:S(2)}, u32[]{:S(2)}) %collective-permute-start.14) | collective-permute-done | bytes 999456 | tf_op jit(solution)/shard_map/ppermute | solution.py:48
  141.6 3.2 %collective-permute-start.16 = (f32[488,256]{1,0:T(8,128)S(1)}, f32[488,256]{1,0:T(8,128)S(1)}, u32[]{:S(2)}, u32[]{:S(2)}) collective-permute-start(f32[488,256]{1,0:T(8,128)S(1)} %get-tuple-element.68), channel_id=1, source_target_pairs={{0,96},{16,112},{32,0},{48,16},{64,32},{80,48},{96,64},{112,80},{1... | collective-permute-start | bytes 1499144 | tf_op jit(solution)/shard_map/ppermute | solution.py:48
  144.8 7.1 %collective-permute-done.18.far_down_ref = f32[488,256]{1,0:T(8,128)S(1)} collective-permute-done((f32[488,256]{1,0:T(8,128)S(1)}, f32[488,256]{1,0:T(8,128)S(1)}, u32[]{:S(2)}, u32[]{:S(2)}) %collective-permute-start.18) | collective-permute-done | bytes 499744 | tf_op jit(solution)/shard_map/ppermute | solution.py:48
  151.9 1.6 place_run.2.refs_0_
  153.5 1.2 run_energy.2.so_far_ref
  154.8 6.4 %collective-permute-done.16.far_down_ref = f32[488,256]{1,0:T(8,128)S(1)} collective-permute-done((f32[488,256]{1,0:T(8,128)S(1)}, f32[488,256]{1,0:T(8,128)S(1)}, u32[]{:S(2)}, u32[]{:S(2)}) %collective-permute-start.16) | collective-permute-done | bytes 499744 | tf_op jit(solution)/shard_map/ppermute | solution.py:48
  161.2 1.2 run_energy.3
  162.5 1.2 collective-permute-done.19
  163.7 1.5 collective-permute-start.20
  165.2 2.1 %collective-permute-done.20 = f32[16,128]{1,0:T(8,128)S(1)} collective-permute-done((f32[16,128]{1,0:T(8,128)S(1)}, f32[16,128]{1,0:T(8,128)S(1)}, u32[]{:S(2)}, u32[]{:S(2)}) %collective-permute-start.20) | collective-permute-done | bytes 8224 | tf_op jit(solution)/shard_map/ppermute | solution.py:337
  167.3 2.9 %collective-permute-start.21 = (f32[16,128]{1,0:T(8,128)S(1)}, f32[16,128]{1,0:T(8,128)S(1)}, u32[]{:S(2)}, u32[]{:S(2)}) collective-permute-start(f32[16,128]{1,0:T(8,128)S(1)} %add.183), channel_id=1, source_target_pairs={{0,64},{16,80},{32,96},{48,112},{64,0},{80,16},{96,32},{112,48},{1... | collective-permute-start | bytes 24584 | tf_op jit(solution)/shard_map/ppermute | solution.py:337
  170.2 2.3 %collective-permute-done.21 = f32[16,128]{1,0:T(8,128)S(1)} collective-permute-done((f32[16,128]{1,0:T(8,128)S(1)}, f32[16,128]{1,0:T(8,128)S(1)}, u32[]{:S(2)}, u32[]{:S(2)}) %collective-permute-start.21) | collective-permute-done | bytes 8224 | tf_op jit(solution)/shard_map/ppermute | solution.py:337
  172.5 1.5 collective-permute-start.22
  174.0 2.2 %collective-permute-done.22 = f32[16,128]{1,0:T(8,128)S(1)} collective-permute-done((f32[16,128]{1,0:T(8,128)S(1)}, f32[16,128]{1,0:T(8,128)S(1)}, u32[]{:S(2)}, u32[]{:S(2)}) %collective-permute-start.22) | collective-permute-done | bytes 8224 | tf_op jit(solution)/shard_map/ppermute | solution.py:337
  176.2 3.1 %collective-permute-start.23 = (f32[16,128]{1,0:T(8,128)S(1)}, f32[16,128]{1,0:T(8,128)S(1)}, u32[]{:S(2)}, u32[]{:S(2)}) collective-permute-start(f32[16,128]{1,0:T(8,128)S(1)} %add.185), channel_id=1, source_target_pairs={{0,1},{1,0},{2,3},{3,2},{4,5},{5,4},{6,7},{7,6},{8,9},{9,8},{10,11... | collective-permute-start | bytes 24584 | tf_op jit(solution)/shard_map/ppermute | solution.py:337
  179.2 2.1 %collective-permute-done.23 = f32[16,128]{1,0:T(8,128)S(1)} collective-permute-done((f32[16,128]{1,0:T(8,128)S(1)}, f32[16,128]{1,0:T(8,128)S(1)}, u32[]{:S(2)}, u32[]{:S(2)}) %collective-permute-start.23) | collective-permute-done | bytes 8224 | tf_op jit(solution)/shard_map/ppermute | solution.py:337
  181.3 1.9 %collective-permute-start.24 = (f32[16,128]{1,0:T(8,128)S(1)}, f32[16,128]{1,0:T(8,128)S(1)}, u32[]{:S(2)}, u32[]{:S(2)}) collective-permute-start(f32[16,128]{1,0:T(8,128)S(1)} %add.186), channel_id=1, source_target_pairs={{0,4},{2,6},{4,0},{6,2},{8,12},{10,14},{12,8},{14,10},{1,5},{3,7},... | collective-permute-start | bytes 24584 | tf_op jit(solution)/shard_map/ppermute | solution.py:337
  183.2 1.8 collective-permute-done.24
  185.0 3.8 %collective-permute-start.25 = (f32[16,128]{1,0:T(8,128)S(1)}, f32[16,128]{1,0:T(8,128)S(1)}, u32[]{:S(2)}, u32[]{:S(2)}) collective-permute-start(f32[16,128]{1,0:T(8,128)S(1)} %add.187), channel_id=1, source_target_pairs={{0,8},{2,10},{4,12},{6,14},{8,0},{10,2},{12,4},{14,6},{1,9},{3,11}... | collective-permute-start | bytes 24584 | tf_op jit(solution)/shard_map/ppermute | solution.py:337
  188.8 1.6 place_run.3
  190.5 0.6 slice_log_fusion
  (59 shorter events, 2.3 us)
Async XLA Ops:
  1.4 2.5 %copy-start.9 = (s32[320,1]{0,1:T(1,128)}, s32[320,1]{0,1:T(1,128)S(1)}, u32[]{:S(2)}) copy-start(s32[320,1]{0,1:T(1,128)S(1)} %reshape.41) | copy-start | bytes 3844
  3.9 39.6 %collective-permute-start.1 = (f32[1,160,512]{2,1,0:T(8,128)}, f32[1,160,512]{2,1,0:T(8,128)}, u32[]{:S(2)}, u32[]{:S(2)}) collective-permute-start(f32[1,160,512]{2,1,0:T(8,128)} %get-tuple-element.35), channel_id=1, source_target_pairs={{0,64},{16,80},{32,96},{48,112},{64,0},{80,16},{96,32},{112,48},{1... | collective-permute-start | bytes 983048 | tf_op jit(solution)/shard_map/ppermute | solution.py:48
  8.0 3.2 %copy-start.10 = (s32[320,1]{0,1:T(1,128)S(1)}, s32[320,1]{0,1:T(1,128)}, u32[]{:S(2)}) copy-start(s32[320,1]{0,1:T(1,128)} %copy-done.9) | copy-start | bytes 3844
  11.0 32.6 %collective-permute-start.2 = (f32[2,160,512]{2,1,0:T(8,128)}, f32[2,160,512]{2,1,0:T(8,128)}, u32[]{:S(2)}, u32[]{:S(2)}) collective-permute-start(f32[2,160,512]{2,1,0:T(8,128)} %get-tuple-element.38), channel_id=1, source_target_pairs={{0,64},{16,80},{32,96},{48,112},{64,0},{80,16},{96,32},{112,48},{1... | collective-permute-start | bytes 1966088 | tf_op jit(solution)/shard_map/ppermute | solution.py:48
  11.4 7.7 %copy-start.11 = (s32[320,1]{0,1:T(1,128)S(1)}, s32[320,1]{0,1:T(1,128)}, u32[]{:S(2)}) copy-start(s32[320,1]{0,1:T(1,128)} %copy-done.9) | copy-start | bytes 3844
  15.8 35.8 %collective-permute-start.3 = (f32[3,160,512]{2,1,0:T(8,128)}, f32[3,160,512]{2,1,0:T(8,128)}, u32[]{:S(2)}, u32[]{:S(2)}) collective-permute-start(f32[3,160,512]{2,1,0:T(8,128)} %get-tuple-element.41), channel_id=1, source_target_pairs={{0,64},{16,80},{32,96},{48,112},{64,0},{80,16},{96,32},{112,48},{1... | collective-permute-start | bytes 2949128 | tf_op jit(solution)/shard_map/ppermute | solution.py:48
  26.0 67.6 %collective-permute-start = (f32[6,160,512]{2,1,0:T(8,128)}, f32[6,160,512]{2,1,0:T(8,128)}, u32[]{:S(2)}, u32[]{:S(2)}) collective-permute-start(f32[6,160,512]{2,1,0:T(8,128)} %get-tuple-element.44), channel_id=1, source_target_pairs={{0,64},{16,80},{32,96},{48,112},{64,0},{80,16},{96,32},{112,48},{1... | collective-permute-start | bytes 5898248 | tf_op jit(solution)/shard_map/ppermute | solution.py:48
  26.3 25.2 %copy-start.2 = (s32[12]{0:T(128)S(1)}, s32[12]{0:T(128)}, u32[]{:S(2)}) copy-start(s32[12]{0:T(128)} %wave_ref.7) | copy-start | bytes 148
  26.3 25.2 %copy-start.4 = (f32[3,160,512]{2,1,0:T(8,128)S(1)}, f32[3,160,512]{2,1,0:T(8,128)}, u32[]{:S(2)}) copy-start(f32[3,160,512]{2,1,0:T(8,128)} %get-tuple-element.47.refs_2_) | copy-start | bytes 2949124
  65.0 4.1 %copy-start = (f32[4,976,256]{2,1,0:T(8,128)}, f32[4,976,256]{2,1,0:T(8,128)S(1)}, u32[]{:S(2)}) copy-start(f32[4,976,256]{2,1,0:T(8,128)S(1)} %get-tuple-element.53) | copy-start | bytes 11993092
  65.0 29.7 %copy-start.3 = (f32[6,160,512]{2,1,0:T(8,128)S(1)}, f32[6,160,512]{2,1,0:T(8,128)}, u32[]{:S(2)}) copy-start(f32[6,160,512]{2,1,0:T(8,128)} %get-tuple-element.43.refs_0_) | copy-start | bytes 5898244
  65.0 2.7 %collective-permute-start.4 = (f32[1,976,256]{2,1,0:T(8,128)S(1)}, f32[1,976,256]{2,1,0:T(8,128)S(1)}, u32[]{:S(2)}, u32[]{:S(2)}) collective-permute-start(f32[1,976,256]{2,1,0:T(8,128)S(1)} %get-tuple-element.54), channel_id=1, source_target_pairs={{0,16},{16,0},{32,48},{48,32},{64,80},{80,64},{96,112},{112,96},{1... | collective-permute-start | bytes 2998280 | tf_op jit(solution)/shard_map/ppermute | solution.py:48
  65.1 4.0 %collective-permute-start.5 = (f32[1,976,256]{2,1,0:T(8,128)S(1)}, f32[1,976,256]{2,1,0:T(8,128)S(1)}, u32[]{:S(2)}, u32[]{:S(2)}) collective-permute-start(f32[1,976,256]{2,1,0:T(8,128)S(1)} %get-tuple-element.55), channel_id=1, source_target_pairs={{0,16},{16,0},{32,48},{48,32},{64,80},{80,64},{96,112},{112,96},{1... | collective-permute-start | bytes 2998280 | tf_op jit(solution)/shard_map/ppermute | solution.py:48
  65.6 28.1 %collective-permute-start.6 = (f32[1,976,256]{2,1,0:T(8,128)S(1)}, f32[1,976,256]{2,1,0:T(8,128)S(1)}, u32[]{:S(2)}, u32[]{:S(2)}) collective-permute-start(f32[1,976,256]{2,1,0:T(8,128)S(1)} %get-tuple-element.58), channel_id=1, source_target_pairs={{0,16},{16,0},{32,48},{48,32},{64,80},{80,64},{96,112},{112,96},{1... | collective-permute-start | bytes 2998280 | tf_op jit(solution)/shard_map/ppermute | solution.py:48
  65.7 28.0 %collective-permute-start.7 = (f32[1,976,256]{2,1,0:T(8,128)S(1)}, f32[1,976,256]{2,1,0:T(8,128)S(1)}, u32[]{:S(2)}, u32[]{:S(2)}) collective-permute-start(f32[1,976,256]{2,1,0:T(8,128)S(1)} %get-tuple-element.59), channel_id=1, source_target_pairs={{0,16},{16,0},{32,48},{48,32},{64,80},{80,64},{96,112},{112,96},{1... | collective-permute-start | bytes 2998280 | tf_op jit(solution)/shard_map/ppermute | solution.py:48
  70.7 43.6 %collective-permute-start.12 = (f32[976,256]{1,0:T(8,128)}, f32[976,256]{1,0:T(8,128)}, u32[]{:S(2)}, u32[]{:S(2)}) collective-permute-start(f32[976,256]{1,0:T(8,128)} %get-tuple-element.80), channel_id=1, source_target_pairs={{0,96},{16,112},{32,0},{48,16},{64,32},{80,48},{96,64},{112,80},{1... | collective-permute-start | bytes 2998280 | tf_op jit(solution)/shard_map/ppermute | solution.py:48
  73.7 40.6 %collective-permute-start.11 = (f32[976,256]{1,0:T(8,128)}, f32[976,256]{1,0:T(8,128)}, u32[]{:S(2)}, u32[]{:S(2)}) collective-permute-start(f32[976,256]{1,0:T(8,128)} %get-tuple-element.81), channel_id=1, source_target_pairs={{0,32},{16,48},{32,64},{48,80},{64,96},{80,112},{96,0},{112,16},{1... | collective-permute-start | bytes 2998280 | tf_op jit(solution)/shard_map/ppermute | solution.py:48
  93.7 1.0 copy-start.5
  94.6 12.4 %copy-start.7 = (f32[1,976,256]{2,1,0:T(8,128)}, f32[1,976,256]{2,1,0:T(8,128)S(1)}, u32[]{:S(2)}) copy-start(f32[1,976,256]{2,1,0:T(8,128)S(1)} %collective-permute-done.7) | copy-start | bytes 2998276
  107.0 11.1 %copy-start.1 = (f32[4,976,256]{2,1,0:T(8,128)S(1)}, f32[4,976,256]{2,1,0:T(8,128)}, u32[]{:S(2)}) copy-start(f32[4,976,256]{2,1,0:T(8,128)} %copy-done) | copy-start | bytes 11993092
  107.0 11.1 %copy-start.6 = (f32[1,976,256]{2,1,0:T(8,128)S(1)}, f32[1,976,256]{2,1,0:T(8,128)}, u32[]{:S(2)}) copy-start(f32[1,976,256]{2,1,0:T(8,128)} %copy-done.5) | copy-start | bytes 2998276
  107.0 11.0 %copy-start.8 = (f32[1,976,256]{2,1,0:T(8,128)S(1)}, f32[1,976,256]{2,1,0:T(8,128)}, u32[]{:S(2)}) copy-start(f32[1,976,256]{2,1,0:T(8,128)} %copy-done.7) | copy-start | bytes 2998276
  107.0 7.3 %collective-permute-start.9 = (f32[1,976,256]{2,1,0:T(8,128)S(1)}, f32[1,976,256]{2,1,0:T(8,128)S(1)}, u32[]{:S(2)}, u32[]{:S(2)}) collective-permute-start(f32[1,976,256]{2,1,0:T(8,128)S(1)} %get-tuple-element.63), channel_id=1, source_target_pairs={{0,16},{16,0},{32,48},{48,32},{64,80},{80,64},{96,112},{112,96},{1... | collective-permute-start | bytes 2998280 | tf_op jit(solution)/shard_map/ppermute | solution.py:48
  107.1 7.2 %collective-permute-start.10 = (f32[1,976,256]{2,1,0:T(8,128)S(1)}, f32[1,976,256]{2,1,0:T(8,128)S(1)}, u32[]{:S(2)}, u32[]{:S(2)}) collective-permute-start(f32[1,976,256]{2,1,0:T(8,128)S(1)} %get-tuple-element.64), channel_id=1, source_target_pairs={{0,16},{16,0},{32,48},{48,32},{64,80},{80,64},{96,112},{112,96},{1... | collective-permute-start | bytes 2998280 | tf_op jit(solution)/shard_map/ppermute | solution.py:48
  107.6 33.6 %collective-permute-start.8 = (f32[2,976,256]{2,1,0:T(8,128)S(1)}, f32[2,976,256]{2,1,0:T(8,128)S(1)}, u32[]{:S(2)}, u32[]{:S(2)}) collective-permute-start(f32[2,976,256]{2,1,0:T(8,128)S(1)} %get-tuple-element.62), channel_id=1, source_target_pairs={{0,16},{16,0},{32,48},{48,32},{64,80},{80,64},{96,112},{112,96},{1... | collective-permute-start | bytes 5996552 | tf_op jit(solution)/shard_map/ppermute | solution.py:48
  114.6 26.5 %collective-permute-start.14 = (f32[976,256]{1,0:T(8,128)S(1)}, f32[976,256]{1,0:T(8,128)S(1)}, u32[]{:S(2)}, u32[]{:S(2)}) collective-permute-start(f32[976,256]{1,0:T(8,128)S(1)} %get-tuple-element.78), channel_id=1, source_target_pairs={{0,32},{16,48},{32,64},{48,80},{64,96},{80,112},{96,0},{112,16},{1... | collective-permute-start | bytes 2998280 | tf_op jit(solution)/shard_map/ppermute | solution.py:48
  116.2 25.0 %collective-permute-start.13 = (f32[976,256]{1,0:T(8,128)S(1)}, f32[976,256]{1,0:T(8,128)S(1)}, u32[]{:S(2)}, u32[]{:S(2)}) collective-permute-start(f32[976,256]{1,0:T(8,128)S(1)} %get-tuple-element.79), channel_id=1, source_target_pairs={{0,96},{16,112},{32,0},{48,16},{64,32},{80,48},{96,64},{112,80},{1... | collective-permute-start | bytes 2998280 | tf_op jit(solution)/shard_map/ppermute | solution.py:48
  120.0 31.9 %collective-permute-start.18 = (f32[488,256]{1,0:T(8,128)S(1)}, f32[488,256]{1,0:T(8,128)S(1)}, u32[]{:S(2)}, u32[]{:S(2)}) collective-permute-start(f32[488,256]{1,0:T(8,128)S(1)} %get-tuple-element.74), channel_id=1, source_target_pairs={{0,96},{16,112},{32,0},{48,16},{64,32},{80,48},{96,64},{112,80},{1... | collective-permute-start | bytes 1499144 | tf_op jit(solution)/shard_map/ppermute | solution.py:48
  121.5 30.5 %collective-permute-start.17 = (f32[488,256]{1,0:T(8,128)S(1)}, f32[488,256]{1,0:T(8,128)S(1)}, u32[]{:S(2)}, u32[]{:S(2)}) collective-permute-start(f32[488,256]{1,0:T(8,128)S(1)} %get-tuple-element.75), channel_id=1, source_target_pairs={{0,32},{16,48},{32,64},{48,80},{64,96},{80,112},{96,0},{112,16},{1... | collective-permute-start | bytes 1499144 | tf_op jit(solution)/shard_map/ppermute | solution.py:48
  141.6 19.6 %collective-permute-start.16 = (f32[488,256]{1,0:T(8,128)S(1)}, f32[488,256]{1,0:T(8,128)S(1)}, u32[]{:S(2)}, u32[]{:S(2)}) collective-permute-start(f32[488,256]{1,0:T(8,128)S(1)} %get-tuple-element.68), channel_id=1, source_target_pairs={{0,96},{16,112},{32,0},{48,16},{64,32},{80,48},{96,64},{112,80},{1... | collective-permute-start | bytes 1499144 | tf_op jit(solution)/shard_map/ppermute | solution.py:48
  144.8 16.4 %collective-permute-start.15 = (f32[488,256]{1,0:T(8,128)S(1)}, f32[488,256]{1,0:T(8,128)S(1)}, u32[]{:S(2)}, u32[]{:S(2)}) collective-permute-start(f32[488,256]{1,0:T(8,128)S(1)} %get-tuple-element.73), channel_id=1, source_target_pairs={{0,32},{16,48},{32,64},{48,80},{64,96},{80,112},{96,0},{112,16},{1... | collective-permute-start | bytes 1499144 | tf_op jit(solution)/shard_map/ppermute | solution.py:48
  162.5 1.2 collective-permute-start.19
  163.7 3.7 %collective-permute-start.20 = (f32[16,128]{1,0:T(8,128)S(1)}, f32[16,128]{1,0:T(8,128)S(1)}, u32[]{:S(2)}, u32[]{:S(2)}) collective-permute-start(f32[16,128]{1,0:T(8,128)S(1)} %add.182), channel_id=1, source_target_pairs={{0,32},{16,48},{32,0},{48,16},{64,96},{80,112},{96,64},{112,80},{1... | collective-permute-start | bytes 24584 | tf_op jit(solution)/shard_map/ppermute | solution.py:337
  167.3 5.2 %collective-permute-start.21 = (f32[16,128]{1,0:T(8,128)S(1)}, f32[16,128]{1,0:T(8,128)S(1)}, u32[]{:S(2)}, u32[]{:S(2)}) collective-permute-start(f32[16,128]{1,0:T(8,128)S(1)} %add.183), channel_id=1, source_target_pairs={{0,64},{16,80},{32,96},{48,112},{64,0},{80,16},{96,32},{112,48},{1... | collective-permute-start | bytes 24584 | tf_op jit(solution)/shard_map/ppermute | solution.py:337
  172.5 3.7 %collective-permute-start.22 = (f32[16,128]{1,0:T(8,128)S(1)}, f32[16,128]{1,0:T(8,128)S(1)}, u32[]{:S(2)}, u32[]{:S(2)}) collective-permute-start(f32[16,128]{1,0:T(8,128)S(1)} %add.184), channel_id=1, source_target_pairs={{0,2},{2,0},{4,6},{6,4},{8,10},{10,8},{12,14},{14,12},{1,3},{3,1},... | collective-permute-start | bytes 24584 | tf_op jit(solution)/shard_map/ppermute | solution.py:337
  176.2 5.2 %collective-permute-start.23 = (f32[16,128]{1,0:T(8,128)S(1)}, f32[16,128]{1,0:T(8,128)S(1)}, u32[]{:S(2)}, u32[]{:S(2)}) collective-permute-start(f32[16,128]{1,0:T(8,128)S(1)} %add.185), channel_id=1, source_target_pairs={{0,1},{1,0},{2,3},{3,2},{4,5},{5,4},{6,7},{7,6},{8,9},{9,8},{10,11... | collective-permute-start | bytes 24584 | tf_op jit(solution)/shard_map/ppermute | solution.py:337
  181.3 3.7 %collective-permute-start.24 = (f32[16,128]{1,0:T(8,128)S(1)}, f32[16,128]{1,0:T(8,128)S(1)}, u32[]{:S(2)}, u32[]{:S(2)}) collective-permute-start(f32[16,128]{1,0:T(8,128)S(1)} %add.186), channel_id=1, source_target_pairs={{0,4},{2,6},{4,0},{6,2},{8,12},{10,14},{12,8},{14,10},{1,5},{3,7},... | collective-permute-start | bytes 24584 | tf_op jit(solution)/shard_map/ppermute | solution.py:337
  185.0 5.4 %collective-permute-start.25 = (f32[16,128]{1,0:T(8,128)S(1)}, f32[16,128]{1,0:T(8,128)S(1)}, u32[]{:S(2)}, u32[]{:S(2)}) collective-permute-start(f32[16,128]{1,0:T(8,128)S(1)} %add.187), channel_id=1, source_target_pairs={{0,8},{2,10},{4,12},{6,14},{8,0},{10,2},{12,4},{14,6},{1,9},{3,11}... | collective-permute-start | bytes 24584 | tf_op jit(solution)/shard_map/ppermute | solution.py:337

commit v8 on v7

--- a/solution.py
+++ b/solution.py
@@ -12,7 +12,7 @@
 RUNS = ((0, 1, 2), (3,))
 F32 = jnp.float32
 BF16 = jnp.bfloat16
-VMEM_LIMIT = 52 * 1024 * 1024
+VMEM_LIMIT = 56 * 1024 * 1024
 VMEM_SMALL = 32 * 1024 * 1024
 
 

time: 192 us -> 193 us (level)
  local copies, waits for them, and re-layouts: 2.83 us -> 5.53 us
    optimization_barrier x3, local copies, waits for them, and re-layouts: 1.08 us -> 3.1 us  [shards(): lax.optimization_barrier((index, legendre, message))]
  transfers between devices with their start and end apart: 26 -> 26, of which waited for: 15 -> 17; matrix products, arithmetic and copies ran while one was open for 3% -> 4% of each run, Pallas kernels for 32% -> 32%
where the time goes in v8:
time: 193 us; the launch traced here: 192 us
  waiting for transfers between devices  81.4 us (42%)
  Pallas kernels  65.7 us (34%)
  starting transfers between devices  33.9 us (18%)
  local copies, waits for them, and re-layouts  5.53 us (3%)
  other arithmetic  5.01 us (3%)
    ppermute x19, waiting for transfers between devices, send_along(): return lax.ppermute(x, 'band', pairs)  69.1 us
    pallas_call x2, Pallas kernels, project(): pl.pallas_call(functools.partial(project_kernel, share=share, first=first...  25.8 us
    ppermute x19, starting transfers between devices, send_along(): return lax.ppermute(x, 'band', pairs)  19.9 us
    pallas_call x1, Pallas kernels, lay_out(): pl.pallas_call(functools.partial(layout_kernel, share=share), grid=(pairs...  17.2 us
    pallas_call x4, Pallas kernels, pick_rows(): pl.pallas_call(pick_kernel, grid=(each,), in_specs=[pl.BlockSpec((count,...  16.9 us
    ppermute x7, starting transfers between devices, all_sum(): x = x + lax.ppermute(x, axis, [(i, i ^ bit) for i in range(size)])  14.1 us
    ppermute x7, waiting for transfers between devices, all_sum(): x = x + lax.ppermute(x, axis, [(i, i ^ bit) for i in range(size)])  12.3 us
  transfers between devices with their start and end apart: 26, of which 17 were waited for; matrix products, arithmetic and copies ran while one was open for 4% of the time, Pallas kernels for 32%

profile of v8, /device:TPU:0, one launch (start us, length us, event | category | flops | bytes accessed | tf_op | source)
XLA Modules:
  0.0 192.3 jit_solution(15958219162066019075)
XLA Ops:
  0.7 0.8 fusion.8
  1.4 0.8 copy.7.index_ref
  2.3 2.5 %pick_rows.4 = (f32[1,160,512]{2,1,0:T(8,128)}, f32[1,160,512]{2,1,0:T(8,128)}) custom-call(s32[320,1]{1,0:T(8,128)} %copy.7.index_ref, f32[12,512,320]{2,1,0:T(8,128)} %bitcast.47), custom_call_target="tpu_custom_call" | custom-call | flops 999999995904 | bytes 10000000000 | tf_op jit(solution)/shard_map/pick_rows/pallas_call | solution.py:77
  4.8 3.3 %collective-permute-start.1 = (f32[1,160,512]{2,1,0:T(8,128)}, f32[1,160,512]{2,1,0:T(8,128)}, u32[]{:S(2)}, u32[]{:S(2)}) collective-permute-start(f32[1,160,512]{2,1,0:T(8,128)} %get-tuple-element.35), channel_id=1, source_target_pairs={{0,64},{16,80},{32,96},{48,112},{64,0},{80,16},{96,32},{112,48},{1... | collective-permute-start | bytes 983048 | tf_op jit(solution)/shard_map/ppermute | solution.py:48
  8.1 1.5 copy.8.index_ref
  9.6 3.1 %pick_rows.5 = (f32[2,160,512]{2,1,0:T(8,128)}, f32[2,160,512]{2,1,0:T(8,128)}) custom-call(s32[320,1]{1,0:T(8,128)} %copy.8.index_ref, f32[12,512,320]{2,1,0:T(8,128)} %bitcast.48), custom_call_target="tpu_custom_call" | custom-call | flops 999999995904 | bytes 10000000000 | tf_op jit(solution)/shard_map/pick_rows/pallas_call | solution.py:77
  12.9 0.8 copy.9.index_ref
  13.7 4.4 %pick_rows.6 = (f32[3,160,512]{2,1,0:T(8,128)}, f32[3,160,512]{2,1,0:T(8,128)}) custom-call(s32[320,1]{1,0:T(8,128)} %copy.9.index_ref, f32[12,512,320]{2,1,0:T(8,128)} %bitcast.49), custom_call_target="tpu_custom_call" | custom-call | flops 999999995904 | bytes 10000000000 | tf_op jit(solution)/shard_map/pick_rows/pallas_call | solution.py:77
  18.1 3.3 %collective-permute-start.3 = (f32[3,160,512]{2,1,0:T(8,128)}, f32[3,160,512]{2,1,0:T(8,128)}, u32[]{:S(2)}, u32[]{:S(2)}) collective-permute-start(f32[3,160,512]{2,1,0:T(8,128)} %get-tuple-element.41), channel_id=1, source_target_pairs={{0,64},{16,80},{32,96},{48,112},{64,0},{80,16},{96,32},{112,48},{1... | collective-permute-start | bytes 2949128 | tf_op jit(solution)/shard_map/ppermute | solution.py:48
  21.4 0.8 copy.10.index_ref
  22.2 6.9 %pick_rows.7 = (f32[6,160,512]{2,1,0:T(8,128)}, f32[6,160,512]{2,1,0:T(8,128)}) custom-call(s32[320,1]{1,0:T(8,128)} %copy.10.index_ref, f32[12,512,320]{2,1,0:T(8,128)} %bitcast.50), custom_call_target="tpu_custom_call" | custom-call | flops 999999995904 | bytes 10000000000 | tf_op jit(solution)/shard_map/pick_rows/pallas_call | solution.py:77
  29.4 17.2 %lay_out.1.refs_6_.refs_2_ = bf16[12,2,8,96,384]{4,3,2,1,0:T(8,128)(2,1)} custom-call(f32[12,160,2,648]{3,2,1,0:T(2,128)} %refs_5_, f32[12,160,2,648]{3,2,1,0:T(2,128)} %refs_5_, f32[12,160,2,648]{3,2,1,0:T(2,128)} %refs_5_, f32[12,160,2,648]{3,2,1,0:T(2,128)} %refs_5_, f32[12,160,2,648]{3,2,1,0:T(2,128)} %refs_5_, f32[12,160,2,648]{3,2,1,0:T(2,128)} %refs_5_), custom_call_target="tpu_custom_call" | custom-call | flops 999999995904 | bytes 10000000000 | tf_op jit(solution)/shard_map/lay_out/pallas_call | solution.py:125
  46.7 6.6 %collective-permute-done.3.refs_5_ = f32[3,160,512]{2,1,0:T(8,128)} collective-permute-done((f32[3,160,512]{2,1,0:T(8,128)}, f32[3,160,512]{2,1,0:T(8,128)}, u32[]{:S(2)}, u32[]{:S(2)}) %collective-permute-start.3) | collective-permute-done | bytes 983072 | tf_op jit(solution)/shard_map/ppermute | solution.py:48
  53.2 13.5 %project.2 = (f32[4,976,256]{2,1,0:T(8,128)S(1)}, f32[1,976,256]{2,1,0:T(8,128)S(1)}, f32[1,976,256]{2,1,0:T(8,128)S(1)}, f32[1,976,256]{2,1,0:T(8,128)S(1)}, f32[1,976,256]{2,1,0:T(8,128)S(1)}) custom-call(s32[3]{0:T(128)S(1)} %pad_add_fusion.place_ref, s32[12]{0:T(128)S(1)} %copy-done.2, f32[1,160,512]{2,1,0:T(8,128)S(1)} %copy-done.6, ...), custom_call_target="tpu_custom_call" | custom-call | flops 999999995904 | bytes 10000000000 | tf_op jit(solution)/shard_map/project/pallas_call | solution.py:215
  67.8 1.6 collective-permute-done.4
  69.4 1.4 collective-permute-done.5
  70.8 1.6 add_bitcast_fusion.2
  72.5 2.2 %collective-permute-start.12 = (f32[976,256]{1,0:T(8,128)}, f32[976,256]{1,0:T(8,128)}, u32[]{:S(2)}, u32[]{:S(2)}) collective-permute-start(f32[976,256]{1,0:T(8,128)} %get-tuple-element.80), channel_id=1, source_target_pairs={{0,96},{16,112},{32,0},{48,16},{64,32},{80,48},{96,64},{112,80},{1... | collective-permute-start | bytes 2998280 | tf_op jit(solution)/shard_map/ppermute | solution.py:48
  74.6 20.7 %collective-permute-done.refs_1_ = f32[6,160,512]{2,1,0:T(8,128)} collective-permute-done((f32[6,160,512]{2,1,0:T(8,128)}, f32[6,160,512]{2,1,0:T(8,128)}, u32[]{:S(2)}, u32[]{:S(2)}) %collective-permute-start) | collective-permute-done | bytes 1966112 | tf_op jit(solution)/shard_map/ppermute | solution.py:48
  95.4 0.9 copy-done.7
  96.4 12.4 %project.3 = (f32[4,976,256]{2,1,0:T(8,128)S(1)}, f32[1,976,256]{2,1,0:T(8,128)S(1)}, f32[1,976,256]{2,1,0:T(8,128)S(1)}, f32[2,976,256]{2,1,0:T(8,128)S(1)}) custom-call(s32[3]{0:T(128)S(1)} %pad_add_fusion.place_ref, s32[12]{0:T(128)S(1)} %copy-done.2, f32[6,160,512]{2,1,0:T(8,128)S(1)} %copy-done.3, f32[6,160,512]{2,1,0:T(8,128)} %collective-permute-done.refs_1_, ...), custom_call_target="tpu_custom_call" | custom-call | flops 999999995904 | bytes 10000000000 | tf_op jit(solution)/shard_map/project/pallas_call | solution.py:215
  109.4 5.7 %collective-permute-done.12 = f32[976,256]{1,0:T(8,128)} collective-permute-done((f32[976,256]{1,0:T(8,128)}, f32[976,256]{1,0:T(8,128)}, u32[]{:S(2)}, u32[]{:S(2)}) %collective-permute-start.12) | collective-permute-done | bytes 999456 | tf_op jit(solution)/shard_map/ppermute | solution.py:48
  115.6 1.5 collective-permute-start.14
  117.1 2.0 %collective-permute-start.13 = (f32[976,256]{1,0:T(8,128)S(1)}, f32[976,256]{1,0:T(8,128)S(1)}, u32[]{:S(2)}, u32[]{:S(2)}) collective-permute-start(f32[976,256]{1,0:T(8,128)S(1)} %get-tuple-element.79), channel_id=1, source_target_pairs={{0,96},{16,112},{32,0},{48,16},{64,32},{80,48},{96,64},{112,80},{1... | collective-permute-start | bytes 2998280 | tf_op jit(solution)/shard_map/ppermute | solution.py:48
  119.1 1.9 slice_add_fusion
  120.9 1.4 collective-permute-start.18
  122.3 0.7 collective-permute-start.17
  123.0 18.9 %collective-permute-done.14 = f32[976,256]{1,0:T(8,128)S(1)} collective-permute-done((f32[976,256]{1,0:T(8,128)S(1)}, f32[976,256]{1,0:T(8,128)S(1)}, u32[]{:S(2)}, u32[]{:S(2)}) %collective-permute-start.14) | collective-permute-done | bytes 999456 | tf_op jit(solution)/shard_map/ppermute | solution.py:48
  142.5 3.3 %collective-permute-start.16 = (f32[488,256]{1,0:T(8,128)S(1)}, f32[488,256]{1,0:T(8,128)S(1)}, u32[]{:S(2)}, u32[]{:S(2)}) collective-permute-start(f32[488,256]{1,0:T(8,128)S(1)} %get-tuple-element.68), channel_id=1, source_target_pairs={{0,96},{16,112},{32,0},{48,16},{64,32},{80,48},{96,64},{112,80},{1... | collective-permute-start | bytes 1499144 | tf_op jit(solution)/shard_map/ppermute | solution.py:48
  145.7 7.1 %collective-permute-done.18.far_down_ref = f32[488,256]{1,0:T(8,128)S(1)} collective-permute-done((f32[488,256]{1,0:T(8,128)S(1)}, f32[488,256]{1,0:T(8,128)S(1)}, u32[]{:S(2)}, u32[]{:S(2)}) %collective-permute-start.18) | collective-permute-done | bytes 499744 | tf_op jit(solution)/shard_map/ppermute | solution.py:48
  152.8 1.6 place_run.2.refs_0_
  154.4 1.2 run_energy.2.so_far_ref
  155.7 6.4 %collective-permute-done.16.far_down_ref = f32[488,256]{1,0:T(8,128)S(1)} collective-permute-done((f32[488,256]{1,0:T(8,128)S(1)}, f32[488,256]{1,0:T(8,128)S(1)}, u32[]{:S(2)}, u32[]{:S(2)}) %collective-permute-start.16) | collective-permute-done | bytes 499744 | tf_op jit(solution)/shard_map/ppermute | solution.py:48
  162.5 1.2 run_energy.3
  163.8 1.2 collective-permute-done.19
  164.9 1.2 collective-permute-start.20
  166.1 2.5 %collective-permute-done.20 = f32[16,128]{1,0:T(8,128)S(1)} collective-permute-done((f32[16,128]{1,0:T(8,128)S(1)}, f32[16,128]{1,0:T(8,128)S(1)}, u32[]{:S(2)}, u32[]{:S(2)}) %collective-permute-start.20) | collective-permute-done | bytes 8224 | tf_op jit(solution)/shard_map/ppermute | solution.py:337
  168.6 2.5 %collective-permute-start.21 = (f32[16,128]{1,0:T(8,128)S(1)}, f32[16,128]{1,0:T(8,128)S(1)}, u32[]{:S(2)}, u32[]{:S(2)}) collective-permute-start(f32[16,128]{1,0:T(8,128)S(1)} %add.183), channel_id=1, source_target_pairs={{0,64},{16,80},{32,96},{48,112},{64,0},{80,16},{96,32},{112,48},{1... | collective-permute-start | bytes 24584 | tf_op jit(solution)/shard_map/ppermute | solution.py:337
  171.1 2.6 %collective-permute-done.21 = f32[16,128]{1,0:T(8,128)S(1)} collective-permute-done((f32[16,128]{1,0:T(8,128)S(1)}, f32[16,128]{1,0:T(8,128)S(1)}, u32[]{:S(2)}, u32[]{:S(2)}) %collective-permute-start.21) | collective-permute-done | bytes 8224 | tf_op jit(solution)/shard_map/ppermute | solution.py:337
  173.8 1.5 collective-permute-start.22
  175.2 2.2 %collective-permute-done.22 = f32[16,128]{1,0:T(8,128)S(1)} collective-permute-done((f32[16,128]{1,0:T(8,128)S(1)}, f32[16,128]{1,0:T(8,128)S(1)}, u32[]{:S(2)}, u32[]{:S(2)}) %collective-permute-start.22) | collective-permute-done | bytes 8224 | tf_op jit(solution)/shard_map/ppermute | solution.py:337
  177.4 3.1 %collective-permute-start.23 = (f32[16,128]{1,0:T(8,128)S(1)}, f32[16,128]{1,0:T(8,128)S(1)}, u32[]{:S(2)}, u32[]{:S(2)}) collective-permute-start(f32[16,128]{1,0:T(8,128)S(1)} %add.185), channel_id=1, source_target_pairs={{0,1},{1,0},{2,3},{3,2},{4,5},{5,4},{6,7},{7,6},{8,9},{9,8},{10,11... | collective-permute-start | bytes 24584 | tf_op jit(solution)/shard_map/ppermute | solution.py:337
  180.5 2.1 %collective-permute-done.23 = f32[16,128]{1,0:T(8,128)S(1)} collective-permute-done((f32[16,128]{1,0:T(8,128)S(1)}, f32[16,128]{1,0:T(8,128)S(1)}, u32[]{:S(2)}, u32[]{:S(2)}) %collective-permute-start.23) | collective-permute-done | bytes 8224 | tf_op jit(solution)/shard_map/ppermute | solution.py:337
  182.6 1.9 collective-permute-start.24
  184.5 1.8 collective-permute-done.24
  186.3 3.8 %collective-permute-start.25 = (f32[16,128]{1,0:T(8,128)S(1)}, f32[16,128]{1,0:T(8,128)S(1)}, u32[]{:S(2)}, u32[]{:S(2)}) collective-permute-start(f32[16,128]{1,0:T(8,128)S(1)} %add.187), channel_id=1, source_target_pairs={{0,8},{2,10},{4,12},{6,14},{8,0},{10,2},{12,4},{14,6},{1,9},{3,11}... | collective-permute-start | bytes 24584 | tf_op jit(solution)/shard_map/ppermute | solution.py:337
  190.1 1.6 place_run.3
  191.7 0.6 slice_log_fusion
  (63 shorter events, 3.7 us)
Async XLA Ops:
  1.4 3.4 %copy-start.11 = (s32[320,1]{0,1:T(1,128)}, s32[320,1]{0,1:T(1,128)S(1)}, u32[]{:S(2)}) copy-start(s32[320,1]{0,1:T(1,128)S(1)} %reshape.41) | copy-start | bytes 3844
  4.8 41.9 %collective-permute-start.1 = (f32[1,160,512]{2,1,0:T(8,128)}, f32[1,160,512]{2,1,0:T(8,128)}, u32[]{:S(2)}, u32[]{:S(2)}) collective-permute-start(f32[1,160,512]{2,1,0:T(8,128)} %get-tuple-element.35), channel_id=1, source_target_pairs={{0,64},{16,80},{32,96},{48,112},{64,0},{80,16},{96,32},{112,48},{1... | collective-permute-start | bytes 983048 | tf_op jit(solution)/shard_map/ppermute | solution.py:48
  9.6 3.4 %copy-start.12 = (s32[320,1]{0,1:T(1,128)S(1)}, s32[320,1]{0,1:T(1,128)}, u32[]{:S(2)}) copy-start(s32[320,1]{0,1:T(1,128)} %copy-done.11) | copy-start | bytes 3844
  12.7 34.0 %collective-permute-start.2 = (f32[2,160,512]{2,1,0:T(8,128)}, f32[2,160,512]{2,1,0:T(8,128)}, u32[]{:S(2)}, u32[]{:S(2)}) collective-permute-start(f32[2,160,512]{2,1,0:T(8,128)} %get-tuple-element.38), channel_id=1, source_target_pairs={{0,64},{16,80},{32,96},{48,112},{64,0},{80,16},{96,32},{112,48},{1... | collective-permute-start | bytes 1966088 | tf_op jit(solution)/shard_map/ppermute | solution.py:48
  13.7 7.7 %copy-start.13 = (s32[320,1]{0,1:T(1,128)S(1)}, s32[320,1]{0,1:T(1,128)}, u32[]{:S(2)}) copy-start(s32[320,1]{0,1:T(1,128)} %copy-done.11) | copy-start | bytes 3844
  18.1 35.1 %collective-permute-start.3 = (f32[3,160,512]{2,1,0:T(8,128)}, f32[3,160,512]{2,1,0:T(8,128)}, u32[]{:S(2)}, u32[]{:S(2)}) collective-permute-start(f32[3,160,512]{2,1,0:T(8,128)} %get-tuple-element.41), channel_id=1, source_target_pairs={{0,64},{16,80},{32,96},{48,112},{64,0},{80,16},{96,32},{112,48},{1... | collective-permute-start | bytes 2949128 | tf_op jit(solution)/shard_map/ppermute | solution.py:48
  29.1 66.3 %collective-permute-start = (f32[6,160,512]{2,1,0:T(8,128)}, f32[6,160,512]{2,1,0:T(8,128)}, u32[]{:S(2)}, u32[]{:S(2)}) collective-permute-start(f32[6,160,512]{2,1,0:T(8,128)} %get-tuple-element.44), channel_id=1, source_target_pairs={{0,64},{16,80},{32,96},{48,112},{64,0},{80,16},{96,32},{112,48},{1... | collective-permute-start | bytes 5898248 | tf_op jit(solution)/shard_map/ppermute | solution.py:48
  29.3 23.9 %copy-start.2 = (s32[12]{0:T(128)S(1)}, s32[12]{0:T(128)}, u32[]{:S(2)}) copy-start(s32[12]{0:T(128)} %wave_ref.7) | copy-start | bytes 148
  29.3 23.9 %copy-start.4 = (f32[3,160,512]{2,1,0:T(8,128)S(1)}, f32[3,160,512]{2,1,0:T(8,128)}, u32[]{:S(2)}) copy-start(f32[3,160,512]{2,1,0:T(8,128)} %get-tuple-element.47.refs_2_) | copy-start | bytes 2949124
  29.4 23.9 %copy-start.5 = (f32[2,160,512]{2,1,0:T(8,128)S(1)}, f32[2,160,512]{2,1,0:T(8,128)}, u32[]{:S(2)}) copy-start(f32[2,160,512]{2,1,0:T(8,128)} %get-tuple-element.46.refs_1_) | copy-start | bytes 1966084
  29.4 23.9 %copy-start.6 = (f32[1,160,512]{2,1,0:T(8,128)S(1)}, f32[1,160,512]{2,1,0:T(8,128)}, u32[]{:S(2)}) copy-start(f32[1,160,512]{2,1,0:T(8,128)} %get-tuple-element.45.refs_0_) | copy-start | bytes 983044
  66.7 4.1 %copy-start = (f32[4,976,256]{2,1,0:T(8,128)}, f32[4,976,256]{2,1,0:T(8,128)S(1)}, u32[]{:S(2)}) copy-start(f32[4,976,256]{2,1,0:T(8,128)S(1)} %get-tuple-element.53) | copy-start | bytes 11993092
  66.7 29.6 %copy-start.3 = (f32[6,160,512]{2,1,0:T(8,128)S(1)}, f32[6,160,512]{2,1,0:T(8,128)}, u32[]{:S(2)}) copy-start(f32[6,160,512]{2,1,0:T(8,128)} %get-tuple-element.43.refs_0_) | copy-start | bytes 5898244
  66.7 2.7 %collective-permute-start.4 = (f32[1,976,256]{2,1,0:T(8,128)S(1)}, f32[1,976,256]{2,1,0:T(8,128)S(1)}, u32[]{:S(2)}, u32[]{:S(2)}) collective-permute-start(f32[1,976,256]{2,1,0:T(8,128)S(1)} %get-tuple-element.54), channel_id=1, source_target_pairs={{0,16},{16,0},{32,48},{48,32},{64,80},{80,64},{96,112},{112,96},{1... | collective-permute-start | bytes 2998280 | tf_op jit(solution)/shard_map/ppermute | solution.py:48
  66.8 4.0 %collective-permute-start.5 = (f32[1,976,256]{2,1,0:T(8,128)S(1)}, f32[1,976,256]{2,1,0:T(8,128)S(1)}, u32[]{:S(2)}, u32[]{:S(2)}) collective-permute-start(f32[1,976,256]{2,1,0:T(8,128)S(1)} %get-tuple-element.55), channel_id=1, source_target_pairs={{0,16},{16,0},{32,48},{48,32},{64,80},{80,64},{96,112},{112,96},{1... | collective-permute-start | bytes 2998280 | tf_op jit(solution)/shard_map/ppermute | solution.py:48
  67.3 28.1 %collective-permute-start.6 = (f32[1,976,256]{2,1,0:T(8,128)S(1)}, f32[1,976,256]{2,1,0:T(8,128)S(1)}, u32[]{:S(2)}, u32[]{:S(2)}) collective-permute-start(f32[1,976,256]{2,1,0:T(8,128)S(1)} %get-tuple-element.58), channel_id=1, source_target_pairs={{0,16},{16,0},{32,48},{48,32},{64,80},{80,64},{96,112},{112,96},{1... | collective-permute-start | bytes 2998280 | tf_op jit(solution)/shard_map/ppermute | solution.py:48
  67.4 28.0 %collective-permute-start.7 = (f32[1,976,256]{2,1,0:T(8,128)S(1)}, f32[1,976,256]{2,1,0:T(8,128)S(1)}, u32[]{:S(2)}, u32[]{:S(2)}) collective-permute-start(f32[1,976,256]{2,1,0:T(8,128)S(1)} %get-tuple-element.59), channel_id=1, source_target_pairs={{0,16},{16,0},{32,48},{48,32},{64,80},{80,64},{96,112},{112,96},{1... | collective-permute-start | bytes 2998280 | tf_op jit(solution)/shard_map/ppermute | solution.py:48
  72.5 42.7 %collective-permute-start.12 = (f32[976,256]{1,0:T(8,128)}, f32[976,256]{1,0:T(8,128)}, u32[]{:S(2)}, u32[]{:S(2)}) collective-permute-start(f32[976,256]{1,0:T(8,128)} %get-tuple-element.80), channel_id=1, source_target_pairs={{0,96},{16,112},{32,0},{48,16},{64,32},{80,48},{96,64},{112,80},{1... | collective-permute-start | bytes 2998280 | tf_op jit(solution)/shard_map/ppermute | solution.py:48
  74.6 40.7 %collective-permute-start.11 = (f32[976,256]{1,0:T(8,128)}, f32[976,256]{1,0:T(8,128)}, u32[]{:S(2)}, u32[]{:S(2)}) collective-permute-start(f32[976,256]{1,0:T(8,128)} %get-tuple-element.81), channel_id=1, source_target_pairs={{0,32},{16,48},{32,64},{48,80},{64,96},{80,112},{96,0},{112,16},{1... | collective-permute-start | bytes 2998280 | tf_op jit(solution)/shard_map/ppermute | solution.py:48
  95.4 1.0 copy-start.7
  96.3 12.4 %copy-start.9 = (f32[1,976,256]{2,1,0:T(8,128)}, f32[1,976,256]{2,1,0:T(8,128)S(1)}, u32[]{:S(2)}) copy-start(f32[1,976,256]{2,1,0:T(8,128)S(1)} %collective-permute-done.7) | copy-start | bytes 2998276
  108.7 10.3 %copy-start.1 = (f32[4,976,256]{2,1,0:T(8,128)S(1)}, f32[4,976,256]{2,1,0:T(8,128)}, u32[]{:S(2)}) copy-start(f32[4,976,256]{2,1,0:T(8,128)} %copy-done) | copy-start | bytes 11993092
  108.7 10.3 %copy-start.8 = (f32[1,976,256]{2,1,0:T(8,128)S(1)}, f32[1,976,256]{2,1,0:T(8,128)}, u32[]{:S(2)}) copy-start(f32[1,976,256]{2,1,0:T(8,128)} %copy-done.7) | copy-start | bytes 2998276
  108.7 10.3 %copy-start.10 = (f32[1,976,256]{2,1,0:T(8,128)S(1)}, f32[1,976,256]{2,1,0:T(8,128)}, u32[]{:S(2)}) copy-start(f32[1,976,256]{2,1,0:T(8,128)} %copy-done.9) | copy-start | bytes 2998276
  108.8 6.5 %collective-permute-start.9 = (f32[1,976,256]{2,1,0:T(8,128)S(1)}, f32[1,976,256]{2,1,0:T(8,128)S(1)}, u32[]{:S(2)}, u32[]{:S(2)}) collective-permute-start(f32[1,976,256]{2,1,0:T(8,128)S(1)} %get-tuple-element.63), channel_id=1, source_target_pairs={{0,16},{16,0},{32,48},{48,32},{64,80},{80,64},{96,112},{112,96},{1... | collective-permute-start | bytes 2998280 | tf_op jit(solution)/shard_map/ppermute | solution.py:48
  108.8 6.5 %collective-permute-start.10 = (f32[1,976,256]{2,1,0:T(8,128)S(1)}, f32[1,976,256]{2,1,0:T(8,128)S(1)}, u32[]{:S(2)}, u32[]{:S(2)}) collective-permute-start(f32[1,976,256]{2,1,0:T(8,128)S(1)} %get-tuple-element.64), channel_id=1, source_target_pairs={{0,16},{16,0},{32,48},{48,32},{64,80},{80,64},{96,112},{112,96},{1... | collective-permute-start | bytes 2998280 | tf_op jit(solution)/shard_map/ppermute | solution.py:48
  109.3 32.7 %collective-permute-start.8 = (f32[2,976,256]{2,1,0:T(8,128)S(1)}, f32[2,976,256]{2,1,0:T(8,128)S(1)}, u32[]{:S(2)}, u32[]{:S(2)}) collective-permute-start(f32[2,976,256]{2,1,0:T(8,128)S(1)} %get-tuple-element.62), channel_id=1, source_target_pairs={{0,16},{16,0},{32,48},{48,32},{64,80},{80,64},{96,112},{112,96},{1... | collective-permute-start | bytes 5996552 | tf_op jit(solution)/shard_map/ppermute | solution.py:48
  115.6 26.4 %collective-permute-start.14 = (f32[976,256]{1,0:T(8,128)S(1)}, f32[976,256]{1,0:T(8,128)S(1)}, u32[]{:S(2)}, u32[]{:S(2)}) collective-permute-start(f32[976,256]{1,0:T(8,128)S(1)} %get-tuple-element.78), channel_id=1, source_target_pairs={{0,32},{16,48},{32,64},{48,80},{64,96},{80,112},{96,0},{112,16},{1... | collective-permute-start | bytes 2998280 | tf_op jit(solution)/shard_map/ppermute | solution.py:48
  117.1 25.0 %collective-permute-start.13 = (f32[976,256]{1,0:T(8,128)S(1)}, f32[976,256]{1,0:T(8,128)S(1)}, u32[]{:S(2)}, u32[]{:S(2)}) collective-permute-start(f32[976,256]{1,0:T(8,128)S(1)} %get-tuple-element.79), channel_id=1, source_target_pairs={{0,96},{16,112},{32,0},{48,16},{64,32},{80,48},{96,64},{112,80},{1... | collective-permute-start | bytes 2998280 | tf_op jit(solution)/shard_map/ppermute | solution.py:48
  120.9 31.8 %collective-permute-start.18 = (f32[488,256]{1,0:T(8,128)S(1)}, f32[488,256]{1,0:T(8,128)S(1)}, u32[]{:S(2)}, u32[]{:S(2)}) collective-permute-start(f32[488,256]{1,0:T(8,128)S(1)} %get-tuple-element.74), channel_id=1, source_target_pairs={{0,96},{16,112},{32,0},{48,16},{64,32},{80,48},{96,64},{112,80},{1... | collective-permute-start | bytes 1499144 | tf_op jit(solution)/shard_map/ppermute | solution.py:48
  122.3 30.5 %collective-permute-start.17 = (f32[488,256]{1,0:T(8,128)S(1)}, f32[488,256]{1,0:T(8,128)S(1)}, u32[]{:S(2)}, u32[]{:S(2)}) collective-permute-start(f32[488,256]{1,0:T(8,128)S(1)} %get-tuple-element.75), channel_id=1, source_target_pairs={{0,32},{16,48},{32,64},{48,80},{64,96},{80,112},{96,0},{112,16},{1... | collective-permute-start | bytes 1499144 | tf_op jit(solution)/shard_map/ppermute | solution.py:48
  142.5 19.6 %collective-permute-start.16 = (f32[488,256]{1,0:T(8,128)S(1)}, f32[488,256]{1,0:T(8,128)S(1)}, u32[]{:S(2)}, u32[]{:S(2)}) collective-permute-start(f32[488,256]{1,0:T(8,128)S(1)} %get-tuple-element.68), channel_id=1, source_target_pairs={{0,96},{16,112},{32,0},{48,16},{64,32},{80,48},{96,64},{112,80},{1... | collective-permute-start | bytes 1499144 | tf_op jit(solution)/shard_map/ppermute | solution.py:48
  145.7 16.7 %collective-permute-start.15 = (f32[488,256]{1,0:T(8,128)S(1)}, f32[488,256]{1,0:T(8,128)S(1)}, u32[]{:S(2)}, u32[]{:S(2)}) collective-permute-start(f32[488,256]{1,0:T(8,128)S(1)} %get-tuple-element.73), channel_id=1, source_target_pairs={{0,32},{16,48},{32,64},{48,80},{64,96},{80,112},{96,0},{112,16},{1... | collective-permute-start | bytes 1499144 | tf_op jit(solution)/shard_map/ppermute | solution.py:48
  163.7 1.2 collective-permute-start.19
  164.9 3.7 %collective-permute-start.20 = (f32[16,128]{1,0:T(8,128)S(1)}, f32[16,128]{1,0:T(8,128)S(1)}, u32[]{:S(2)}, u32[]{:S(2)}) collective-permute-start(f32[16,128]{1,0:T(8,128)S(1)} %add.182), channel_id=1, source_target_pairs={{0,32},{16,48},{32,0},{48,16},{64,96},{80,112},{96,64},{112,80},{1... | collective-permute-start | bytes 24584 | tf_op jit(solution)/shard_map/ppermute | solution.py:337
  168.6 5.2 %collective-permute-start.21 = (f32[16,128]{1,0:T(8,128)S(1)}, f32[16,128]{1,0:T(8,128)S(1)}, u32[]{:S(2)}, u32[]{:S(2)}) collective-permute-start(f32[16,128]{1,0:T(8,128)S(1)} %add.183), channel_id=1, source_target_pairs={{0,64},{16,80},{32,96},{48,112},{64,0},{80,16},{96,32},{112,48},{1... | collective-permute-start | bytes 24584 | tf_op jit(solution)/shard_map/ppermute | solution.py:337
  173.8 3.7 %collective-permute-start.22 = (f32[16,128]{1,0:T(8,128)S(1)}, f32[16,128]{1,0:T(8,128)S(1)}, u32[]{:S(2)}, u32[]{:S(2)}) collective-permute-start(f32[16,128]{1,0:T(8,128)S(1)} %add.184), channel_id=1, source_target_pairs={{0,2},{2,0},{4,6},{6,4},{8,10},{10,8},{12,14},{14,12},{1,3},{3,1},... | collective-permute-start | bytes 24584 | tf_op jit(solution)/shard_map/ppermute | solution.py:337
  177.4 5.2 %collective-permute-start.23 = (f32[16,128]{1,0:T(8,128)S(1)}, f32[16,128]{1,0:T(8,128)S(1)}, u32[]{:S(2)}, u32[]{:S(2)}) collective-permute-start(f32[16,128]{1,0:T(8,128)S(1)} %add.185), channel_id=1, source_target_pairs={{0,1},{1,0},{2,3},{3,2},{4,5},{5,4},{6,7},{7,6},{8,9},{9,8},{10,11... | collective-permute-start | bytes 24584 | tf_op jit(solution)/shard_map/ppermute | solution.py:337
  182.6 3.7 %collective-permute-start.24 = (f32[16,128]{1,0:T(8,128)S(1)}, f32[16,128]{1,0:T(8,128)S(1)}, u32[]{:S(2)}, u32[]{:S(2)}) collective-permute-start(f32[16,128]{1,0:T(8,128)S(1)} %add.186), channel_id=1, source_target_pairs={{0,4},{2,6},{4,0},{6,2},{8,12},{10,14},{12,8},{14,10},{1,5},{3,7},... | collective-permute-start | bytes 24584 | tf_op jit(solution)/shard_map/ppermute | solution.py:337
  186.3 5.4 %collective-permute-start.25 = (f32[16,128]{1,0:T(8,128)S(1)}, f32[16,128]{1,0:T(8,128)S(1)}, u32[]{:S(2)}, u32[]{:S(2)}) collective-permute-start(f32[16,128]{1,0:T(8,128)S(1)} %add.187), channel_id=1, source_target_pairs={{0,8},{2,10},{4,12},{6,14},{8,0},{10,2},{12,4},{14,6},{1,9},{3,11}... | collective-permute-start | bytes 24584 | tf_op jit(solution)/shard_map/ppermute | solution.py:337
